TPU v7x, 32 devices: a whole 2x2x4 slice. The times are simulated.
32 devices in a mesh: section: 2 (over core), dp: 16 (over z, y, x).
Axes of the slice: x: 2, y: 2, z: 4, core: 2. Of those that a mesh axis runs over, the one named last changes fastest.
Arguments:
- stream_in: bfloat16 [4, 128, 4, 8, 512], P(None, 'dp'), may hold values from -12 to 12
- image_count: int32 [16, 4], P('dp'), may hold values from 1 to 2, 6 in all within a row
- out_grad: bfloat16 [4, 128, 1, 2, 512], P(None, 'dp'), may hold values from -6 to 6
- first_conv: bfloat16 [2, 512, 4608], P('section'), may hold values from -0.09375 to 0.09375
- second_conv: bfloat16 [2, 512, 4608], P('section'), may hold values from -0.09375 to 0.09375
- squeeze: bfloat16 [2, 3, 512, 1024], P('section'), may hold values from -0.1875 to 0.1875
- expand: bfloat16 [2, 3, 512, 512], P('section'), may hold values from -0.25 to 0.25
- task_conv: bfloat16 [2, 3, 512, 4608], P('section'), may hold values from -0.09375 to 0.09375
- norm_gain: float32 [2, 8, 512], P('section'), may hold values from 0.5 to 1.5
- norm_shift: float32 [2, 8, 512], P('section'), may hold values from -2.5 to 2.5
- squeeze_gain: float32 [2, 3, 512], P('section'), may hold values from 0.5 to 1.5
- squeeze_shift: float32 [2, 3, 512], P('section'), may hold values from -2.5 to 2.5
Outputs:
- features: bfloat16 [2, 4, 128, 2, 4, 512], P('section', None, 'dp')
- input_grad: float32 [2, 4, 128, 4, 8, 512], P('section', None, 'dp')
- first_conv_grad: float32 [2, 2359296], P('section', 'dp')
- second_conv_grad: float32 [2, 2359296], P('section', 'dp')
- squeeze_grad: float32 [2, 1572864], P('section', 'dp')
- expand_grad: float32 [2, 786432], P('section', 'dp')
- task_conv_grad: float32 [2, 7077888], P('section', 'dp')
- norm_gain_grad: float32 [2, 8, 512], P('section')
- norm_shift_grad: float32 [2, 8, 512], P('section')
- squeeze_gain_grad: float32 [2, 3, 512], P('section')
- squeeze_shift_grad: float32 [2, 3, 512], P('section')
- rms: float32 [2, 4], P('section')
Inputs may be any that keep to these rules, and one draw needn't show every extreme that they name: `image_count`: each device's counts over its 4 micro-batches sum to 6.
All inputs are finite; a program needn't handle non-finite values.
Results may differ from a plain program's by a relative error of at most 0.024.
Values may be sent and summed in bfloat16 or wider, within the bound.
A program may use at most 576 MiB of HBM per device.

v0:
```python
import jax
import jax.numpy as jnp
from jax import lax
from jax.sharding import PartitionSpec as P

EPSILON = 1e-05


def from_behind(shard, axis, by):
    size = lax.axis_size(axis)
    pairs = [(i, i + by) for i in range(size) if 0 <= i + by < size]
    return lax.ppermute(shard, axis, pairs)


def broadcast_rows(vector):
    return vector[..., None, None, None, :]


def affine_rows(normed, scale_by, offset_by):
    return normed * broadcast_rows(scale_by) + broadcast_rows(offset_by)


def silu_slope(active):
    sigmoid_of = jax.nn.sigmoid(active)
    return sigmoid_of * (1.0 + active * (1.0 - sigmoid_of))


def pixel_sums(values, pixel_weight):
    weighted = values * pixel_weight
    return jnp.stack(
        [jnp.sum(weighted, axis=(-4, -3, -2)), jnp.sum(weighted * values, axis=(-4, -3, -2))],
        axis=-2,
    )


def gradient_sums(upstream, normed, pixel_weight):
    weighted = upstream * pixel_weight
    return jnp.stack(
        [jnp.sum(weighted, axis=(-4, -3, -2)), jnp.sum(weighted * normed, axis=(-4, -3, -2))],
        axis=-2,
    )


def pack_members(members):
    return jnp.concatenate([member.reshape(-1) for member in members])


def unpack_members(packed, members):
    results = []
    offset = 0
    for member in members:
        results.append(packed[offset : offset + member.size].reshape(member.shape))
        offset += member.size
    return results


def forward_moments(members, local_pixels):
    summed, counted = lax.psum((pack_members(members), local_pixels), "dp")
    return (unpack_members(summed, members), counted)


def backward_moments(members):
    summed = lax.psum(pack_members(members), "dp")
    return unpack_members(summed, members)


def normalize(values, moments, counted):
    average = moments[..., 0, :] / counted
    spread = moments[..., 1, :] / counted - average * average
    inverse = lax.rsqrt(spread + EPSILON)
    return ((values - broadcast_rows(average)) * broadcast_rows(inverse), inverse)


def norm_backward(upstream, normed, inverse, scale_by, sums, counted, pixel_weight):
    shift_part = broadcast_rows(sums[..., 0, :])
    scale_part = broadcast_rows(sums[..., 1, :])
    return (
        broadcast_rows(inverse * scale_by)
        * (upstream - (shift_part + normed * scale_part) / counted)
        * pixel_weight
    )


def window_blocks(values):
    leading = values.shape[:-3]
    height, breadth, channels = values.shape[-3:]
    return values.reshape(leading + (height // 2, 2, breadth // 2, 2, channels))


def soft_pool_blocks(blocks):
    summit = jnp.max(blocks, axis=(-4, -2), keepdims=True)
    return summit + jnp.log(jnp.mean(jnp.exp(blocks - summit), axis=(-4, -2), keepdims=True))


def soft_pool(values):
    pooled = soft_pool_blocks(window_blocks(values))
    return pooled.reshape(
        values.shape[:-3] + (values.shape[-3] // 2, values.shape[-2] // 2, values.shape[-1])
    )


def pool_back(upstream, values):
    blocks = window_blocks(values)
    pooled = soft_pool_blocks(blocks)
    weight_share = jnp.exp(blocks - pooled) * 0.25
    spread = upstream.reshape(pooled.shape) * weight_share
    return spread.reshape(values.shape)


def patch_columns(frames):
    height, breadth = (frames.shape[-3], frames.shape[-2])
    padding = [(0, 0)] * (frames.ndim - 3) + [(1, 1), (1, 1), (0, 0)]
    padded = jnp.pad(frames, padding)
    return jnp.concatenate(
        [
            padded[..., down_shift : down_shift + height, side_shift : side_shift + breadth, :]
            for down_shift in range(3)
            for side_shift in range(3)
        ],
        axis=-1,
    )


def columns_back(grad_columns, channels):
    height, breadth = (grad_columns.shape[-3], grad_columns.shape[-2])
    leading = [(0, 0)] * (grad_columns.ndim - 3)
    summed = None
    for tap_index in range(9):
        down_shift, side_shift = (tap_index // 3, tap_index % 3)
        piece_of = grad_columns[..., tap_index * channels : (tap_index + 1) * channels]
        placed = jnp.pad(
            piece_of, leading + [(down_shift, 2 - down_shift), (side_shift, 2 - side_shift), (0, 0)]
        )
        summed = placed if summed is None else summed + placed
    return summed[..., 1 : height + 1, 1 : breadth + 1, :]


def section_forward(frames, pixel_weight, region, weights):
    (
        first_conv,
        second_conv,
        squeeze,
        expand,
        task_conv,
        norm_gain,
        norm_shift,
        squeeze_gain,
        squeeze_shift,
    ) = weights
    channels = frames.shape[-1]
    tasks = squeeze.shape[0]
    local_pixels = jnp.sum(pixel_weight)
    input_columns = patch_columns(frames[0])
    first_pre = jnp.einsum(
        "shwk,ok->shwo", input_columns, first_conv, preferred_element_type=jnp.float32
    )
    first_moments, counted = forward_moments([pixel_sums(first_pre, pixel_weight)], local_pixels)
    first_normed, first_inverse = normalize(first_pre, first_moments[0], counted)
    first_output = jax.nn.silu(affine_rows(first_normed, norm_gain[0], norm_shift[0]))
    rounded_first = (first_output * region).astype(jnp.bfloat16)
    middle_columns = patch_columns(rounded_first)
    second_pre = jnp.einsum(
        "shwk,ok->shwo", middle_columns, second_conv, preferred_element_type=jnp.float32
    )
    earlier = frames[1:]
    narrow = jnp.einsum(
        "shwc,trc->tshwr",
        rounded_first,
        squeeze[:, :, :channels],
        preferred_element_type=jnp.float32,
    ) + jnp.einsum(
        "tshwc,trc->tshwr", earlier, squeeze[:, :, channels:], preferred_element_type=jnp.float32
    )
    middle_moments, counted = forward_moments(
        [pixel_sums(second_pre, pixel_weight), pixel_sums(narrow, pixel_weight)], local_pixels
    )
    second_normed, second_inverse = normalize(second_pre, middle_moments[0], counted)
    narrow_normed, narrow_inverse = normalize(narrow, middle_moments[1], counted)
    shared_out = jax.nn.silu(affine_rows(second_normed, norm_gain[1], norm_shift[1]))
    rounded_hidden = jax.nn.silu(affine_rows(narrow_normed, squeeze_gain, squeeze_shift)).astype(
        jnp.bfloat16
    )
    widened = jnp.einsum(
        "tshwr,tcr->tshwc", rounded_hidden, expand, preferred_element_type=jnp.float32
    )
    mask_moments, counted = forward_moments([pixel_sums(widened, pixel_weight)], local_pixels)
    widened_normed, widened_inverse = normalize(widened, mask_moments[0], counted)
    task_mask = jax.nn.sigmoid(
        affine_rows(widened_normed, norm_gain[2 : 2 + tasks], norm_shift[2 : 2 + tasks])
    )
    rounded_attended = (task_mask * shared_out * region).astype(jnp.bfloat16)
    attended_columns = patch_columns(rounded_attended)
    task_pre = jnp.einsum(
        "tshwk,tok->tshwo", attended_columns, task_conv, preferred_element_type=jnp.float32
    )
    task_moments, counted = forward_moments([pixel_sums(task_pre, pixel_weight)], local_pixels)
    task_normed, task_inverse = normalize(task_pre, task_moments[0], counted)
    task_out = jax.nn.silu(
        affine_rows(task_normed, norm_gain[2 + tasks :], norm_shift[2 + tasks :])
    )
    pooled = jnp.concatenate([soft_pool(shared_out)[None], soft_pool(task_out)], axis=0)
    kept_state = (
        frames,
        counted,
        first_normed,
        first_inverse,
        rounded_first,
        second_normed,
        second_inverse,
        narrow_normed,
        narrow_inverse,
        rounded_hidden,
        widened_normed,
        widened_inverse,
        rounded_attended,
        task_normed,
        task_inverse,
    )
    return (pooled, kept_state)


def section_backward(upstream, kept_state, pixel_weight, region, weights):
    (
        first_conv,
        second_conv,
        squeeze,
        expand,
        task_conv,
        norm_gain,
        norm_shift,
        squeeze_gain,
        squeeze_shift,
    ) = weights
    (
        frames,
        counted,
        first_normed,
        first_inverse,
        rounded_first,
        second_normed,
        second_inverse,
        narrow_normed,
        narrow_inverse,
        rounded_hidden,
        widened_normed,
        widened_inverse,
        rounded_attended,
        task_normed,
        task_inverse,
    ) = kept_state
    channels = frames.shape[-1]
    tasks = squeeze.shape[0]
    task_gain = norm_gain[2 + tasks :]
    mask_gain = norm_gain[2 : 2 + tasks]
    task_active = affine_rows(task_normed, task_gain, norm_shift[2 + tasks :])
    task_out = jax.nn.silu(task_active)
    grad_task_act = pool_back(upstream[1:], task_out) * silu_slope(task_active)
    task_sums = backward_moments([gradient_sums(grad_task_act, task_normed, pixel_weight)])[0]
    grad_task = norm_backward(
        grad_task_act, task_normed, task_inverse, task_gain, task_sums, counted, pixel_weight
    ).astype(jnp.bfloat16)
    attended_columns = patch_columns(rounded_attended)
    task_conv_grad = jnp.einsum(
        "tshwo,tshwk->tok", grad_task, attended_columns, preferred_element_type=jnp.float32
    )
    grad_attended = (
        columns_back(
            jnp.einsum(
                "tshwo,tok->tshwk", grad_task, task_conv, preferred_element_type=jnp.float32
            ),
            channels,
        )
        * region
    )
    second_active = affine_rows(second_normed, norm_gain[1], norm_shift[1])
    shared_out = jax.nn.silu(second_active)
    task_mask = jax.nn.sigmoid(affine_rows(widened_normed, mask_gain, norm_shift[2 : 2 + tasks]))
    grad_mask_act = grad_attended * shared_out * task_mask * (1.0 - task_mask)
    mask_sums = backward_moments([gradient_sums(grad_mask_act, widened_normed, pixel_weight)])[0]
    grad_widened = norm_backward(
        grad_mask_act, widened_normed, widened_inverse, mask_gain, mask_sums, counted, pixel_weight
    ).astype(jnp.bfloat16)
    expand_grad = jnp.einsum(
        "tshwc,tshwr->tcr", grad_widened, rounded_hidden, preferred_element_type=jnp.float32
    )
    narrow_active = affine_rows(narrow_normed, squeeze_gain, squeeze_shift)
    grad_narrow_act = jnp.einsum(
        "tshwc,tcr->tshwr", grad_widened, expand, preferred_element_type=jnp.float32
    ) * silu_slope(narrow_active)
    grad_shared = pool_back(upstream[0], shared_out) + jnp.sum(grad_attended * task_mask, axis=0)
    grad_second_act = grad_shared * silu_slope(second_active)
    second_sums, narrow_sums = backward_moments(
        [
            gradient_sums(grad_second_act, second_normed, pixel_weight),
            gradient_sums(grad_narrow_act, narrow_normed, pixel_weight),
        ]
    )
    grad_second = norm_backward(
        grad_second_act,
        second_normed,
        second_inverse,
        norm_gain[1],
        second_sums,
        counted,
        pixel_weight,
    ).astype(jnp.bfloat16)
    grad_narrow = norm_backward(
        grad_narrow_act,
        narrow_normed,
        narrow_inverse,
        squeeze_gain,
        narrow_sums,
        counted,
        pixel_weight,
    ).astype(jnp.bfloat16)
    middle_columns = patch_columns(rounded_first)
    second_conv_grad = jnp.einsum(
        "shwo,shwk->ok", grad_second, middle_columns, preferred_element_type=jnp.float32
    )
    earlier = frames[1:]
    squeeze_grad = jnp.concatenate(
        [
            jnp.einsum(
                "tshwr,shwc->trc", grad_narrow, rounded_first, preferred_element_type=jnp.float32
            ),
            jnp.einsum(
                "tshwr,tshwc->trc", grad_narrow, earlier, preferred_element_type=jnp.float32
            ),
        ],
        axis=-1,
    )
    grad_joined = jnp.einsum(
        "tshwr,trc->tshwc", grad_narrow, squeeze, preferred_element_type=jnp.float32
    )
    grad_first_out = (
        columns_back(
            jnp.einsum(
                "shwo,ok->shwk", grad_second, second_conv, preferred_element_type=jnp.float32
            ),
            channels,
        )
        + jnp.sum(grad_joined[..., :channels], axis=0)
    ) * region
    grad_earlier = grad_joined[..., channels:] * region
    first_active = affine_rows(first_normed, norm_gain[0], norm_shift[0])
    grad_first_act = grad_first_out * silu_slope(first_active)
    first_sums = backward_moments([gradient_sums(grad_first_act, first_normed, pixel_weight)])[0]
    grad_first = norm_backward(
        grad_first_act, first_normed, first_inverse, norm_gain[0], first_sums, counted, pixel_weight
    ).astype(jnp.bfloat16)
    input_columns = patch_columns(frames[0])
    first_conv_grad = jnp.einsum(
        "shwo,shwk->ok", grad_first, input_columns, preferred_element_type=jnp.float32
    )
    grad_shared_in = (
        columns_back(
            jnp.einsum("shwo,ok->shwk", grad_first, first_conv, preferred_element_type=jnp.float32),
            channels,
        )
        * region
    )
    grad_frames = jnp.concatenate([grad_shared_in[None], grad_earlier], axis=0)
    gain_rows = jnp.concatenate(
        [first_sums[1][None], second_sums[1][None], mask_sums[:, 1], task_sums[:, 1]], axis=0
    )
    shift_rows = jnp.concatenate(
        [first_sums[0][None], second_sums[0][None], mask_sums[:, 0], task_sums[:, 0]], axis=0
    )
    weight_terms = (first_conv_grad, second_conv_grad, squeeze_grad, expand_grad, task_conv_grad)
    norm_terms = (gain_rows, shift_rows, narrow_sums[:, 1], narrow_sums[:, 0])
    return (grad_frames, weight_terms, norm_terms)


def shards(
    stream_in,
    image_count,
    out_grad,
    first_conv,
    second_conv,
    squeeze,
    expand,
    task_conv,
    norm_gain,
    norm_shift,
    squeeze_gain,
    squeeze_shift,
):
    weights = (
        first_conv[0],
        second_conv[0],
        squeeze[0],
        expand[0],
        task_conv[0],
        norm_gain[0],
        norm_shift[0],
        squeeze_gain[0],
        squeeze_shift[0],
    )
    maps_count, images, height, breadth, channels = stream_in.shape
    micro_count = image_count.shape[1]
    slot_count = images // micro_count
    section_index = lax.axis_index("section")
    leading_section = section_index == 0
    region_height = jnp.where(leading_section, height, height // 2)
    region_breadth = jnp.where(leading_section, breadth, breadth // 2)
    down_iota = jnp.arange(height)[:, None, None]
    side_iota = jnp.arange(breadth)[None, :, None]
    region = ((down_iota < region_height) & (side_iota < region_breadth)).astype(jnp.float32)
    pooled_region = (
        (jnp.arange(height // 2)[:, None, None] < region_height // 2)
        & (jnp.arange(breadth // 2)[None, :, None] < region_breadth // 2)
    ).astype(jnp.float32)
    counts_row = image_count[0]
    slot_iota = jnp.arange(slot_count)

    def micro_weights(micro_index):
        clamped = jnp.clip(micro_index, 0, micro_count - 1)
        live_count = lax.dynamic_index_in_dim(counts_row, clamped, keepdims=False)
        image_weight = (slot_iota < live_count).astype(jnp.float32)[:, None, None, None]
        return (clamped, image_weight * region, image_weight * pooled_region)

    half_shape = (maps_count, slot_count, height // 2, breadth // 2, channels)
    arrived = jnp.zeros(half_shape, jnp.bfloat16)
    returned = jnp.zeros(half_shape, jnp.bfloat16)
    feature_out = jnp.zeros((maps_count, images, height // 2, breadth // 2, channels), jnp.bfloat16)
    input_grad_out = jnp.zeros((maps_count, images, height, breadth, channels), jnp.float32)
    weight_sums = None
    norm_sums = None
    square_total = jnp.zeros((maps_count,), jnp.float32)
    pixel_total = jnp.zeros((), jnp.float32)
    history = []
    for tick_index in range(micro_count + 2):
        forward_index = tick_index - section_index
        forward_live = (forward_index >= 0) & (forward_index < micro_count)
        forward_slot, forward_pixels, forward_pooled = micro_weights(forward_index)
        own_frames = lax.dynamic_slice_in_dim(
            stream_in, forward_slot * slot_count, slot_count, axis=1
        )
        grown_frames = jnp.pad(
            arrived, ((0, 0), (0, 0), (0, height // 2), (0, breadth // 2), (0, 0))
        )
        frames = jnp.where(leading_section, own_frames, grown_frames)
        pooled, kept_state = section_forward(frames, forward_pixels, region, weights)
        masked = pooled * forward_pooled
        outgoing = masked.astype(jnp.bfloat16)
        feature_out = jnp.where(
            forward_live,
            lax.dynamic_update_slice_in_dim(
                feature_out, outgoing, forward_slot * slot_count, axis=1
            ),
            feature_out,
        )
        square_total = square_total + jnp.where(
            forward_live, jnp.sum(masked * masked, axis=(1, 2, 3, 4)), 0.0
        )
        pixel_total = pixel_total + jnp.where(forward_live, jnp.sum(forward_pooled) * channels, 0.0)
        history.append(kept_state)
        backward_index = tick_index - 2 + section_index
        backward_live = (backward_index >= 0) & (backward_index < micro_count)
        backward_slot, backward_pixels, backward_pooled = micro_weights(backward_index)
        if tick_index >= 2:
            older_state = history[tick_index - 2]
            stored_state = jax.tree.map(
                lambda former, latest: jnp.where(leading_section, former, latest),
                older_state,
                kept_state,
            )
        else:
            stored_state = kept_state
        cotangent_slice = lax.dynamic_slice_in_dim(
            out_grad, backward_slot * slot_count, slot_count, axis=1
        )
        cotangent = jnp.pad(
            cotangent_slice, ((0, 0), (0, 0), (0, height // 4), (0, breadth // 4), (0, 0))
        )
        upstream = (
            jnp.where(leading_section, returned, cotangent).astype(jnp.float32) * backward_pooled
        )
        grad_frames, weight_terms, norm_terms = section_backward(
            upstream, stored_state, backward_pixels, region, weights
        )
        live_norms = tuple((jnp.where(backward_live, member, 0.0) for member in norm_terms))
        norm_sums = (
            live_norms
            if norm_sums is None
            else tuple((former + latest for former, latest in zip(norm_sums, live_norms)))
        )
        live_terms = tuple(
            (jnp.where(backward_live, member.reshape(-1), 0.0) for member in weight_terms)
        )
        weight_sums = (
            live_terms
            if weight_sums is None
            else tuple((former + latest for former, latest in zip(weight_sums, live_terms)))
        )
        sendback = grad_frames[:, :, : height // 2, : breadth // 2, :].astype(jnp.bfloat16)
        rounded_back = lax.optimization_barrier(grad_frames.astype(jnp.bfloat16)).astype(
            jnp.float32
        )
        recorded = jnp.where(leading_section, grad_frames, rounded_back)
        input_grad_out = jnp.where(
            backward_live,
            lax.dynamic_update_slice_in_dim(
                input_grad_out, recorded, backward_slot * slot_count, axis=1
            ),
            input_grad_out,
        )
        arrived = from_behind(outgoing, "section", 1)
        returned = from_behind(sendback, "section", -1)
    reduced = (
        lax.psum_scatter(weight_sums[0], "dp", scatter_dimension=0, tiled=True),
        lax.psum_scatter(weight_sums[1], "dp", scatter_dimension=0, tiled=True),
        lax.psum_scatter(weight_sums[2], "dp", scatter_dimension=0, tiled=True),
        lax.psum_scatter(weight_sums[3], "dp", scatter_dimension=0, tiled=True),
        lax.psum_scatter(weight_sums[4], "dp", scatter_dimension=0, tiled=True),
    )
    square_all, count_all = lax.psum((square_total, pixel_total), "dp")
    root_square = jnp.sqrt(square_all / count_all)
    return (
        feature_out[None],
        input_grad_out[None],
        reduced[0][None],
        reduced[1][None],
        reduced[2][None],
        reduced[3][None],
        reduced[4][None],
        norm_sums[0][None],
        norm_sums[1][None],
        norm_sums[2][None],
        norm_sums[3][None],
        root_square[None],
    )


def solution(mesh):
    return jax.shard_map(
        shards,
        mesh=mesh,
        in_specs=(
            P(None, "dp", None, None, None),
            P("dp", None),
            P(None, "dp", None, None, None),
            P("section", None, None),
            P("section", None, None),
            P("section", None, None, None),
            P("section", None, None, None),
            P("section", None, None, None),
            P("section", None, None),
            P("section", None, None),
            P("section", None, None),
            P("section", None, None),
        ),
        out_specs=(
            P("section", None, "dp", None, None, None),
            P("section", None, "dp", None, None, None),
            P("section", "dp"),
            P("section", "dp"),
            P("section", "dp"),
            P("section", "dp"),
            P("section", "dp"),
            P("section", None, None),
            P("section", None, None),
            P("section", None, None),
            P("section", None, None),
            P("section", None),
        ),
        check_vma=False,
    )
```

profile of v0, /device:TPU:6, one launch (start us, length us, event | category | flops | bytes accessed | tf_op | source)
XLA Modules:
  0.0 4385.7 jit_solution(12190726574103168360)
XLA Ops:
  66.7 73.1 %psum.448 = f32[4096]{0:T(1024)S(1)} all-reduce(f32[4096]{0:T(1024)S(1)} %pad_maximum_fusion.6), channel_id=1, replica_groups=mesh['section'=2,'dp'=16] {'dp'}, use_global_device_ids=true, to_apply=%region_9.10 | all-reduce | flops 4096 | bytes 32768 | tf_op jit(solution)/shard_map/psum | solution.py:58
  142.9 71.8 %psum.449 = f32[3,2,512]{2,0,1:T(4,128)S(1)} all-reduce(f32[3,2,512]{2,0,1:T(4,128)S(1)} %pad_maximum_fusion.7), channel_id=1, replica_groups=mesh['section'=2,'dp'=16] {'dp'}, use_global_device_ids=true, to_apply=%region_14.15 | all-reduce | flops 3072 | bytes 24576 | tf_op jit(solution)/shard_map/psum | solution.py:58
  228.7 71.7 %psum.450 = f32[3,2,512]{2,0,1:T(4,128)S(1)} all-reduce(f32[3,2,512]{2,0,1:T(4,128)S(1)} %pad_maximum_fusion.8), channel_id=1, replica_groups=mesh['section'=2,'dp'=16] {'dp'}, use_global_device_ids=true, to_apply=%region_17.18 | all-reduce | flops 3072 | bytes 24576 | tf_op jit(solution)/shard_map/psum | solution.py:58
  340.2 71.8 %all-reduce.229 = (f32[1024]{0:T(1024)S(1)}, f32[]{:T(128)}, f32[3,2,512]{2,0,1:T(4,128)S(1)}) all-reduce(f32[1024]{0:T(1024)S(1)} %bitcast.1625, f32[]{:T(128)} %get-tuple-element.139, f32[3,2,512]{2,0,1:T(4,128)S(1)} %pad_maximum_fusion.24), channel_id=1, replica_groups=mesh['section'=2,'dp'=16] {'dp'}, use_global_device_ids=true, to_apply=%region_22.23 | all-reduce | flops 4097 | bytes 32776 | tf_op jit(solution)/shard_map/psum | solution.py:58
  432.0 71.9 %all-reduce.228 = (f32[4096]{0:T(1024)S(1)}, f32[3,2,512]{2,0,1:T(4,128)S(1)}) all-reduce(f32[4096]{0:T(1024)S(1)} %pad_maximum_fusion.9, f32[3,2,512]{2,0,1:T(4,128)S(1)} %pad_maximum_fusion.25), channel_id=1, replica_groups=mesh['section'=2,'dp'=16] {'dp'}, use_global_device_ids=true, to_apply=%region_29.30 | all-reduce | flops 7168 | bytes 57344 | tf_op jit(solution)/shard_map/psum | solution.py:58
  514.5 71.8 %all-reduce.227 = (f32[3,2,512]{2,0,1:T(4,128)S(1)}, f32[4096]{0:T(1024)S(1)}) all-reduce(f32[3,2,512]{2,0,1:T(4,128)S(1)} %pad_maximum_fusion.10, f32[4096]{0:T(1024)S(1)} %pad_maximum_fusion.26), channel_id=1, replica_groups=mesh['section'=2,'dp'=16] {'dp'}, use_global_device_ids=true, to_apply=%region_34.35 | all-reduce | flops 7168 | bytes 57344 | tf_op jit(solution)/shard_map/psum | solution.py:58
  610.5 80.0 %all-reduce.226 = (f32[3,2,512]{2,0,1:T(4,128)S(1)}, f32[1024]{0:T(1024)S(1)}) all-reduce(f32[3,2,512]{2,0,1:T(4,128)S(1)} %pad_maximum_fusion.11, f32[1024]{0:T(1024)S(1)} %bitcast.1618), channel_id=1, replica_groups=mesh['section'=2,'dp'=16] {'dp'}, use_global_device_ids=true, to_apply=%region_37.38 | all-reduce | flops 4096 | bytes 32768 | tf_op jit(solution)/shard_map/psum | solution.py:58
  751.2 72.2 %all-reduce.225 = (f32[1024]{0:T(1024)S(1)}, f32[]{:T(128)}, f32[3,2,512]{2,0,1:T(4,128)}) all-reduce(f32[1024]{0:T(1024)S(1)} %bitcast.1624, f32[]{:T(128)} %get-tuple-element.140, f32[3,2,512]{2,0,1:T(4,128)S(1)} %pad_maximum_fusion.27), channel_id=1, replica_groups=mesh['section'=2,'dp'=16] {'dp'}, use_global_device_ids=true, to_apply=%region_42.43 | all-reduce | flops 4097 | bytes 32776 | tf_op jit(solution)/shard_map/psum | solution.py:58
  846.8 72.3 %all-reduce.224 = (f32[4096]{0:T(1024)}, f32[3,2,512]{2,0,1:T(4,128)}) all-reduce(f32[4096]{0:T(1024)} %pad_maximum_fusion.12, f32[3,2,512]{2,0,1:T(4,128)S(1)} %pad_maximum_fusion.28), channel_id=1, replica_groups=mesh['section'=2,'dp'=16] {'dp'}, use_global_device_ids=true, to_apply=%region_49.50 | all-reduce | flops 7168 | bytes 57344 | tf_op jit(solution)/shard_map/psum | solution.py:58
  939.4 72.0 %all-reduce.223 = (f32[3,2,512]{2,0,1:T(4,128)S(1)}, f32[4096]{0:T(1024)S(1)}) all-reduce(f32[3,2,512]{2,0,1:T(4,128)S(1)} %pad_maximum_fusion.13, f32[4096]{0:T(1024)S(1)} %pad_maximum_fusion.29), channel_id=1, replica_groups=mesh['section'=2,'dp'=16] {'dp'}, use_global_device_ids=true, to_apply=%region_54.55 | all-reduce | flops 7168 | bytes 57344 | tf_op jit(solution)/shard_map/psum | solution.py:58
  1036.6 72.3 %all-reduce.222 = (f32[3,2,512]{2,0,1:T(4,128)S(1)}, f32[1024]{0:T(1024)}) all-reduce(f32[3,2,512]{2,0,1:T(4,128)S(1)} %pad_maximum_fusion.14, f32[1024]{0:T(1024)S(1)} %bitcast.1617), channel_id=1, replica_groups=mesh['section'=2,'dp'=16] {'dp'}, use_global_device_ids=true, to_apply=%region_57.58 | all-reduce | flops 4096 | bytes 32768 | tf_op jit(solution)/shard_map/psum | solution.py:58
  1280.5 71.9 %all-reduce.220 = (f32[4096]{0:T(1024)S(1)}, f32[3,2,512]{2,0,1:T(4,128)}) all-reduce(f32[4096]{0:T(1024)S(1)} %pad_maximum_fusion.15, f32[3,2,512]{2,0,1:T(4,128)S(1)} %pad_maximum_fusion.31), channel_id=1, replica_groups=mesh['section'=2,'dp'=16] {'dp'}, use_global_device_ids=true, to_apply=%region_69.70 | all-reduce | flops 7168 | bytes 57344 | tf_op jit(solution)/shard_map/psum | solution.py:58
  1365.6 72.3 %all-reduce.219 = (f32[3,2,512]{2,0,1:T(4,128)S(1)}, f32[4096]{0:T(1024)S(1)}) all-reduce(f32[3,2,512]{2,0,1:T(4,128)S(1)} %pad_maximum_fusion.16, f32[4096]{0:T(1024)S(1)} %pad_maximum_fusion.32), channel_id=1, replica_groups=mesh['section'=2,'dp'=16] {'dp'}, use_global_device_ids=true, to_apply=%region_74.75 | all-reduce | flops 7168 | bytes 57344 | tf_op jit(solution)/shard_map/psum | solution.py:58
  1605.7 71.9 %all-reduce.217 = (f32[1024]{0:T(1024)S(1)}, f32[]{:T(128)}, f32[3,2,512]{2,0,1:T(4,128)S(1)}) all-reduce(f32[1024]{0:T(1024)S(1)} %bitcast.1623, f32[]{:T(128)} %get-tuple-element.142, f32[3,2,512]{2,0,1:T(4,128)S(1)} %pad_maximum_fusion.33), channel_id=1, replica_groups=mesh['section'=2,'dp'=16] {'dp'}, use_global_device_ids=true, to_apply=%region_82.83 | all-reduce | flops 4097 | bytes 32776 | tf_op jit(solution)/shard_map/psum | solution.py:58
  1702.1 71.9 %all-reduce.216 = (f32[4096]{0:T(1024)S(1)}, f32[3,2,512]{2,0,1:T(4,128)S(1)}) all-reduce(f32[4096]{0:T(1024)S(1)} %pad_maximum_fusion.18, f32[3,2,512]{2,0,1:T(4,128)S(1)} %pad_maximum_fusion.34), channel_id=1, replica_groups=mesh['section'=2,'dp'=16] {'dp'}, use_global_device_ids=true, to_apply=%region_89.90 | all-reduce | flops 7168 | bytes 57344 | tf_op jit(solution)/shard_map/psum | solution.py:58
  1784.7 72.3 %all-reduce.215 = (f32[3,2,512]{2,0,1:T(4,128)S(1)}, f32[4096]{0:T(1024)S(1)}) all-reduce(f32[3,2,512]{2,0,1:T(4,128)S(1)} %pad_maximum_fusion.19, f32[4096]{0:T(1024)S(1)} %pad_maximum_fusion.35), channel_id=1, replica_groups=mesh['section'=2,'dp'=16] {'dp'}, use_global_device_ids=true, to_apply=%region_94.95 | all-reduce | flops 7168 | bytes 57344 | tf_op jit(solution)/shard_map/psum | solution.py:58
  1880.2 71.7 %all-reduce.214 = (f32[3,2,512]{2,0,1:T(4,128)S(1)}, f32[1024]{0:T(1024)}) all-reduce(f32[3,2,512]{2,0,1:T(4,128)S(1)} %pad_maximum_fusion.20, f32[1024]{0:T(1024)S(1)} %bitcast.1616), channel_id=1, replica_groups=mesh['section'=2,'dp'=16] {'dp'}, use_global_device_ids=true, to_apply=%region_97.98 | all-reduce | flops 4096 | bytes 32768 | tf_op jit(solution)/shard_map/psum | solution.py:58
  2024.5 71.8 %all-reduce.213 = (f32[1024]{0:T(1024)S(1)}, f32[]{:T(128)}, f32[3,2,512]{2,0,1:T(4,128)S(1)}) all-reduce(f32[1024]{0:T(1024)S(1)} %bitcast.1621, f32[]{:T(128)} %get-tuple-element.138, f32[3,2,512]{2,0,1:T(4,128)S(1)} %pad_maximum_fusion.36), channel_id=1, replica_groups=mesh['section'=2,'dp'=16] {'dp'}, use_global_device_ids=true, to_apply=%region_102.103 | all-reduce | flops 4097 | bytes 32776 | tf_op jit(solution)/shard_map/psum | solution.py:58
  2116.4 71.9 %all-reduce.212 = (f32[4096]{0:T(1024)S(1)}, f32[3,2,512]{2,0,1:T(4,128)}) all-reduce(f32[4096]{0:T(1024)S(1)} %pad_maximum_fusion.21, f32[3,2,512]{2,0,1:T(4,128)S(1)} %pad_maximum_fusion.37), channel_id=1, replica_groups=mesh['section'=2,'dp'=16] {'dp'}, use_global_device_ids=true, to_apply=%region_109.110 | all-reduce | flops 7168 | bytes 57344 | tf_op jit(solution)/shard_map/psum | solution.py:58
  2202.9 72.9 %all-reduce.211 = (f32[3,2,512]{2,0,1:T(4,128)S(1)}, f32[4096]{0:T(1024)S(1)}) all-reduce(f32[3,2,512]{2,0,1:T(4,128)S(1)} %pad_maximum_fusion.22, f32[4096]{0:T(1024)} %pad_maximum_fusion.38), channel_id=1, replica_groups=mesh['section'=2,'dp'=16] {'dp'}, use_global_device_ids=true, to_apply=%region_114.115 | all-reduce | flops 7168 | bytes 57344 | tf_op jit(solution)/shard_map/psum | solution.py:58
  2443.3 71.8 %psum.496 = f32[3,2,512]{2,0,1:T(4,128)S(1)} all-reduce(f32[3,2,512]{2,0,1:T(4,128)S(1)} %pad_maximum_fusion.39), channel_id=1, replica_groups=mesh['section'=2,'dp'=16] {'dp'}, use_global_device_ids=true, to_apply=%region_218.219 | all-reduce | flops 3072 | bytes 24576 | tf_op jit(solution)/shard_map/psum | solution.py:63
  2531.5 71.9 %psum.497 = f32[3,2,512]{2,0,1:T(4,128)S(1)} all-reduce(f32[3,2,512]{2,0,1:T(4,128)S(1)} %pad_maximum_fusion.40), channel_id=1, replica_groups=mesh['section'=2,'dp'=16] {'dp'}, use_global_device_ids=true, to_apply=%region_224.225 | all-reduce | flops 3072 | bytes 24576 | tf_op jit(solution)/shard_map/psum | solution.py:63
  2606.0 71.8 %psum.498 = f32[4096]{0:T(1024)S(1)} all-reduce(f32[4096]{0:T(1024)S(1)} %pad_maximum_fusion.41), channel_id=1, replica_groups=mesh['section'=2,'dp'=16] {'dp'}, use_global_device_ids=true, to_apply=%region_227.228 | all-reduce | flops 4096 | bytes 32768 | tf_op jit(solution)/shard_map/psum | solution.py:63
  2927.4 1441.0 %all-reduce.234.cloned.1.call-done = (f32[2359296]{0:T(1024)}, f32[2359296]{0:T(1024)}, f32[1572864]{0:T(1024)}, f32[786432]{0:T(1024)}, f32[7077888]{0:T(1024)}) async-done(((f32[2359296]{0:T(1024)}, f32[2359296]{0:T(1024)}, f32[1572864]{0:T(1024)}, f32[786432]{0:T(1024)}, f32[7077888]{0:T(1024)}), (f32[2359296]{0:T(1024)}, f32[2359296]{0:T(1024)}, f32[1572864]{0:T(1024)}, f32[786432]{0:T(1024)}, ...) | async-done | bytes 56623120
  (2438 shorter events, 1242.1 us)
Async XLA Ops:
  7.2 135.0 %copy-start = (bf16[1,3,512,512]{3,2,1,0:T(8,128)(2,1)S(1)}, bf16[1,3,512,512]{3,2,1,0:T(8,128)(2,1)}, u32[]{:S(2)}) copy-start(bf16[1,3,512,512]{3,2,1,0:T(8,128)(2,1)} %param.18) | copy-start | bytes 4718596
  7.2 4361.2 %all-reduce.234.cloned.1.call-start = ((), (), s32[]{:S(2)}) async-start(), calls=%async_computation | async-start | bytes 113246208
  18.5 2670.4 %copy-start.68 = (f32[4,8]{1,0:T(4,128)}, f32[4,8]{1,0:T(4,128)S(1)}, u32[]{:S(2)}) copy-start(f32[4,8]{1,0:T(4,128)S(1)} %and_convert_fusion.1) | copy-start | bytes 388
  19.9 122.3 %copy-start.369 = (f32[2,4,8]{2,1,0:T(4,128)}, f32[2,4,8]{2,1,0:T(4,128)S(1)}, u32[]{:S(2)}) copy-start(f32[2,4,8]{2,1,0:T(4,128)S(1)} %get-tuple-element.682) | copy-start | bytes 772
  20.0 312.1 %copy-start.295 = (f32[2,4,8]{2,1,0:T(4,128)}, f32[2,4,8]{2,1,0:T(4,128)S(1)}, u32[]{:S(2)}) copy-start(f32[2,4,8]{2,1,0:T(4,128)S(1)} %get-tuple-element.672) | copy-start | bytes 772
  24.0 800.8 %copy-start.29 = (f32[2,4,8,512]{3,2,1,0:T(8,128)}, f32[2,4,8,512]{3,2,1,0:T(8,128)S(1)}, u32[]{:S(2)}) copy-start(f32[2,4,8,512]{3,2,1,0:T(8,128)S(1)} %get-tuple-element.708) | copy-start | bytes 393220
  24.1 193.6 %copy-start.299 = (f32[1,1,512]{2,1,0:T(1,128)}, f32[1,1,512]{2,1,0:T(1,128)S(1)}, u32[]{:S(2)}) copy-start(f32[1,1,512]{2,1,0:T(1,128)S(1)} %get-tuple-element.611) | copy-start | bytes 6148
  65.3 152.4 %copy-start.73 = (f32[2,4,8,512]{3,2,1,0:T(8,128)}, f32[2,4,8,512]{3,2,1,0:T(8,128)S(1)}, u32[]{:S(2)}) copy-start(f32[2,4,8,512]{3,2,1,0:T(8,128)S(1)} %get-tuple-element.710) | copy-start | bytes 393220
  66.6 527.5 %copy-start.31 = (f32[3,2,4,8,512]{4,3,2,1,0:T(8,128)}, f32[3,2,4,8,512]{4,3,2,1,0:T(8,128)S(1)}, u32[]{:S(2)}) copy-start(f32[3,2,4,8,512]{4,3,2,1,0:T(8,128)S(1)} %get-tuple-element.709) | copy-start | bytes 1179652
  216.5 115.6 %copy-start.144 = (f32[3,512]{1,0:T(4,128)}, f32[3,512]{1,0:T(4,128)S(1)}, u32[]{:S(2)}) copy-start(f32[3,512]{1,0:T(4,128)S(1)} %get-tuple-element.606) | copy-start | bytes 18436
  216.5 115.6 %copy-start.147 = (f32[3,512]{1,0:T(4,128)}, f32[3,512]{1,0:T(4,128)S(1)}, u32[]{:S(2)}) copy-start(f32[3,512]{1,0:T(4,128)S(1)} %get-tuple-element.608) | copy-start | bytes 18436
  228.7 187.5 %copy-start.17 = (f32[3,2,4,8,512]{4,3,2,1,0:T(8,128)}, f32[3,2,4,8,512]{4,3,2,1,0:T(8,128)S(1)}, u32[]{:S(2)}) copy-start(f32[3,2,4,8,512]{4,3,2,1,0:T(8,128)S(1)} %get-tuple-element.712) | copy-start | bytes 1179652
  311.8 22.4 collective-permute-start
  726.5 14.8 collective-permute-start.5
  735.5 8.0 collective-permute-start.1
  935.3 178.1 %copy-start.366 = (f32[3,512]{1,0:T(4,128)}, f32[3,512]{1,0:T(4,128)S(1)}, u32[]{:S(2)}) copy-start(f32[3,512]{1,0:T(4,128)S(1)} %get-tuple-element.304) | copy-start | bytes 18436
  1157.6 16.0 collective-permute-start.6
  1167.8 8.9 collective-permute-start.2
  1558.0 38.0 collective-permute-start.7
  1561.6 36.4 collective-permute-start.3
  1973.0 42.8 collective-permute-start.8
  1978.0 40.1 collective-permute-start.4
  2400.3 39.7 collective-permute-start.9
  2531.5 155.2 %slice-start.10 = ((s8[4718592]{0:T(1024)(128)(4,1)}), s8[524288]{0:T(1024)(128)(4,1)S(1)}, s32[]{:S(2)}) async-start(s8[4718592]{0:T(1024)(128)(4,1)} %bitcast.1407), calls=%async_computation.11 | async-start | bytes 1048576
  (691 other events, 13028.0 us)
Sparse Core Ops, SparseCore 0:
  2911.9 1456.4 all-reduce.233
where the time goes:
time: 4400 us; the launch traced here: 4390 us
  blocking collectives  1960 us (45%)
  waiting for transfers between devices  1440 us (33%)
  matrix products  481 us (11%)
  other arithmetic  234 us (5%)
  local copies, waits for them, and re-layouts  211 us (5%)
    psum x24, blocking collectives, forward_moments(): summed, counted = lax.psum((pack_members(members), local_pixels), 'dp')  1700 us
    unnamed x2, waiting for transfers between devices  1440 us
    psum x4, blocking collectives, backward_moments(): summed = lax.psum(pack_members(members), 'dp')  257 us
    dot_general x6, matrix products, section_backward(): jnp.einsum('tshwo,tshwk->tok', grad_task, attended_columns, preferred_ele...  116 us
  transfers between devices with their start and end apart: 11, of which 1 were waited for; matrix products, arithmetic and copies ran while one was open for 4% of the time, Pallas kernels for 0%

commit v1 on v0

v1 whole, which is shorter than its diff:
```python
import functools
import types

import jax
import jax.numpy as jnp
from jax import lax
from jax.experimental import pallas as pl
from jax.experimental.pallas import tpu as pltpu
from jax.sharding import PartitionSpec as P

EPSILON = 1e-05
SUM_ROWS = 40


def stages_of(size):
    stages = []
    stride = 1
    while stride < size:
        radix = next(r for r in (4, 2, 3, 5, 7, size // stride) if (size // stride) % r == 0)
        stages.append((radix, stride))
        stride *= radix
    return stages


def sum_kernel(stages, own_ref, out_ref, *scratch):
    slots, (send_sem, recv_sem) = scratch[: len(stages)], scratch[len(stages) :]
    section = lax.axis_index("section")
    me = lax.axis_index("dp")
    barrier = pltpu.get_barrier_semaphore()
    peers = []
    for radix, stride in stages:
        digit = lax.rem(me // stride, radix)
        group = [
            me + (lax.rem(digit + step, radix) - digit) * stride for step in range(1, radix)
        ]
        peers.append((digit, group))
    total = sum(len(group) for _, group in peers)
    for _, group in peers:
        for peer in group:
            pl.semaphore_signal(
                barrier, inc=1, device_id=(section, peer), device_id_type=pl.DeviceIdType.MESH
            )
    pl.semaphore_wait(barrier, total)
    for index, (radix, stride) in enumerate(stages):
        digit, group = peers[index]
        held = slots[index]
        held[digit] = own_ref[...] if index == 0 else out_ref[...]
        copies = []
        for step, peer in enumerate(group):
            copy = pltpu.make_async_remote_copy(
                src_ref=held.at[digit],
                dst_ref=held.at[digit],
                send_sem=send_sem.at[index, step],
                recv_sem=recv_sem.at[index, step],
                device_id=(section, peer),
                device_id_type=pl.DeviceIdType.MESH,
            )
            copy.start()
            copies.append(copy)
        for copy in copies:
            copy.wait_recv()
        summed = held[0]
        for place in range(1, radix):
            summed = summed + held[place]
        out_ref[...] = summed
        for copy in copies:
            copy.wait_send()


def sum_over_groups(rows):
    stages = stages_of(lax.axis_size("dp"))
    widest = max(radix for radix, _ in stages)
    return pl.pallas_call(
        functools.partial(sum_kernel, stages),
        out_shape=jax.ShapeDtypeStruct(rows.shape, jnp.float32),
        in_specs=[pl.BlockSpec(memory_space=pltpu.VMEM)],
        out_specs=pl.BlockSpec(memory_space=pltpu.VMEM),
        scratch_shapes=[pltpu.VMEM((radix,) + rows.shape, jnp.float32) for radix, _ in stages]
        + [
            pltpu.SemaphoreType.DMA((len(stages), widest)),
            pltpu.SemaphoreType.DMA((len(stages), widest)),
        ],
        compiler_params=pltpu.CompilerParams(collective_id=0, has_side_effects=True),
        name="group_sum",
    )(rows)


def from_behind(shard, axis, by):
    size = lax.axis_size(axis)
    pairs = [(i, i + by) for i in range(size) if 0 <= i + by < size]
    return lax.ppermute(shard, axis, pairs)


def broadcast_rows(vector):
    return vector[..., None, None, None, :]


def affine_rows(normed, scale_by, offset_by):
    return normed * broadcast_rows(scale_by) + broadcast_rows(offset_by)


def silu_slope(active):
    sigmoid_of = jax.nn.sigmoid(active)
    return sigmoid_of * (1.0 + active * (1.0 - sigmoid_of))


def pixel_sums(values, pixel_weight):
    weighted = values * pixel_weight
    return jnp.stack(
        [jnp.sum(weighted, axis=(-4, -3, -2)), jnp.sum(weighted * values, axis=(-4, -3, -2))],
        axis=-2,
    )


def gradient_sums(upstream, normed, pixel_weight):
    weighted = upstream * pixel_weight
    return jnp.stack(
        [jnp.sum(weighted, axis=(-4, -3, -2)), jnp.sum(weighted * normed, axis=(-4, -3, -2))],
        axis=-2,
    )


def summed_members(members):
    rows = [member.reshape(-1, member.shape[-1]) for member in members]
    used = sum(row.shape[0] for row in rows)
    packed = jnp.concatenate(
        rows + [jnp.zeros((SUM_ROWS - used, rows[0].shape[-1]), jnp.float32)], axis=0
    )
    summed = sum_over_groups(packed)
    results = []
    offset = 0
    for member, row in zip(members, rows):
        results.append(summed[offset : offset + row.shape[0]].reshape(member.shape))
        offset += row.shape[0]
    return results


def normalize(values, moments, counted):
    average = moments[..., 0, :] / counted
    spread = moments[..., 1, :] / counted - average * average
    inverse = lax.rsqrt(spread + EPSILON)
    return ((values - broadcast_rows(average)) * broadcast_rows(inverse), inverse)


def norm_backward(upstream, normed, inverse, scale_by, sums, counted, pixel_weight):
    shift_part = broadcast_rows(sums[..., 0, :])
    scale_part = broadcast_rows(sums[..., 1, :])
    return (
        broadcast_rows(inverse * scale_by)
        * (upstream - (shift_part + normed * scale_part) / broadcast_rows(counted))
        * pixel_weight
    )


def window_blocks(values):
    leading = values.shape[:-3]
    height, breadth, channels = values.shape[-3:]
    return values.reshape(leading + (height // 2, 2, breadth // 2, 2, channels))


def soft_pool_blocks(blocks):
    summit = jnp.max(blocks, axis=(-4, -2), keepdims=True)
    return summit + jnp.log(jnp.mean(jnp.exp(blocks - summit), axis=(-4, -2), keepdims=True))


def soft_pool(values):
    pooled = soft_pool_blocks(window_blocks(values))
    return pooled.reshape(
        values.shape[:-3] + (values.shape[-3] // 2, values.shape[-2] // 2, values.shape[-1])
    )


def pool_back(upstream, values):
    blocks = window_blocks(values)
    pooled = soft_pool_blocks(blocks)
    weight_share = jnp.exp(blocks - pooled) * 0.25
    spread = upstream.reshape(pooled.shape) * weight_share
    return spread.reshape(values.shape)


def patch_columns(frames):
    height, breadth = (frames.shape[-3], frames.shape[-2])
    padding = [(0, 0)] * (frames.ndim - 3) + [(1, 1), (1, 1), (0, 0)]
    padded = jnp.pad(frames, padding)
    return jnp.concatenate(
        [
            padded[..., down_shift : down_shift + height, side_shift : side_shift + breadth, :]
            for down_shift in range(3)
            for side_shift in range(3)
        ],
        axis=-1,
    )


def columns_back(grad_columns, channels):
    height, breadth = (grad_columns.shape[-3], grad_columns.shape[-2])
    leading = [(0, 0)] * (grad_columns.ndim - 3)
    summed = None
    for tap_index in range(9):
        down_shift, side_shift = (tap_index // 3, tap_index % 3)
        piece_of = grad_columns[..., tap_index * channels : (tap_index + 1) * channels]
        placed = jnp.pad(
            piece_of, leading + [(down_shift, 2 - down_shift), (side_shift, 2 - side_shift), (0, 0)]
        )
        summed = placed if summed is None else summed + placed
    return summed[..., 1 : height + 1, 1 : breadth + 1, :]


def live_rows(pixel_weight, channels):
    live = jnp.sum(pixel_weight, axis=(-4, -3, -2, -1))
    return jnp.broadcast_to(live[:, None], (live.shape[0], channels))


def section_forward(frames, pixel_weight, weights):
    (
        first_conv,
        second_conv,
        squeeze,
        expand,
        task_conv,
        norm_gain,
        norm_shift,
        squeeze_gain,
        squeeze_shift,
    ) = weights
    channels = frames.shape[-1]
    tasks = squeeze.shape[0]
    input_columns = patch_columns(frames[0])
    first_pre = jnp.einsum(
        "mshwk,ok->mshwo", input_columns, first_conv, preferred_element_type=jnp.float32
    )
    first_moments = summed_members(
        [pixel_sums(first_pre, pixel_weight), live_rows(pixel_weight, channels)]
    )
    counted = first_moments[1] * (frames.shape[-3] * frames.shape[-2])
    first_normed, first_inverse = normalize(first_pre, first_moments[0], counted)
    first_output = jax.nn.silu(affine_rows(first_normed, norm_gain[0], norm_shift[0]))
    rounded_first = (first_output).astype(jnp.bfloat16)
    middle_columns = patch_columns(rounded_first)
    second_pre = jnp.einsum(
        "mshwk,ok->mshwo", middle_columns, second_conv, preferred_element_type=jnp.float32
    )
    earlier = frames[1:]
    narrow = jnp.einsum(
        "mshwc,trc->tmshwr",
        rounded_first,
        squeeze[:, :, :channels],
        preferred_element_type=jnp.float32,
    ) + jnp.einsum(
        "tmshwc,trc->tmshwr", earlier, squeeze[:, :, channels:], preferred_element_type=jnp.float32
    )
    middle_moments = summed_members([pixel_sums(second_pre, pixel_weight), pixel_sums(narrow, pixel_weight)])
    second_normed, second_inverse = normalize(second_pre, middle_moments[0], counted)
    narrow_normed, narrow_inverse = normalize(narrow, middle_moments[1], counted)
    shared_out = jax.nn.silu(affine_rows(second_normed, norm_gain[1], norm_shift[1]))
    rounded_hidden = jax.nn.silu(affine_rows(narrow_normed, squeeze_gain[:, None], squeeze_shift[:, None])).astype(
        jnp.bfloat16
    )
    widened = jnp.einsum(
        "tmshwr,tcr->tmshwc", rounded_hidden, expand, preferred_element_type=jnp.float32
    )
    mask_moments = summed_members([pixel_sums(widened, pixel_weight)])
    widened_normed, widened_inverse = normalize(widened, mask_moments[0], counted)
    task_mask = jax.nn.sigmoid(
        affine_rows(widened_normed, norm_gain[2 : 2 + tasks][:, None], norm_shift[2 : 2 + tasks][:, None])
    )
    rounded_attended = (task_mask * shared_out).astype(jnp.bfloat16)
    attended_columns = patch_columns(rounded_attended)
    task_pre = jnp.einsum(
        "tmshwk,tok->tmshwo", attended_columns, task_conv, preferred_element_type=jnp.float32
    )
    task_moments = summed_members([pixel_sums(task_pre, pixel_weight)])
    task_normed, task_inverse = normalize(task_pre, task_moments[0], counted)
    task_out = jax.nn.silu(
        affine_rows(task_normed, norm_gain[2 + tasks :][:, None], norm_shift[2 + tasks :][:, None])
    )
    pooled = jnp.concatenate([soft_pool(shared_out)[None], soft_pool(task_out)], axis=0)
    kept_state = (
        frames,
        counted,
        first_normed,
        first_inverse,
        rounded_first,
        second_normed,
        second_inverse,
        narrow_normed,
        narrow_inverse,
        rounded_hidden,
        widened_normed,
        widened_inverse,
        rounded_attended,
        task_normed,
        task_inverse,
    )
    return (pooled, kept_state)


def section_backward(upstream, kept_state, pixel_weight, squares, weights):
    (
        first_conv,
        second_conv,
        squeeze,
        expand,
        task_conv,
        norm_gain,
        norm_shift,
        squeeze_gain,
        squeeze_shift,
    ) = weights
    (
        frames,
        counted,
        first_normed,
        first_inverse,
        rounded_first,
        second_normed,
        second_inverse,
        narrow_normed,
        narrow_inverse,
        rounded_hidden,
        widened_normed,
        widened_inverse,
        rounded_attended,
        task_normed,
        task_inverse,
    ) = kept_state
    channels = frames.shape[-1]
    tasks = squeeze.shape[0]
    task_gain = norm_gain[2 + tasks :][:, None]
    mask_gain = norm_gain[2 : 2 + tasks][:, None]
    task_active = affine_rows(task_normed, task_gain, norm_shift[2 + tasks :][:, None])
    task_out = jax.nn.silu(task_active)
    grad_task_act = pool_back(upstream[1:], task_out) * silu_slope(task_active)
    task_sums, square_all = summed_members(
        [gradient_sums(grad_task_act, task_normed, pixel_weight), squares]
    )
    grad_task = norm_backward(
        grad_task_act, task_normed, task_inverse, task_gain, task_sums, counted, pixel_weight
    ).astype(jnp.bfloat16)
    attended_columns = patch_columns(rounded_attended)
    task_conv_grad = jnp.einsum(
        "tmshwo,tmshwk->tok", grad_task, attended_columns, preferred_element_type=jnp.float32
    )
    grad_attended = (
        columns_back(
            jnp.einsum(
                "tmshwo,tok->tmshwk", grad_task, task_conv, preferred_element_type=jnp.float32
            ),
            channels,
        )

    )
    second_active = affine_rows(second_normed, norm_gain[1], norm_shift[1])
    shared_out = jax.nn.silu(second_active)
    task_mask = jax.nn.sigmoid(affine_rows(widened_normed, mask_gain, norm_shift[2 : 2 + tasks][:, None]))
    grad_mask_act = grad_attended * shared_out * task_mask * (1.0 - task_mask)
    mask_sums = summed_members([gradient_sums(grad_mask_act, widened_normed, pixel_weight)])[0]
    grad_widened = norm_backward(
        grad_mask_act, widened_normed, widened_inverse, mask_gain, mask_sums, counted, pixel_weight
    ).astype(jnp.bfloat16)
    expand_grad = jnp.einsum(
        "tmshwc,tmshwr->tcr", grad_widened, rounded_hidden, preferred_element_type=jnp.float32
    )
    narrow_active = affine_rows(narrow_normed, squeeze_gain[:, None], squeeze_shift[:, None])
    grad_narrow_act = jnp.einsum(
        "tmshwc,tcr->tmshwr", grad_widened, expand, preferred_element_type=jnp.float32
    ) * silu_slope(narrow_active)
    grad_shared = pool_back(upstream[0], shared_out) + jnp.sum(grad_attended * task_mask, axis=0)
    grad_second_act = grad_shared * silu_slope(second_active)
    second_sums, narrow_sums = summed_members(
        [
            gradient_sums(grad_second_act, second_normed, pixel_weight),
            gradient_sums(grad_narrow_act, narrow_normed, pixel_weight),
        ]
    )
    grad_second = norm_backward(
        grad_second_act,
        second_normed,
        second_inverse,
        norm_gain[1],
        second_sums,
        counted,
        pixel_weight,
    ).astype(jnp.bfloat16)
    grad_narrow = norm_backward(
        grad_narrow_act,
        narrow_normed,
        narrow_inverse,
        squeeze_gain[:, None],
        narrow_sums,
        counted,
        pixel_weight,
    ).astype(jnp.bfloat16)
    middle_columns = patch_columns(rounded_first)
    second_conv_grad = jnp.einsum(
        "mshwo,mshwk->ok", grad_second, middle_columns, preferred_element_type=jnp.float32
    )
    earlier = frames[1:]
    squeeze_grad = jnp.concatenate(
        [
            jnp.einsum(
                "tmshwr,mshwc->trc", grad_narrow, rounded_first, preferred_element_type=jnp.float32
            ),
            jnp.einsum(
                "tmshwr,tmshwc->trc", grad_narrow, earlier, preferred_element_type=jnp.float32
            ),
        ],
        axis=-1,
    )
    grad_joined = jnp.einsum(
        "tmshwr,trc->tmshwc", grad_narrow, squeeze, preferred_element_type=jnp.float32
    )
    grad_first_out = (
        columns_back(
            jnp.einsum(
                "mshwo,ok->mshwk", grad_second, second_conv, preferred_element_type=jnp.float32
            ),
            channels,
        )
        + jnp.sum(grad_joined[..., :channels], axis=0)
    )
    grad_earlier = grad_joined[..., channels:]
    first_active = affine_rows(first_normed, norm_gain[0], norm_shift[0])
    grad_first_act = grad_first_out * silu_slope(first_active)
    first_sums = summed_members([gradient_sums(grad_first_act, first_normed, pixel_weight)])[0]
    grad_first = norm_backward(
        grad_first_act, first_normed, first_inverse, norm_gain[0], first_sums, counted, pixel_weight
    ).astype(jnp.bfloat16)
    input_columns = patch_columns(frames[0])
    first_conv_grad = jnp.einsum(
        "mshwo,mshwk->ok", grad_first, input_columns, preferred_element_type=jnp.float32
    )
    grad_shared_in = (
        columns_back(
            jnp.einsum("mshwo,ok->mshwk", grad_first, first_conv, preferred_element_type=jnp.float32),
            channels,
        )

    )
    grad_frames = jnp.concatenate([grad_shared_in[None], grad_earlier], axis=0)
    first_norm, second_norm, mask_norm, task_norm, narrow_norm = (
        jnp.sum(sums, axis=-3)
        for sums in (first_sums, second_sums, mask_sums, task_sums, narrow_sums)
    )
    norm_rows = jnp.concatenate(
        [first_norm[None], second_norm[None], mask_norm, task_norm], axis=0
    )
    weight_terms = (first_conv_grad, second_conv_grad, squeeze_grad, expand_grad, task_conv_grad)
    norm_terms = (norm_rows[:, 1], norm_rows[:, 0], narrow_norm[:, 1], narrow_norm[:, 0])
    return (grad_frames, weight_terms, norm_terms, square_all)


def shards(
    stream_in,
    image_count,
    out_grad,
    first_conv,
    second_conv,
    squeeze,
    expand,
    task_conv,
    norm_gain,
    norm_shift,
    squeeze_gain,
    squeeze_shift,
):
    weights = (
        first_conv[0],
        second_conv[0],
        squeeze[0],
        expand[0],
        task_conv[0],
        norm_gain[0],
        norm_shift[0],
        squeeze_gain[0],
        squeeze_shift[0],
    )
    maps_count, images, height, breadth, channels = stream_in.shape
    micro_count = image_count.shape[1]
    slot_count = images // micro_count
    leading_section = lax.axis_index("section") == 0
    live = jnp.arange(slot_count)[None, :] < image_count[0][:, None]
    pixel_weight = live.astype(jnp.float32)[:, :, None, None, None]

    def by_micro(maps):
        return maps.reshape((maps_count, micro_count, slot_count) + maps.shape[2:])

    def whole_pool(pooled):
        masked = pooled * pixel_weight
        squares = jnp.sum(masked * masked, axis=(1, 2, 3, 4, 5))
        return masked.astype(jnp.bfloat16), jnp.broadcast_to(squares[:, None], (maps_count, channels))

    one_pooled, one_state = section_forward(by_micro(stream_in), pixel_weight, weights)
    one_features, one_squares = whole_pool(one_pooled)
    arrived = from_behind(one_features, "section", 1)
    two_pooled, two_state = section_forward(arrived, pixel_weight, weights)
    two_features, two_squares = whole_pool(two_pooled)
    two_upstream = by_micro(out_grad).astype(jnp.float32) * pixel_weight
    two_back = section_backward(two_upstream, two_state, pixel_weight, two_squares, weights)
    sendback = two_back[0].astype(jnp.bfloat16)
    returned = from_behind(sendback, "section", -1)
    one_upstream = returned.astype(jnp.float32) * pixel_weight
    one_back = section_backward(one_upstream, one_state, pixel_weight, one_squares, weights)

    half = ((0, 0),) * 3 + ((0, height // 4), (0, breadth // 4), (0, 0))
    full = ((0, 0),) * 3 + ((0, height // 2), (0, breadth // 2), (0, 0))
    feature_out = jnp.where(leading_section, one_features, jnp.pad(two_features, half))
    feature_out = feature_out.reshape((maps_count, images) + feature_out.shape[3:])
    recorded = lax.optimization_barrier(sendback).astype(jnp.float32)
    input_grad_out = jnp.where(leading_section, one_back[0], jnp.pad(recorded, full))
    input_grad_out = input_grad_out.reshape((maps_count, images) + input_grad_out.shape[3:])
    reduced = tuple(
        lax.psum_scatter(
            jnp.where(leading_section, one, two).reshape(-1).astype(jnp.bfloat16),
            "dp",
            scatter_dimension=0,
            tiled=True,
        ).astype(jnp.float32)
        for one, two in zip(one_back[1], two_back[1])
    )
    norm_sums = tuple(
        jnp.where(leading_section, one, two) for one, two in zip(one_back[2], two_back[2])
    )
    live_images = jnp.sum(one_state[1][:, 0]) / (height * breadth)
    feature_pixels = jnp.where(leading_section, height * breadth // 4, height * breadth // 16)
    root_square = jnp.sqrt(
        jnp.where(leading_section, one_back[3], two_back[3])[:, 0]
        / (live_images * feature_pixels * channels)
    )
    return (
        feature_out[None],
        input_grad_out[None],
        reduced[0][None],
        reduced[1][None],
        reduced[2][None],
        reduced[3][None],
        reduced[4][None],
        norm_sums[0][None],
        norm_sums[1][None],
        norm_sums[2][None],
        norm_sums[3][None],
        root_square[None],
    )


TAPS = 9
MESH = pl.DeviceIdType.MESH
FIRST, SECOND, MASK, TASK, NARROW = 0, 1, 2, 5, 8
NORMS = 11
(F_FIRST, F_SECOND, B_FIRST, F_NARROW, F_MASK, F_TASK, B_NARROW, B_TASK, B_MASK) = range(9)
GROUPS_OF_SUMS = 9
(
    P_FIRST, P_OWN, P_NARROW, P_HIDDEN, P_MASK, P_MASKED, P_TASK, P_TASKED, P_SUMMED, P_POOL,
    P_ATTENDED,
    P_START, P_STARTED, P_SUMS, P_BACK, P_MASK_START, P_MASK_SUMS, P_MASK_BACK, P_FIRST_START,
    P_FIRST_SUMS,
) = range(20)
KIND_CORE = (0, 0, 1, 1, 0)


def sigmoid(active):
    return 0.5 * jnp.tanh(0.5 * active) + 0.5


def silu_parts(active):
    sigmoid_of = sigmoid(active)
    return active * sigmoid_of, sigmoid_of * (1.0 + active * (1.0 - sigmoid_of))


def dot_nt(left, right):
    return lax.dot_general(
        left, right, (((1,), (1,)), ((), ())), preferred_element_type=jnp.float32
    )


def dot_nn(left, right):
    return lax.dot_general(
        left, right, (((1,), (0,)), ((), ())), preferred_element_type=jnp.float32
    )


def loop(count, body, start=0):
    lax.fori_loop(start, count, lambda i, _: (body(i), 0)[1], 0)


def main_kernel(plan, *refs):
    (
        count_ref, stream, cotangent, gain_in, shift_in, narrow_gain, narrow_shift,
        w1, w2, sq, ex, tc,
        o_out, ig_out, norm_out, total_out, a_one, a_two, d_one, d_two,
        r_first, r_second, r_squeeze, r_expand, r_task,
        w1s, w2s, sqs, exs, tcs, params, params_away, x_one, x_two, og_ref, sg_ref,
        pads_one, pads_two, xh_one, xh_two, aux_one, aux_two, share_one, share_two,
        p_one, p_two, ub_one, ub_two, ab_one, ab_two, nb_one, nb_two,
        ex_in, ex_away, turned_one, turned_two, ig_one, ig_two, o_two,
        norm_one, norm_two, masks_one, masks_two, inv_one, inv_two, osq_one, osq_two,
        dr, gp, gpad, rows, tot, counts, wide, tbuf, square_kept, slots_one, slots_three, slots_four,
        held, dbuf, cols, stage, stage_flat,
        w_load, w_away, p_recv, p_send, sync_send, sync_recv, f_send, f_recv, b_send, b_recv,
        a_send, a_recv, d_send, d_recv, out_send, out_recv, t_send, t_own, r_recv, load_sem,
    ) = refs
    lines, mates, tasks, c = plan["lines"], plan["mates"], plan["tasks"], plan["channels"]
    high, across, live = plan["high"], plan["across"], plan["live"]
    hc = c // 2
    acc = dr.at[0]
    stage_squeeze, stage_expand = stage_flat, stage_flat.at[:, pl.ds(0, c)]
    micro = masks_one.shape[0]
    section = lax.axis_index("section")
    other = 1 - section
    me = lax.axis_index("dp")
    z, j = me // mates, lax.rem(me, mates)
    unit = c // lines
    pieces = unit // mates
    task_rows = tasks * c // lines
    kinds = (
        (0, unit), (unit, unit), (2 * unit, task_rows), (2 * unit + task_rows, task_rows),
        (2 * unit + 2 * task_rows, task_rows),
    )
    mine = pl.ds(pl.multiple_of(section * hc, hc), hc)
    theirs = pl.ds(pl.multiple_of(other * hc, hc), hc)

    def plane_tasks(line):
        return (task_rows * line) // c, (task_rows * (line + 1) - 1) // c

    def plane_needs(line, task):
        first, last = plane_tasks(line)
        return (first <= task) & (task <= last)

    def mate(step):
        return z * mates + lax.rem(j + step, mates)

    def liner(step):
        return lax.rem(z + step, lines) * mates + j

    def remote(source, target, send, recv, to, device):
        return pltpu.make_async_remote_copy(
            src_ref=source, dst_ref=target, send_sem=send, recv_sem=recv,
            device_id=(to, device), device_id_type=MESH,
        )

    def got(some, recv):
        remote(some, some, sync_send.at[0, 0], recv, section, me).wait_recv()

    def sent(some, send):
        remote(some, some, send, sync_recv.at[0, 0], section, me).wait_send()

    def push(source, target, send, recv, to, device, own=None):
        same = (section == to) & (me == device)

        @pl.when(same)
        def _():
            pltpu.make_async_copy(source, target, recv if own is None else own).start()

        @pl.when(jnp.logical_not(same))
        def _():
            remote(source, target, send, recv, to, device).start()

    def pushed(some, send, to, device, own=None):
        same = (section == to) & (me == device)

        @pl.when(jnp.logical_not(same))
        def _():
            sent(some, send)

        if own is not None:

            @pl.when(same)
            def _():
                pltpu.make_async_copy(some, some, own).wait()

    def across_cores(source, target, send, recv):
        remote(source, target, send, recv, other, me).start()

    def sums_at(block, group):
        if group < 3:
            ref, at, count = slots_one, 3 * block + group, 2 if group + block == 0 else 1
        elif group < 7:
            ref, at, count = slots_three, 4 * block + group - 3, 3
        else:
            ref, at, count = slots_four, 2 * block + group - 7, 4
        return ref.at[at], count, GROUPS_OF_SUMS * block + group

    def sums_place(block, group, stage, digits):
        ref, count, _ = sums_at(block, group)
        return ref.at[stage, digits, pl.ds(0, count)]

    def sums_send(block, group, stage, digit, devices):
        at = sums_at(block, group)[2]
        here = sums_place(block, group, stage, digit)
        for device in devices:
            remote(
                here, here, sync_send.at[at, stage], sync_recv.at[at, stage], section, device
            ).start()

    def sums_got(block, group, stage, digits):
        ref, count, at = sums_at(block, group)
        got(sums_place(block, group, stage, pl.ds(0, digits - 1)), sync_recv.at[at, stage])
        summed = ref[stage, 0, pl.ds(0, count)]
        for digit in range(1, digits):
            summed = summed + ref[stage, digit, pl.ds(0, count)]
        return summed

    def sums_start(block, group):
        sums_send(block, group, 0, j, [mate(step) for step in range(1, mates)])

    def sums_mid(block, group):
        ref, count, _ = sums_at(block, group)
        ref[1, z, pl.ds(0, count)] = sums_got(block, group, 0, mates)
        sums_send(block, group, 1, z, [liner(step) for step in range(1, lines)])

    def sums_end(block, group):
        count = sums_at(block, group)[1]
        tot[pl.ds(0, count)] = sums_got(block, group, 1, lines)

    def sums_sent(block, group):
        at = sums_at(block, group)[2]
        for stage, digits in enumerate((mates, lines)):
            sent(
                sums_place(block, group, stage, pl.ds(0, digits - 1)), sync_send.at[at, stage]
            )

    half_rows = pl.ds(pl.multiple_of(section * hc, hc), hc)
    away_rows = pl.ds(pl.multiple_of(other * hc, hc), hc)
    third = 3 * c
    W_SQUEEZE, W_SECOND, W_EXPAND, W_TASK = 3, 4, 5, 6
    W_COUNT = W_TASK + tasks

    def weight_refs(index, block, which):
        if index < 3:
            lanes = pl.ds(index * third, third)
            return w1.at[which, lanes], w1s.at[block, :, lanes]
        if index >= W_TASK:
            return tc.at[index - W_TASK, which], tcs.at[block, index - W_TASK]
        source, target = {
            W_SQUEEZE: (sq, sqs), W_SECOND: (w2, w2s), W_EXPAND: (ex, exs),
        }[index]
        if index == W_SECOND:
            return source.at[which], target.at[block]
        return source.at[:, which], target.at[block]

    def load_weights(index):
        source, target = weight_refs(index, section, half_rows)
        pltpu.make_async_copy(source, target, w_load.at[section, index]).start()
        source, target = weight_refs(index, section, away_rows)
        across_cores(source, target, w_away.at[index], w_load.at[section, index])

    def weights_got(index, block):
        got(weight_refs(index, block, half_rows)[1], w_load.at[block, index])

    def make_block(b):
        leading = b == 0
        rows_high, rows_across, images = (
            (high, across, live) if leading else (high // 2, across // 2, 8)
        )
        per_row = images * rows_across
        n = rows_high * per_row
        wide_n = plan["wide"] if leading else 128
        pixels = float(rows_high * rows_across)
        half = per_row // 2
        pick = 0 if leading else 1
        (
            source, pads, xh, aux, share, p_act, ub, ab, nb, turned, ig,
            norm_sums, masks, inv, osq, a_ref, d_ref,
        ) = tuple(
            pair[pick]
            for pair in (
                (x_one, x_two), (pads_one, pads_two), (xh_one, xh_two), (aux_one, aux_two),
                (share_one, share_two), (p_one, p_two), (ub_one, ub_two), (ab_one, ab_two),
                (nb_one, nb_two),
                (turned_one, turned_two), (ig_one, ig_two), (norm_one, norm_two),
                (masks_one, masks_two), (inv_one, inv_two), (osq_one, osq_two),
                (a_one, a_two), (d_one, d_two),
            )
        )
        position = lax.rem(
            lax.broadcasted_iota(jnp.int32, (per_row, hc), 0), jnp.int32(rows_across)
        )
        even = lax.rem(position, jnp.int32(2)) == 0
        span = pl.ds(0, n)
        used = pl.ds(0, per_row)

        def each(body):
            for h in range(rows_high):
                body(h)

        def part(h):
            return pl.ds(h * per_row, per_row)

        def shifted(values):
            left = jnp.where(position >= 1, pltpu.roll(values, 1, 0), 0.0)
            right = jnp.where(position <= rows_across - 2, pltpu.roll(values, per_row - 1, 0), 0.0)
            return [v.astype(jnp.bfloat16) for v in (left, values, right)]

        def put_pad(pad, h, which, values):
            for side, v in enumerate(shifted(values)):
                lanes = side * c + which * hc
                lanes = lanes if isinstance(lanes, int) else pl.multiple_of(lanes, hc)
                pad[pl.ds((h + 1) * per_row, per_row), pl.ds(lanes, hc)] = v

        def trade_pad(k, index):
            for side in range(3):
                here = pads.at[
                    k, pl.ds(per_row, n), pl.ds(pl.multiple_of(side * c + section * hc, hc), hc)
                ]
                across_cores(here, here, f_send.at[b, index], f_recv.at[b, index])

        def pad_bytes():
            return pads.at[0, pl.ds(per_row, n), pl.ds(0, 3 * hc)]

        def conv_to(pad, weight, store_at, before=None):
            total_of = None
            for dy in range(3):
                if before is not None:
                    before(dy)
                one = dot_nt(
                    pad[pl.ds(dy * per_row, n), :], weight[:, pl.ds(dy * 3 * c, 3 * c)]
                )
                total_of = one if total_of is None else total_of + one
            store_at[...] = total_of

        def conv_back_half(which, weight, store_at):
            total_of = None
            for dy in range(3):
                taps = jnp.concatenate(
                    [
                        weight[
                            :, pl.ds(pl.multiple_of((dy * 3 + side) * c + which * hc, hc), hc)
                        ]
                        for side in range(3)
                    ],
                    axis=0,
                )
                one = dot_nn(gpad[pl.ds((2 - dy) * per_row, n), :], taps)
                total_of = one if total_of is None else total_of + one
            store_at[...] = total_of

        def write_stats(group, member, first, second):
            ref = sums_at(b, group)[0]
            for k in range(micro):
                weight = masks[k]
                ref[0, j, member, pl.ds(k, 1), :] = jnp.sum(first * weight, 0, keepdims=True)
                ref[0, j, member, pl.ds(micro + k, 1), :] = jnp.sum(
                    second * weight, 0, keepdims=True
                )

        def moments(group, member, values_ref):
            first = second = None
            for h in range(rows_high):
                v = values_ref[pl.ds(h * per_row, per_row), :]
                first = v if h == 0 else first + v
                second = v * v if h == 0 else second + v * v
            write_stats(group, member, first, second)

        def start(group):
            sums_start(b, group)

        def mid(group):
            sums_mid(b, group)

        def end(group):
            sums_end(b, group)

        def row(ref, k):
            return ref[pl.ds(k, 1), :]

        def total(member, k):
            return tot[member, pl.ds(k, 1), :]

        def norm_rows(index, member):
            mean_rows = inv_rows = None
            for k in range(micro):
                n_k = row(counts, k) * pixels
                mean = total(member, k) / n_k
                spread_of = total(member, micro + k) / n_k - mean * mean
                inverse = lax.rsqrt(spread_of + EPSILON)
                inv[index, pl.ds(k, 1), :] = inverse
                weight = masks[k]
                mean_rows = weight * mean if k == 0 else mean_rows + weight * mean
                inv_rows = weight * inverse if k == 0 else inv_rows + weight * inverse
            rows[0, used, :] = mean_rows
            rows[1, used, :] = inv_rows

        def normalized(index, h, raw):
            normed = (raw - rows[0, used, :]) * rows[1, used, :]
            xh[index, part(h), :] = normed
            return normed * params[b, 0, index] + params[b, 1, index]

        def back_rows(index, member):
            norm_sums[index] = tot[member]
            scale_rows = shift_rows = slope_rows = None
            for k in range(micro):
                n_k = row(counts, k) * pixels
                weight = masks[k]
                scale = inv[index, pl.ds(k, 1), :] * params[b, 0, index]
                by_shift = total(member, k) / n_k
                by_gain = total(member, micro + k) / n_k
                scale_rows = weight * scale if k == 0 else scale_rows + weight * scale
                shift_rows = weight * by_shift if k == 0 else shift_rows + weight * by_shift
                slope_rows = weight * by_gain if k == 0 else slope_rows + weight * by_gain
            rows[0, used, :] = scale_rows
            rows[1, used, :] = shift_rows
            rows[2, used, :] = slope_rows

        def partner(v):
            return jnp.where(even, pltpu.roll(v, per_row - 1, 0), pltpu.roll(v, 1, 0))

        def soft_pool(index, read):
            squares = None
            for pair in range(rows_high // 2):
                upper, lower = read(2 * pair), read(2 * pair + 1)
                top = jnp.maximum(upper, lower)
                top = jnp.maximum(top, partner(top))
                upper, lower = jnp.exp(upper - top), jnp.exp(lower - top)
                summed = upper + lower
                summed = summed + partner(summed)
                share[index, pl.ds(2 * pair * per_row, per_row), :] = upper / summed
                share[index, pl.ds((2 * pair + 1) * per_row, per_row), :] = lower / summed
                pooled = top + jnp.log(summed * 0.25)
                for lane in range(hc // 128):
                    wide[lane, used, :] = pooled[:, lane * 128 : (lane + 1) * 128]
                pooled = jnp.concatenate(
                    [wide[lane, pl.ds(0, half, stride=2), :] for lane in range(hc // 128)], axis=1
                )
                if leading:
                    kept = pooled
                    pooled = jnp.concatenate(
                        [pooled, jnp.zeros((32 - half, hc), jnp.float32)], axis=0
                    )
                    x_two[section, index, pl.ds(32 * pair, 32), :] = pooled.astype(jnp.bfloat16)
                else:
                    alive = lax.broadcasted_iota(jnp.int32, (half, hc), 0) < live * (
                        rows_across // 2
                    )
                    kept = jnp.where(alive, pooled, 0.0)
                    o_two[index, pl.ds(half * pair, half), :] = kept.astype(jnp.bfloat16)
                square = jnp.sum(kept * kept, 0, keepdims=True)
                squares = square if squares is None else squares + square
            osq[index] = squares
            if leading:
                across_cores(
                    x_two.at[section, index], x_two.at[section, index],
                    f_send.at[b, 7 + index], f_recv.at[b, 7 + index],
                )

        def widened(index, pair):
            if leading:
                upstream = sg_ref[index, pl.ds(pl.multiple_of(32 * pair, 32), 32), :]
                upstream = upstream.astype(jnp.float32)[:half]
            else:
                upstream = og_ref[index]
            for lane in range(hc // 128):
                piece = upstream[:, lane * 128 : (lane + 1) * 128]
                wide[lane, pl.ds(0, half, stride=2), :] = piece
                wide[lane, pl.ds(1, half, stride=2), :] = piece
            return jnp.concatenate(
                [wide[lane, used, :] for lane in range(hc // 128)], axis=1
            )

        pair_at = 2 * (z // 2)
        far_at = lines - 2 - pair_at
        inner = (z == 1) | (z == 2)

        def send_shared(which):
            from_ref = source.at[section, 0] if which == 0 else ub.at[span]
            neighbour = 2 * pair_at + 1 - z
            for at, plane in enumerate((z, neighbour)):
                push(
                    from_ref, a_ref.at[which, section, z], a_send.at[b, which, at],
                    a_recv.at[b, which, 0], 0, plane * mates + j,
                )

        def pair_lines(which, first):
            return a_ref.at[which, :, pl.ds(first, 2)]

        def relay_pair(which):
            got(pair_lines(which, 0), a_recv.at[b, which, 0])

            @pl.when(inner)
            def _():
                here = pair_lines(which, pair_at)
                remote(
                    here, here, a_send.at[b, which, 2], a_recv.at[b, which, 1], 0,
                    (lines - 1 - z) * mates + j,
                ).start()

        def relay_far(which):
            @pl.when(inner)
            def _():
                got(pair_lines(which, 0), a_recv.at[b, which, 1])
                here = pair_lines(which, far_at)
                remote(
                    here, here, a_send.at[b, which, 3], a_recv.at[b, which, 1], 0,
                    (2 * pair_at + 1 - z) * mates + j,
                ).start()

        def shared_got(which):
            @pl.when(jnp.logical_not(inner))
            def _():
                got(pair_lines(which, 0), a_recv.at[b, which, 1])

        def task_planes(task):
            first = (c * task) // task_rows
            return first, first + 1

        def task_slot(kind, task, plane):
            return 2 + 2 * kind + task - plane_tasks(plane)[0]

        def task_core(kind):
            return 0 if kind == 0 else 1

        def task_source(kind, task):
            return (
                source.at[section, 1 + task] if kind == 0
                else ab.at[task, section] if kind == 1 else nb.at[task]
            )

        def send_task(kind, task):
            first, last = task_planes(task)
            near = jnp.clip(z, first, last)
            passed_on = (z < first) | (z > last)
            tensor = 2 + tasks * kind + task
            push(
                task_source(kind, task), a_ref.at[task_slot(kind, task, near), section, z],
                a_send.at[b, tensor, 0],
                a_recv.at[b, tensor, jnp.where(passed_on, jnp.int32(0), jnp.int32(1))],
                task_core(kind), near * mates + j,
            )

            @pl.when(jnp.logical_not(passed_on))
            def _():
                opposite = first + last - z
                push(
                    task_source(kind, task),
                    a_ref.at[task_slot(kind, task, opposite), section, z],
                    a_send.at[b, tensor, 1], a_recv.at[b, tensor, 1], task_core(kind),
                    opposite * mates + j,
                )

        def task_passes(kind, task):
            first, last = task_planes(task)
            passes = []
            if first > 0:
                passes.append((first, 0, first, last))
            if last < lines - 1:
                passes.append((last, last + 1, lines - 1 - last, first))
            return passes

        def relay_task(kind, task):
            tensor = 2 + tasks * kind + task
            for plane, first, count, to_plane in task_passes(kind, task):

                @pl.when(z == plane)
                def _():
                    some = pl.ds(first, count)
                    here = a_ref.at[task_slot(kind, task, plane), :, some]
                    got(here, a_recv.at[b, tensor, 0])
                    remote(
                        here, a_ref.at[task_slot(kind, task, to_plane), :, some],
                        a_send.at[b, tensor, 2], a_recv.at[b, tensor, 1], task_core(kind),
                        to_plane * mates + j,
                    ).start()

        def task_got(kind, task):
            tensor = 2 + tasks * kind + task
            first, last = task_planes(task)
            for plane, count in ((first, lines - first), (last, last + 1)):

                @pl.when(z == plane)
                def _():
                    got(a_ref.at[0, :, pl.ds(0, count)], a_recv.at[b, tensor, 1])

        def gather_sent():
            one_piece = ub.at[span]
            for which in range(2):
                for at, plane in enumerate((z, 2 * pair_at + 1 - z)):
                    pushed(one_piece, a_send.at[b, which, at], 0, plane * mates + j)

                @pl.when(inner & (section == 0))
                def _():
                    for at in (2, 3):
                        sent(pair_lines(which, 0), a_send.at[b, which, at])

            for kind in range(3):
                for task in range(tasks):
                    first, last = task_planes(task)
                    tensor = 2 + tasks * kind + task
                    near = jnp.clip(z, first, last)
                    pushed(
                        one_piece, a_send.at[b, tensor, 0], task_core(kind), near * mates + j
                    )

                    @pl.when((z == first) | (z == last))
                    def _():
                        pushed(
                            one_piece, a_send.at[b, tensor, 1], task_core(kind),
                            (first + last - z) * mates + j,
                        )

                    for plane, _, count, _ in task_passes(kind, task):

                        @pl.when((z == plane) & (section == task_core(kind)))
                        def _():
                            sent(a_ref.at[0, :, pl.ds(0, count)], a_send.at[b, tensor, 2])

        def spread_place(kind, task, k):
            offset, _ = kinds[kind]
            if kind < 2:
                return kind, 2 * section + k, offset
            number = lines * task + 2 * section + k
            at = pl.multiple_of(offset + lax.rem(number, tasks) * unit, unit)
            return 2 + tasks * (kind - 2) + task, number // tasks, at

        def spread(kind, task=0):
            for k in range(2):
                index, plane, offset = spread_place(kind, task, k)
                push(
                    turned.at[index, pl.ds(k * unit, unit)],
                    d_ref.at[z, pl.ds(offset, unit)],
                    d_send.at[b, index, k], d_recv.at[b, kind],
                    KIND_CORE[kind], plane * mates + j,
                )

        def spread_sent(kind, task=0):
            for k in range(2):
                index, plane, _ = spread_place(kind, task, k)
                pushed(
                    turned.at[index, pl.ds(k * unit, unit)], d_send.at[b, index, k],
                    KIND_CORE[kind], plane * mates + j,
                )

        def spread_got(kind):
            offset, count = kinds[kind]
            got(d_ref.at[:, pl.ds(offset, count)], d_recv.at[b, kind])

        def rounded(index, member, slot, turned_at):
            back_rows(index, member)

            def body(h):
                value = rows[0, used, :] * (
                    dr[slot, part(h), :] - rows[1, used, :] - xh[index, part(h), :] * rows[2, used, :]
                )
                tbuf[part(h), :] = value
                for side, v in enumerate(reversed(shifted(value))):
                    gpad[pl.ds((h + 1) * per_row, per_row), pl.ds(side * hc, hc)] = v

            each(body)
            turned[turned_at] = jnp.transpose(tbuf[pl.ds(0, wide_n), :]).astype(jnp.bfloat16)

        def middle():
            return gpad[pl.ds(per_row, n), pl.ds(hc, hc)]

        def give(index):
            across_cores(
                ex_away.at[index, span], ex_in.at[index, span], b_send.at[b, index], b_recv.at[b, index]
            )

        def taken(index):
            got(ex_in.at[index, span], b_recv.at[b, index])

        def center(k, lanes):
            return pads[k, pl.ds(per_row, n), lanes]

        own_center = pl.ds(pl.multiple_of(c + section * hc, hc), hc)
        other_center = pl.ds(pl.multiple_of(c + other * hc, hc), hc)

        def forward_start():
            if not leading:
                got(x_two.at[0, 0], f_recv.at[0, 7])

            def first_pad(h):
                for which in range(2):
                    put_pad(
                        pads.at[1], h, which, source[which, 0, part(h), :].astype(jnp.float32)
                    )

            each(first_pad)
            if leading:
                conv_to(
                    pads.at[1], w1s.at[b], xh.at[FIRST],
                    lambda dy: got(w1s.at[b, :, pl.ds(0, third)], w_load.at[b, dy]),
                )
            else:
                for dy in range(3):
                    got(w1s.at[b, :, pl.ds(0, third)], w_load.at[b, dy])
                conv_to(pads.at[1], w1s.at[b], xh.at[FIRST])
            moments(F_FIRST, 0, xh.at[FIRST])
            start(F_FIRST)

        def forward(pump):
            if leading:
                load_weights(W_SECOND)
            else:
                for index in range(1, 1 + tasks):
                    got(x_two.at[0, index], f_recv.at[0, 7 + index])
            weights_got(W_SQUEEZE, b)

            def outer_narrow(task):
                xh[NARROW + task] = dot_nt(
                    source[0, 1 + task], sqs[b, task, :, pl.ds(c, hc)]
                ) + dot_nt(source[1, 1 + task], sqs[b, task, :, pl.ds(c + hc, hc)])

            loop(tasks, outer_narrow)
            if leading:
                mid(F_FIRST)
            pump(P_FIRST, 0)
            end(F_FIRST)
            if leading:
                counts[...] = tot[1]
                got(params.at[0], p_recv.at[other])
            norm_rows(FIRST, 0)

            def first_act(h):
                active, slope = silu_parts(normalized(FIRST, h, xh[FIRST, part(h), :]))
                aux[FIRST, part(h), :] = slope
                ub[part(h), :] = active.astype(jnp.bfloat16)
                put_pad(pads.at[0], h, section, active)

            each(first_act)
            trade_pad(0, 0)
            if leading:
                load_weights(W_EXPAND)

            def narrow_own(task):
                pump(P_OWN, task)
                xh[NARROW + task] += dot_nt(center(0, own_center), sqs[b, task, :, mine])

            loop(tasks, narrow_own)
            got(pad_bytes(), f_recv.at[b, 0])

            def narrow(task):
                xh[NARROW + task] += dot_nt(center(0, other_center), sqs[b, task, :, theirs])
                moments(F_NARROW, task, xh.at[NARROW + task])

            loop(tasks, narrow)
            start(F_NARROW)
            if leading:
                load_weights(W_TASK)
            weights_got(W_SECOND, b)
            conv_to(pads.at[0], w2s.at[b], acc.at[span])
            mid(F_NARROW)
            moments(F_SECOND, 0, acc)
            start(F_SECOND)
            pump(P_NARROW, 0)
            weights_got(W_EXPAND, b)
            end(F_NARROW)

            def hidden(task):
                norm_rows(NARROW + task, task)

                def act(h):
                    active, slope = silu_parts(
                        normalized(NARROW + task, h, xh[NARROW + task, part(h), :])
                    )
                    aux[NARROW + task, part(h), :] = slope
                    ab[task, section, part(h), :] = active.astype(jnp.bfloat16)

                each(act)
                across_cores(
                    ab.at[task, section], ab.at[task, section],
                    f_send.at[b, 1 + task], f_recv.at[b, 1 + task],
                )
                pump(P_HIDDEN, task)

            loop(tasks, hidden)
            mid(F_SECOND)
            if leading:
                load_weights(W_TASK + 1)

            def mask_own(task):
                xh[MASK + task] = dot_nt(ab[task, section], exs[b, task, :, mine])

            loop(tasks, mask_own)

            def mask_of(task):
                got(ab.at[task, 0], f_recv.at[b, 1 + task])
                xh[MASK + task] += dot_nt(ab[task, other], exs[b, task, :, theirs])
                moments(F_MASK, task, xh.at[MASK + task])

            loop(tasks, mask_of)
            start(F_MASK)
            pump(P_MASK, 0)
            if leading:
                for index in range(W_TASK + 2, W_COUNT):
                    load_weights(index)
            end(F_SECOND)
            norm_rows(SECOND, 0)

            def second_act(h):
                active, slope = silu_parts(normalized(SECOND, h, acc[part(h), :]))
                aux[SECOND, part(h), :] = slope
                p_act[part(h), :] = active

            each(second_act)
            mid(F_MASK)
            pump(P_MASKED, 0)
            soft_pool(0, lambda h: p_act[pl.ds(h * per_row, per_row), :])
            end(F_MASK)

            def attend(task):
                norm_rows(MASK + task, task)
                pad = pads.at[1 + task]

                def act(h):
                    active = normalized(MASK + task, h, xh[MASK + task, part(h), :])
                    sigmoid_of = sigmoid(active)
                    aux[MASK + task, part(h), :] = sigmoid_of
                    attended = sigmoid_of * p_act[part(h), :]
                    nb[task, part(h), :] = attended.astype(jnp.bfloat16)
                    put_pad(pad, h, section, attended)

                each(act)
                trade_pad(1 + task, 4 + task)

            loop(tasks, attend)
            pump(P_ATTENDED, 0)

            def task_conv(task):
                got(tcs.at[b, 0], w_load.at[b, W_TASK + task])
                got(pad_bytes(), f_recv.at[b, 4 + task])
                conv_to(pads.at[1 + task], tcs.at[b, task], xh.at[TASK + task])
                moments(F_TASK, task, xh.at[TASK + task])
                pump(P_TASK, task)

            loop(tasks, task_conv)
            start(F_TASK)
            pump(P_TASKED, 0)
            mid(F_TASK)
            pump(P_SUMMED, 0)
            end(F_TASK)

            def task_pool(task):
                norm_rows(TASK + task, task)

                def act(h):
                    active, slope = silu_parts(
                        normalized(TASK + task, h, xh[TASK + task, part(h), :])
                    )
                    aux[TASK + task, part(h), :] = slope
                    acc[part(h), :] = active

                each(act)
                soft_pool(1 + task, lambda h: acc[pl.ds(h * per_row, per_row), :])
                pump(P_POOL, task)

            loop(tasks, task_pool)
            squares = sums_at(b, B_TASK)[0]
            squares[0, j, tasks] = jnp.zeros((8, hc), jnp.float32)
            for index in range(1 + tasks):
                squares[0, j, tasks, pl.ds(index, 1), :] = osq[index]

        DU, DE, DX = 2 * tasks, 2 * tasks + 1, 3 * tasks + 1

        def backward_start(pump):
            def task_start(task):
                first = second = None
                for pair in range(rows_high // 2):
                    upstream = widened(1 + task, pair)
                    for h in (2 * pair, 2 * pair + 1):
                        at = pl.ds(h * per_row, per_row)
                        up = upstream * share[1 + task, at, :] * aux[TASK + task, at, :]
                        dr[task, at, :] = up
                        by = up * xh[TASK + task, at, :]
                        first = up if first is None else first + up
                        second = by if second is None else second + by
                write_stats(B_TASK, task, first, second)
                pump(P_START, task)

            loop(tasks, task_start)
            start(B_TASK)

        def backward(pump):
            if not leading:
                mid(B_TASK)
            pump(P_SUMS, 0)
            end(B_TASK)
            square_kept[b] = tot[tasks]

            def task_back(task):
                rounded(TASK + task, task, task, 2 + task)
                spread(2, task)
                conv_back_half(other, tcs.at[b, task], ex_away.at[task, span])
                give(task)
                conv_back_half(section, tcs.at[b, task], dr.at[task, span])
                pump(P_BACK, task)

            loop(tasks, task_back)

            def task_through(task):
                taken(task)
                first = second = None
                for h in range(rows_high):
                    at = pl.ds(h * per_row, per_row)
                    grad = dr[task, at, :] + ex_in[task, at, :]
                    m, p = aux[MASK + task, at, :], p_act[at, :]
                    through = grad * m

                    @pl.when(task == 0)
                    def _():
                        gp[at, :] = through

                    @pl.when(task > 0)
                    def _():
                        gp[at, :] += through

                    up = through * p * (1.0 - m)
                    dr[task, at, :] = up
                    by = up * xh[MASK + task, at, :]
                    first = up if first is None else first + up
                    second = by if second is None else second + by
                write_stats(B_MASK, task, first, second)

            loop(tasks, task_through)
            first = second = None
            for pair in range(rows_high // 2):
                upstream = widened(0, pair)
                for h in (2 * pair, 2 * pair + 1):
                    at = pl.ds(h * per_row, per_row)
                    up = (gp[at, :] + upstream * share[0, at, :]) * aux[SECOND, at, :]
                    dr[3, at, :] = up
                    by = up * xh[SECOND, at, :]
                    first = up if first is None else first + up
                    second = by if second is None else second + by
            write_stats(B_MASK, tasks, first, second)
            start(B_MASK)
            pump(P_MASK_START, 0)
            mid(B_MASK)
            pump(P_MASK_SUMS, 0)
            end(B_MASK)

            def mask_back(task):
                rounded(MASK + task, task, task, 5 + task)
                spread(3, task)
                ex_away[tasks + task, span] = dot_nn(middle(), exs[b, task, :, theirs])
                give(tasks + task)
                dr[task, span] = dot_nn(middle(), exs[b, task, :, mine])
                pump(P_MASK_BACK, task)

            loop(tasks, mask_back)
            rounded(SECOND, tasks, 3, 1)
            spread(1)

            def mask_through(task):
                taken(tasks + task)
                first = second = None
                for h in range(rows_high):
                    at = pl.ds(h * per_row, per_row)
                    up = (dr[task, at, :] + ex_in[tasks + task, at, :]) * aux[
                        NARROW + task, at, :
                    ]
                    dr[task, at, :] = up
                    by = up * xh[NARROW + task, at, :]
                    first = up if first is None else first + up
                    second = by if second is None else second + by
                write_stats(B_NARROW, task, first, second)

            loop(tasks, mask_through)
            start(B_NARROW)
            conv_back_half(other, w2s.at[b], ex_away.at[DU, span])
            mid(B_NARROW)
            conv_back_half(section, w2s.at[b], gp.at[span])
            end(B_NARROW)

            def narrow_back(task):
                rounded(NARROW + task, task, task, 8 + task)
                spread(4, task)
                low = middle()
                ex_away[DU, span] += dot_nn(low, sqs[b, task, :, theirs])
                ex_away[DE + task, span] = dot_nn(
                    low, sqs[b, task, :, pl.ds(pl.multiple_of(c + other * hc, hc), hc)]
                )
                give(DE + task)
                gp[span, :] += dot_nn(low, sqs[b, task, :, mine])
                ig[1 + task] = dot_nn(
                    low, sqs[b, task, :, pl.ds(pl.multiple_of(c + section * hc, hc), hc)]
                )

            loop(tasks, narrow_back)
            give(DU)

            def outer_grad(index, slot):
                taken(slot)
                grad = ig[index] + ex_in[slot, span]
                if leading:
                    ig[index] = grad
                else:
                    low = grad.astype(jnp.bfloat16)
                    sg_ref[index] = low
                    ig[index] = low.astype(jnp.float32)
                push(
                    ig.at[index], ig_out.at[section, index, span], out_send.at[b, index],
                    out_recv.at[0], b, me,
                )

            loop(tasks, lambda t: outer_grad(1 + t, DE + t))
            taken(DU)
            first = second = None
            for h in range(rows_high):
                at = pl.ds(h * per_row, per_row)
                up = (gp[at, :] + ex_in[DU, at, :]) * aux[FIRST, at, :]
                dr[3, at, :] = up
                by = up * xh[FIRST, at, :]
                first = up if first is None else first + up
                second = by if second is None else second + by
            write_stats(B_FIRST, 0, first, second)
            start(B_FIRST)
            pump(P_FIRST_START, 0)
            mid(B_FIRST)
            pump(P_FIRST_SUMS, 0)
            end(B_FIRST)
            rounded(FIRST, 0, 3, 0)
            spread(0)
            conv_back_half(other, w1s.at[b], ex_away.at[DX, span])
            give(DX)
            conv_back_half(section, w1s.at[b], ig.at[0])
            outer_grad(0, DX)
            push(
                norm_sums, norm_out.at[section], out_send.at[b, 4], out_recv.at[1], b, me
            )
            push(
                square_kept.at[b], total_out.at[section, 1], out_send.at[b, 5],
                out_recv.at[2], b, me,
            )
            push(counts, total_out.at[section, 0], out_send.at[b, 6], out_recv.at[2], b, me)
            from_o = x_two.at[section] if leading else o_two
            count = 64 if leading else o_two.shape[1]
            push(
                from_o, o_out.at[section, :, pl.ds(0, count)], out_send.at[b, 7],
                out_recv.at[3], b, me,
            )

        def settle():
            gather_sent()
            for kind in range(2):
                spread_sent(kind)
            for kind in range(2, 5):
                for task in range(tasks):
                    spread_sent(kind, task)
            for index in range(1 + 2 * tasks):
                size = pad_bytes() if index == 0 or index > tasks else ab.at[0, 0]
                sent(size, f_send.at[b, index])
            if leading:
                for index in range(1 + tasks):
                    sent(x_two.at[0, 0], f_send.at[b, 7 + index])
            for group in range(GROUPS_OF_SUMS):
                sums_sent(b, group)
            for index in range(1 + tasks):
                pushed(ig.at[0], out_send.at[b, index], b, me)
            pushed(norm_sums, out_send.at[b, 4], b, me)
            pushed(counts, out_send.at[b, 5], b, me)
            pushed(counts, out_send.at[b, 6], b, me)
            pushed(x_two.at[0] if leading else o_two, out_send.at[b, 7], b, me)

        def exchanged():
            loop(NORMS, lambda index: sent(ex_away.at[0, span], b_send.at[b, index]))

        def results_got():
            got(ig_out.at[:, :, span], out_recv.at[0])
            got(norm_out, out_recv.at[1])
            got(total_out, out_recv.at[2])
            count = 64 if leading else o_two.shape[1]
            got(o_out.at[:, :, pl.ds(0, count)], out_recv.at[3])

        deep = lines * wide_n

        def fetch(from_ref, target, index):
            copy = pltpu.make_async_copy(from_ref, target, load_sem.at[index])
            copy.start()
            return copy

        def hold(at):
            return [
                fetch(
                    a_ref.at[at, which], held.at[:, span, pl.ds(which * hc, hc)], which
                )
                for which in range(2)
            ]

        def rows_held():
            return held[:, pl.ds(0, wide_n), :].reshape(deep, c)

        def slot_of(piece):
            return (task_rows * z + piece * unit) // c - plane_tasks(z)[0]

        def clear_tail():
            held[:, pl.ds(n, wide_n - n), :] = jnp.zeros((lines, wide_n - n, c), jnp.bfloat16)

        per_unit = task_rows // mates // pieces

        def piece_place(kind, piece, part):
            if kind < 2:
                return part, 0, (r_first, r_second)[kind], kind
            number = mates * piece + part
            return number // per_unit, number % per_unit, r_task, 2 + piece

        def conv_unit(kind, piece, buffer):
            offset, _ = kinds[kind]
            copies = hold(kind if kind < 2 else 2 + 2 * 2 + slot_of(piece))
            copies.append(
                fetch(
                    d_ref.at[:, pl.ds(offset + piece * unit, unit)],
                    dbuf.at[:, :, pl.ds(0, wide_n)], 2,
                )
            )
            for copy in copies:
                copy.wait()
            here = lax.rem(
                lax.broadcasted_iota(jnp.int32, (unit, wide_n), 1), jnp.int32(rows_across)
            )

            def side_terms(side):
                def line_cols(line):
                    value = dbuf[line, :, pl.ds(0, wide_n)].astype(jnp.float32)
                    if side == 0:
                        value = jnp.where(
                            here <= rows_across - 2, pltpu.roll(value, wide_n - 1, 1), 0.0
                        )
                    elif side == 2:
                        value = jnp.where(here >= 1, pltpu.roll(value, 1, 1), 0.0)
                    lanes = pl.ds(pl.multiple_of(line * wide_n, 128), wide_n)
                    for down in range(3):
                        shifted = value
                        if down == 0:
                            shifted = pltpu.roll(value, wide_n - per_row, 1)
                        elif down == 2:
                            shifted = pltpu.roll(value, per_row, 1)
                        cols[down, :, lanes] = shifted.astype(jnp.bfloat16)

                loop(lines, line_cols)

                def terms_of(down):
                    terms = dot_nn(cols[down, :, pl.ds(0, deep)], rows_held())
                    stage[buffer, :, pl.ds(pl.multiple_of((3 * down + side) * c, c), c)] = (
                        terms.astype(jnp.bfloat16)
                    )

                loop(3, terms_of)

            for side in range(3):
                side_terms(side)
            for part_at in range(mates):
                mate_at, at_row, target, index = piece_place(kind, piece, part_at)
                push(
                    stage.at[buffer, pl.ds(part_at * pieces, pieces)],
                    target.at[j, pl.ds(at_row * pieces, pieces)],
                    t_send.at[b, index, part_at], r_recv.at[index], b, z * mates + mate_at,
                    t_own.at[index, part_at],
                )

        def conv_unit_sent(kind, piece):
            for part_at in range(mates):
                mate_at, _, _, index = piece_place(kind, piece, part_at)
                pushed(
                    stage.at[0, pl.ds(0, pieces)], t_send.at[b, index, part_at], b,
                    z * mates + mate_at, t_own.at[index, part_at],
                )

        def flat_terms(kind, target, staged, index, parts):
            offset, _ = kinds[kind]
            copies = [
                fetch(
                    d_ref.at[line, pl.ds(offset + piece * unit, unit)],
                    cols.at[piece, :, pl.ds(line * wide_n, wide_n)], 3 + piece * lines + line,
                )
                for piece in range(tasks)
                for line in range(lines)
            ]
            for copy in copies:
                copy.wait()
            for at, a_kind in parts:
                if a_kind is None:
                    for copy in hold(1):
                        copy.wait()
                for piece in range(tasks):
                    if a_kind is not None:
                        for copy in hold(2 + 2 * a_kind + slot_of(piece)):
                            copy.wait()
                    terms = dot_nn(cols[piece, :, pl.ds(0, deep)], rows_held())
                    staged[pl.ds(piece * unit, unit), pl.ds(at, c)] = terms.astype(jnp.bfloat16)
            count = task_rows // mates
            for mate_at in range(mates):
                push(
                    staged.at[pl.ds(mate_at * count, count)], target.at[j],
                    t_send.at[b, index, mate_at], r_recv.at[index], b, z * mates + mate_at,
                    t_own.at[index, mate_at],
                )

        def flat_sent(staged, index):
            for mate_at in range(mates):
                pushed(
                    staged.at[pl.ds(0, task_rows // mates)], t_send.at[b, index, mate_at], b,
                    z * mates + mate_at, t_own.at[index, mate_at],
                )

        def free(name, waits):
            if name in in_use:
                in_use[name]()
            in_use[name] = waits

        def staged_conv(kind, piece, core):
            buffer = turn[core] % 2
            turn[core] += 1
            free((core, buffer), lambda: conv_unit_sent(kind, piece))
            conv_unit(kind, piece, buffer)

        def terms_second():
            spread_got(1)
            shared_got(1)
            staged_conv(1, 0, 0)

        def terms_first():
            spread_got(0)
            shared_got(0)
            staged_conv(0, 0, 0)

        def terms_squeeze():
            spread_got(4)
            for task in range(tasks):
                task_got(0, task)
            free((0, 2), lambda: flat_sent(stage_squeeze, 5))
            flat_terms(4, r_squeeze, stage_squeeze, 5, [(0, None), (c, 0)])

        def terms_expand():
            spread_got(3)
            for task in range(tasks):
                task_got(1, task)
            free((1, 2), lambda: flat_sent(stage_expand, 6))
            flat_terms(3, r_expand, stage_expand, 6, [(0, 1)])

        def terms_task(piece):
            if piece == 0:
                spread_got(2)
                for task in range(tasks):
                    task_got(2, task)
            staged_conv(2, piece, 1)

        def terms_got():
            def senders(kind):
                return pl.ds(0, mates - 1 if KIND_CORE[kind] == b else mates)

            for kind, index, target in (
                (0, 0, r_first), (1, 1, r_second), (4, 5, r_squeeze), (3, 6, r_expand)
            ):
                got(target.at[senders(kind)], r_recv.at[index])
            for piece in range(tasks):
                for mate_at in range(mates):
                    count = sum(
                        (mates * piece + part_at) // per_unit == mate_at
                        for part_at in range(mates)
                    )
                    if count:

                        @pl.when(j == mate_at)
                        def _():
                            some = r_task.at[senders(2), pl.ds(0, count * pieces)]
                            got(some, r_recv.at[2 + piece])

        def set_up():
            image = lax.div(
                lax.broadcasted_iota(jnp.int32, (per_row, hc), 0), jnp.int32(rows_across)
            )
            for k in range(micro):
                masks[k] = (
                    jnp.where(image == k, 1.0, 0.0)
                    + jnp.where(image == micro, fourth[k], 0.0)
                    + jnp.where(image == micro + 1, fifth[k], 0.0)
                )
            zero = jnp.zeros((per_row, 3 * c), jnp.bfloat16)
            for pad in range(1 + tasks):
                pads[pad, pl.ds(0, per_row), :] = zero
                pads[pad, pl.ds(n + per_row, per_row), :] = zero

        def back_set_up():
            zero = jnp.zeros((per_row, 3 * hc), jnp.bfloat16)
            gpad[pl.ds(0, per_row), :] = zero
            gpad[pl.ds(n + per_row, per_row), :] = zero
            tbuf[pl.ds(n, wide_n - n), :] = jnp.zeros((wide_n - n, hc), jnp.float32)

        return types.SimpleNamespace(
            forward_start=forward_start, forward=forward, backward_start=backward_start,
            backward=backward, settle=settle, exchanged=exchanged, results_got=results_got,
            mid=mid, set_up=set_up, back_set_up=back_set_up, clear_tail=clear_tail,
            second=terms_second, first=terms_first, squeeze=terms_squeeze, expand=terms_expand,
            task=terms_task, terms_got=terms_got, send_shared=send_shared, send_task=send_task,
            relay_pair=relay_pair, relay_far=relay_far, relay_task=relay_task,
        )

    barrier = pltpu.get_barrier_semaphore()
    greeted = (
        [(section, mate(step)) for step in range(1, mates)]
        + [(section, liner(step)) for step in range(1, lines)]
        + [(other, mate(step)) for step in range(mates)]
        + [(other, liner(step)) for step in range(1, lines)]
    )
    for device in greeted:
        pl.semaphore_signal(barrier, inc=1, device_id=device, device_id_type=MESH)
    numbers = [count_ref[0, k] for k in range(micro)]
    double = [jnp.where(number >= 2, jnp.float32(1.0), jnp.float32(0.0)) for number in numbers]
    fourth, fifth = [], []
    before = jnp.float32(0.0)
    for k in range(micro):
        fourth.append(double[k] * (1.0 - before))
        fifth.append(double[k] * before)
        before = before + double[k]
    count_slot = sums_at(0, F_FIRST)[0]
    count_slot[0, j, 1] = jnp.zeros((8, hc), jnp.float32)
    for k in range(micro):
        count_slot[0, j, 1, pl.ds(k, 1), :] = jnp.full((1, hc), 1.0) * (1.0 + double[k])
    for index in range(NORMS):
        at = pl.ds(index if index < NARROW else index - NARROW, 1)
        for which, (wider, narrower) in enumerate(
            ((gain_in, narrow_gain), (shift_in, narrow_shift))
        ):
            from_ref = wider if index < NARROW else narrower
            params[section, which, index] = from_ref[at, mine]
            params_away[which, index] = from_ref[at, theirs]
    pl.semaphore_wait(barrier, len(greeted))
    for index in range(W_SECOND):
        load_weights(index)
    across_cores(params_away, params.at[section], p_send.at[0], p_recv.at[section])
    in_use, turn = {}, [0, 0]
    one, two = make_block(0), make_block(1)

    def compact(index):
        for h in range(high):
            doubles = [
                stream[index, 2 * k + 1, h].astype(jnp.float32) for k in range(micro)
            ]
            rows_of = [stream[index, 2 * k, h].astype(jnp.float32) for k in range(micro)]
            for weight in (fourth, fifth):
                picked = doubles[0] * weight[0]
                for k in range(1, micro):
                    picked = picked + doubles[k] * weight[k]
                rows_of.append(picked)
            whole = jnp.concatenate(rows_of, axis=0).astype(jnp.bfloat16)
            at = pl.ds(h * live * across, live * across)
            for which in range(2):
                x_one[which, index, at, :] = whole[:, which * hc : (which + 1) * hc]

    one.set_up()
    loop(1 + tasks, compact)
    def on(core, *bodies):
        @pl.when(section == core)
        def _():
            for body in bodies:
                body()

    def cotangents():
        for index in range(1 + tasks):
            doubles = [cotangent[index, 2 * k + 1, 0].astype(jnp.float32) for k in range(micro)]
            rows_of = [cotangent[index, 2 * k, 0].astype(jnp.float32) for k in range(micro)]
            for weight in (fourth, fifth):
                picked = doubles[0] * weight[0]
                for k in range(1, micro):
                    picked = picked + doubles[k] * weight[k]
                rows_of.append(picked)
            og_ref[index] = jnp.zeros(og_ref.shape[1:], jnp.float32)
            for i, upstream in enumerate(rows_of):
                mine_of = jnp.where(section == 0, upstream[:, :hc], upstream[:, hc:])
                og_ref[index, pl.ds(i * (across // 4), across // 4), :] = mine_of

    def passes(block, kind):
        def run():
            for task in range(tasks):
                block.relay_task(kind, task)

        return run

    def one_forward(place, t):
        if place == P_FIRST:
            one.send_shared(0)
            two.set_up()
        elif place == P_HIDDEN:
            one.send_task(0, t)
        elif place == P_MASKED:
            on(0, lambda: one.relay_pair(0))
        elif place == P_ATTENDED:
            two.forward_start()
        elif place == P_TASKED:
            two.mid(F_FIRST)
            one.send_shared(1)
            on(0, lambda: one.relay_far(0))
        elif place == P_SUMMED:
            cotangents()
        elif place == P_POOL:
            one.send_task(1, t)

    def two_forward(place, t):
        if place == P_FIRST:
            on(0, lambda: one.relay_pair(1))
        elif place == P_NARROW:
            on(0, passes(one, 0))
        elif place == P_HIDDEN:
            one.send_task(2, t)
        elif place == P_MASK:
            on(0, lambda: one.relay_far(1))
            on(1, passes(one, 1))
        elif place == P_TASK:
            two.send_task(0, t)
        elif place == P_TASKED:
            on(1, passes(one, 2))
            two.back_set_up()
        elif place == P_SUMMED:
            two.send_shared(0)
        elif place == P_POOL:
            two.send_task(1, t)

    def two_backward(place, t):
        if place == P_SUMS:
            two.send_shared(1)
            on(0, lambda: two.relay_pair(0), passes(two, 0))
        elif place == P_BACK:
            two.send_task(2, t)
        elif place == P_MASK_START:
            on(0, lambda: two.relay_far(0), lambda: two.relay_pair(1))
            on(1, passes(two, 1))
        elif place == P_MASK_SUMS:
            on(0, lambda: two.relay_far(1))
        elif place == P_FIRST_START:
            one.backward_start(nothing)
        elif place == P_FIRST_SUMS:
            one.mid(B_TASK)
            on(1, passes(two, 2))

    def one_backward(place, t):
        if place == P_MASK_START:
            on(0, two.clear_tail, two.second)
            on(1, two.clear_tail, lambda: two.task(0))
        elif place == P_MASK_SUMS:
            on(0, two.squeeze)
            on(1, lambda: two.task(1))
        elif place == P_FIRST_START:
            on(0, two.first, one.clear_tail)
            on(1, lambda: two.task(2), two.expand, one.clear_tail)
        elif place == P_FIRST_SUMS:
            on(0, one.second)
            on(1, lambda: one.task(0))

    def nothing(place, t):
        pass

    one.forward_start()
    one.forward(one_forward)
    two.forward(two_forward)
    two.backward_start(two_backward)
    two.backward(two_backward)
    two.exchanged()
    one.back_set_up()
    one.backward(one_backward)
    on(0, one.squeeze, one.first)
    on(1, lambda: one.task(1), lambda: one.task(2), one.expand)
    for (core, _), waits in in_use.items():
        on(core, waits)
    one.exchanged()
    one.settle()
    two.settle()
    sent(params_away, p_send.at[0])
    for index in range(W_COUNT):
        sent(weight_refs(index, 0, away_rows)[1], w_away.at[index])
    on(0, one.results_got, one.terms_got)
    on(1, two.results_got, two.terms_got)


def result_kernel(plan, *refs):
    (
        count_ref, first, second, squeeze, expand, task, pooled, grads, norms, totals,
        first_out, second_out, squeeze_out, expand_out, task_out, feature_out, input_out,
        gain_out, shift_out, narrow_gain_out, narrow_shift_out, rms_out,
    ) = refs
    mates, tasks, c = plan["mates"], plan["tasks"], plan["channels"]
    section = lax.axis_index("section")
    live, micro = plan["live"], plan["micro"]
    images_of = []
    before = jnp.int32(micro)
    for k in range(micro):
        double = count_ref[0, k] >= 2
        images_of.append(jnp.where(double, before, jnp.int32(-1)))
        before = before + jnp.where(double, jnp.int32(1), jnp.int32(0))

    def joined(ref, index, at):
        return jnp.concatenate([ref[0, index, at, :], ref[1, index, at, :]], axis=1)

    def aligned(values, image, rows, used):
        start = image * rows
        values = pltpu.roll(values, values.shape[0] - start, 0) if start else values
        inside = lax.broadcasted_iota(jnp.int32, (8, c), 0) < used
        return jnp.where(inside, values[:8], 0.0)

    def by_slot(values, rows, used, store):
        two = [aligned(values, micro, rows, used), aligned(values, micro + 1, rows, used)]
        for k in range(micro):
            store(2 * k, aligned(values, k, rows, used))
            which = images_of[k]
            store(
                2 * k + 1,
                jnp.where(which == micro, two[0], jnp.where(which == micro + 1, two[1], 0.0)),
            )

    def place_out(high, across, images, leading):
        per_row = images * across
        for index in range(1 + tasks):
            for h in range(plan["high"]):

                def store(slot, values):
                    input_out[index, slot, h] = values

                if h < high:
                    at = pl.ds(h * per_row, per_row)
                    by_slot(joined(grads, index, at), across, across, store)
                else:
                    for slot in range(2 * micro):
                        store(slot, jnp.zeros((8, c), jnp.float32))
            for h in range(plan["high"] // 2):

                def store_feature(slot, values):
                    feature_out[index, slot, h] = values[: plan["across"] // 2].astype(
                        jnp.bfloat16
                    )

                if h < high // 2:
                    count = 8 * (across // 2)
                    by_slot(
                        joined(pooled, index, pl.ds(h * count, count)).astype(jnp.float32),
                        across // 2, across // 2, store_feature,
                    )
                else:
                    for slot in range(2 * micro):
                        store_feature(slot, jnp.zeros((8, c), jnp.float32))
        cells = float(high * across // 4 * c)
        live_total = jnp.sum(
            totals[0, 0, pl.ds(0, micro), pl.ds(0, 1)], axis=0, keepdims=True
        )
        lane = lax.broadcasted_iota(jnp.int32, (1, 1 + tasks), 1)
        result = jnp.zeros((1, 1 + tasks), jnp.float32)
        for index in range(1 + tasks):
            both_halves = totals[0, 1, pl.ds(index, 1), :] + totals[1, 1, pl.ds(index, 1), :]
            square = jnp.sum(both_halves, axis=1, keepdims=True)
            result = jnp.where(lane == index, jnp.sqrt(square / (live_total * cells)), result)
        rms_out[...] = result
        for index in range(NORMS):
            shift_sum = jnp.sum(
                joined(norms, index, pl.ds(0, micro)), axis=0, keepdims=True
            )
            gain_sum = jnp.sum(
                joined(norms, index, pl.ds(micro, micro)), axis=0, keepdims=True
            )
            if index < NARROW:
                gain_out[pl.ds(index, 1), :] = gain_sum
                shift_out[pl.ds(index, 1), :] = shift_sum
            else:
                narrow_gain_out[pl.ds(index - NARROW, 1), :] = gain_sum
                narrow_shift_out[pl.ds(index - NARROW, 1), :] = shift_sum

    @pl.when((pl.program_id(0) == 0) & (section == 0))
    def _():
        place_out(plan["high"], plan["across"], live, True)

    @pl.when((pl.program_id(0) == 0) & (section == 1))
    def _():
        place_out(plan["high"] // 2, plan["across"] // 2, 8, False)

    for terms, target in (
        (first, first_out), (second, second_out), (squeeze, squeeze_out),
        (expand, expand_out), (task, task_out),
    ):
        _, count, width = terms.shape
        per_row = width // 128
        for lane in range(per_row):
            at = pl.ds(lane * 128, 128)
            summed = terms[0, :, at].astype(jnp.float32)
            for place in range(1, mates):
                summed = summed + terms[place, :, at].astype(jnp.float32)
            target[pl.ds(lane, count, stride=per_row), :] = summed


def gathered_shards(
    stream_in, image_count, out_grad, first_conv, second_conv, squeeze, expand, task_conv,
    norm_gain, norm_shift, squeeze_gain, squeeze_shift,
):
    maps, images, high, across, c = stream_in.shape
    micro = image_count.shape[1]
    tasks = maps - 1
    groups = lax.axis_size("dp")
    mates = 4
    lines = groups // mates
    live = images - 2
    n = high * live * across
    wide_n = 256
    plan = {
        "lines": lines, "mates": mates, "tasks": tasks, "channels": c,
        "high": high, "across": across, "live": live, "wide": wide_n, "micro": micro,
    }
    conv_rows = c // groups
    task_rows = tasks * c // groups
    turned_rows = 2 * c + 3 * tasks * c
    bf16, f32 = jnp.bfloat16, jnp.float32
    vmem = pl.BlockSpec(memory_space=pltpu.VMEM)
    whole = pl.BlockSpec(memory_space=pl.ANY)
    shapes = (
        (conv_rows, TAPS * c), (conv_rows, TAPS * c), (task_rows, 2 * c), (task_rows, c),
        (task_rows, TAPS * c),
    )
    hc = c // 2
    small = 64
    out_shape = (
        [
            jax.ShapeDtypeStruct((2, maps, small, hc), bf16),
            jax.ShapeDtypeStruct((2, maps, n, hc), f32),
            jax.ShapeDtypeStruct((2, NORMS, 8, hc), f32),
            jax.ShapeDtypeStruct((2, 2, 8, hc), f32),
            jax.ShapeDtypeStruct((8, 2, lines, n, hc), bf16),
            jax.ShapeDtypeStruct((8, 2, lines, small, hc), bf16),
            jax.ShapeDtypeStruct((lines, turned_rows // lines, wide_n), bf16),
            jax.ShapeDtypeStruct((lines, turned_rows // lines, 128), bf16),
        ]
        + [jax.ShapeDtypeStruct((mates,) + shape, bf16) for shape in shapes]
    )
    row_one, row_two = live * across, 4 * across

    def pair(shape_of, dtype):
        return [pltpu.VMEM(shape_of(n), dtype), pltpu.VMEM(shape_of(small), dtype)]

    unit = c // lines
    scratch = (
        [
            pltpu.VMEM((2, hc, TAPS * c), bf16),
            pltpu.VMEM((2, hc, TAPS * c), bf16),
            pltpu.VMEM((2, tasks, hc, 2 * c), bf16),
            pltpu.VMEM((2, tasks, hc, c), bf16),
            pltpu.VMEM((2, tasks, hc, TAPS * c), bf16),
            pltpu.VMEM((2, 2, NORMS, 1, hc), f32),
            pltpu.VMEM((2, NORMS, 1, hc), f32),
            pltpu.VMEM((2, maps, n, hc), bf16),
            pltpu.VMEM((2, maps, small, hc), bf16),
            pltpu.VMEM((maps, 16, hc), f32),
            pltpu.VMEM((maps, small, hc), bf16),
            pltpu.VMEM((maps, (high + 2) * row_one, 3 * c), bf16),
            pltpu.VMEM((maps, (high // 2 + 2) * row_two, 3 * c), bf16),
        ]
        + pair(lambda rows: (NORMS, rows, hc), f32)
        + pair(lambda rows: (NORMS, rows, hc), f32)
        + pair(lambda rows: (maps, rows, hc), f32)
        + pair(lambda rows: (rows, hc), f32)
        + pair(lambda rows: (rows, hc), bf16)
        + pair(lambda rows: (tasks, 2, rows, hc), bf16)
        + pair(lambda rows: (tasks, rows, hc), bf16)
        + [pltpu.VMEM((NORMS, n, hc), f32), pltpu.VMEM((NORMS, n, hc), f32)]
        + [pltpu.VMEM((NORMS, hc, wide_n), bf16), pltpu.VMEM((NORMS, hc, 128), bf16)]
        + pair(lambda rows: (maps, rows, hc), f32)
        + [
            pltpu.VMEM((maps, 16, hc), bf16),
            pltpu.VMEM((NORMS, 8, hc), f32),
            pltpu.VMEM((NORMS, 8, hc), f32),
            pltpu.VMEM((micro, row_one, hc), f32),
            pltpu.VMEM((micro, row_two, hc), f32),
            pltpu.VMEM((NORMS, micro, hc), f32),
            pltpu.VMEM((NORMS, micro, hc), f32),
            pltpu.VMEM((maps, 1, hc), f32),
            pltpu.VMEM((maps, 1, hc), f32),
            pltpu.VMEM((4, n, hc), f32),
            pltpu.VMEM((n, hc), f32),
            pltpu.VMEM(((high + 2) * row_one, 3 * hc), bf16),
            pltpu.VMEM((3, row_one, hc), f32),
            pltpu.VMEM((4, 8, hc), f32),
            pltpu.VMEM((8, hc), f32),
            pltpu.VMEM((hc // 128, row_one, 128), f32),
            pltpu.VMEM((wide_n, hc), f32),
            pltpu.VMEM((2, 8, hc), f32),
            pltpu.VMEM((6, 2, 4, 2, 8, hc), f32),
            pltpu.VMEM((8, 2, 4, 3, 8, hc), f32),
            pltpu.VMEM((4, 2, 4, 4, 8, hc), f32),
            pltpu.VMEM((lines, wide_n, c), bf16),
            pltpu.VMEM((lines, unit, wide_n), bf16),
            pltpu.VMEM((3, unit, lines * wide_n), bf16),
            pltpu.VMEM((2, unit, TAPS * c), bf16),
            pltpu.VMEM((mates * task_rows, 2 * c), bf16),
        ]
        + [
            pltpu.SemaphoreType.DMA(shape)
            for shape in (
                (2, 6 + tasks), (6 + tasks,), (2,), (1,), (2 * GROUPS_OF_SUMS, 2),
                (2 * GROUPS_OF_SUMS, 2),
                (2, NORMS), (2, NORMS), (2, NORMS), (2, NORMS), (2, NORMS, lines), (2, NORMS, 2),
                (2, NORMS, 2), (2, 5), (2, 8), (4,), (2, 7, mates), (7, mates), (7,),
                (3 + tasks * lines,),
            )
        ]
    )
    results = pl.pallas_call(
        functools.partial(main_kernel, plan),
        out_shape=out_shape,
        in_specs=[pl.BlockSpec(memory_space=pltpu.SMEM)] + [vmem] * 6 + [whole] * 5,
        out_specs=[whole] * 13,
        scratch_shapes=scratch,
        compiler_params=pltpu.CompilerParams(
            collective_id=1, has_side_effects=True, vmem_limit_bytes=62 * 2**20
        ),
        name="blocks",
    )(
        image_count, stream_in, out_grad, norm_gain[0], norm_shift[0], squeeze_gain[0],
        squeeze_shift[0], first_conv[0], second_conv[0], squeeze[0], expand[0], task_conv[0],
    )
    pooled, grads, norms, totals = results[:4]
    terms = results[8:]
    steps = 2

    def flat(shape):
        return jax.ShapeDtypeStruct((shape[0] * shape[1] // 128, 128), f32)

    results = pl.pallas_call(
        functools.partial(result_kernel, plan),
        grid=(steps,),
        out_shape=[flat(shape) for shape in shapes]
        + [
            jax.ShapeDtypeStruct((maps, images, high // 2, across // 2, c), bf16),
            jax.ShapeDtypeStruct((maps, images, high, across, c), f32),
            jax.ShapeDtypeStruct((NARROW, c), f32),
            jax.ShapeDtypeStruct((NARROW, c), f32),
            jax.ShapeDtypeStruct((tasks, c), f32),
            jax.ShapeDtypeStruct((tasks, c), f32),
            jax.ShapeDtypeStruct((1, maps), f32),
        ],
        in_specs=[pl.BlockSpec(memory_space=pltpu.SMEM)]
        + [
            pl.BlockSpec((mates, shape[0] // steps, shape[1]), lambda i: (0, i, 0))
            for shape in shapes
        ]
        + [vmem] * 4,
        out_specs=[
            pl.BlockSpec((shape[0] // steps * shape[1] // 128, 128), lambda i: (i, 0))
            for shape in shapes
        ]
        + [vmem] * 7,
        compiler_params=pltpu.CompilerParams(vmem_limit_bytes=62 * 2**20),
        name="results",
    )(image_count, *terms, pooled, grads, norms, totals)
    first_g, second_g, squeeze_g, expand_g, task_g = (
        grad.reshape(1, -1) for grad in results[:5]
    )
    feature_out, input_out, gain_g, shift_g, narrow_gain_g, narrow_shift_g, rms = results[5:]
    return (
        feature_out[None], input_out[None], first_g, second_g, squeeze_g, expand_g, task_g,
        gain_g[None], shift_g[None], narrow_gain_g[None], narrow_shift_g[None], rms,
    )


def solution(mesh):
    groups = mesh.shape["dp"]
    whole_tiles = groups == 4 * 4
    return jax.shard_map(
        gathered_shards if whole_tiles else shards,
        mesh=mesh,
        in_specs=(
            P(None, "dp", None, None, None),
            P("dp", None),
            P(None, "dp", None, None, None),
            P("section", None, None),
            P("section", None, None),
            P("section", None, None, None),
            P("section", None, None, None),
            P("section", None, None, None),
            P("section", None, None),
            P("section", None, None),
            P("section", None, None),
            P("section", None, None),
        ),
        out_specs=(
            P("section", None, "dp", None, None, None),
            P("section", None, "dp", None, None, None),
            P("section", "dp"),
            P("section", "dp"),
            P("section", "dp"),
            P("section", "dp"),
            P("section", "dp"),
            P("section", None, None),
            P("section", None, None),
            P("section", None, None),
            P("section", None, None),
            P("section", None),
        ),
        check_vma=False,
    )
```

time: 4400 us -> 270 us (0.06)
  blocking collectives: 1960 us -> 0 us
  waiting for transfers between devices: 1440 us -> 0 us
  matrix products: 481 us -> 0 us
  Pallas kernels: 0 us -> 265 us
  other arithmetic: 234 us -> 0 us
  local copies, waits for them, and re-layouts: 211 us -> 3.91 us
    psum x28 -> x0, blocking collectives: 1960 us -> none  [the longest x24 1700 us: forward_moments(): summed, counted = lax.psum((pack_members(members), local_pixels), 'dp')]
    unnamed x2 -> x0, waiting for transfers between devices: 1440 us -> none
    dot_general x102 -> x0, matrix products: 481 us -> none  [the longest x6 116 us: section_backward(): jnp.einsum('tshwo,tshwk->tok', grad_task, attended_columns, preferred_ele...]
    pallas_call x0 -> x2, Pallas kernels: none -> 265 us  [the longest x1 259 us: gathered_shards(): pl.pallas_call(functools.partial(main_kernel, plan), out_shape=out_shape,...]
    mul x66 -> x0, other arithmetic: 75.2 us -> none  [the longest x30 40.7 us: norm_backward(): inverse * scale_by]
    unnamed x1705 -> x3, local copies, waits for them, and re-layouts: 76.5 us -> 3.91 us
    add x5 -> x0, local copies, waits for them, and re-layouts: 53.7 us -> none  [the longest x4 53.7 us: shards(): former + latest]
  transfers between devices with their start and end apart: 11 -> 0, of which waited for: 1 -> 0; matrix products, arithmetic and copies ran while one was open for 4% -> 0% of each run, Pallas kernels for 0% -> 0%
where the time goes in v1:
time: 270 us; the launch traced here: 269 us
  Pallas kernels  265 us (98%)
  local copies, waits for them, and re-layouts  3.91 us (1%)
    pallas_call x1, Pallas kernels, gathered_shards(): pl.pallas_call(functools.partial(main_kernel, plan), out_shape=out_shape,...  259 us
    pallas_call x1, Pallas kernels, gathered_shards(): pl.pallas_call(functools.partial(result_kernel, plan), grid=(steps,), out...  5.99 us

profile of v1, /device:TPU:6, one launch (start us, length us, event | category | flops | bytes accessed | tf_op | source)
XLA Modules:
  0.0 269.3 jit_solution(14323538127137581219)
XLA Ops:
  0.6 1.3 copy_bitcast_fusion
  2.0 258.7 %blocks.1 = (bf16[2,4,64,256]{3,2,1,0:T(8,128)(2,1)}, f32[2,4,192,256]{3,2,1,0:T(8,128)}, f32[2,11,8,256]{3,2,1,0:T(8,128)}, f32[2,2,8,256]{3,2,1,0:T(8,128)}, b...) custom-call(s32[1,4]{1,0:T(1,128)} %refs_0_.3, ...), custom_call_target="tpu_custom_call" | custom-call | tf_op jit(solution)/shard_map/blocks/pallas_call | solution.py:2188
  260.7 6.0 %results.1 = (f32[1152,128]{1,0:T(8,128)}, f32[1152,128]{1,0:T(8,128)}, f32[768,128]{1,0:T(8,128)}, f32[384,128]{1,0:T(8,128)}, f32[3456,128]{1,0:T(8,128)}, /*i...) custom-call(s32[1,4]{1,0:T(1,128)} %refs_0_.3, ...), custom_call_target="tpu_custom_call" | custom-call | tf_op jit(solution)/shard_map/results/pallas_call | solution.py:2209
  266.7 1.3 copy.24
  268.0 1.3 copy.25

commit v2 on v1

v2 whole, which is shorter than its diff:
```python
import functools
import types

import jax
import jax.numpy as jnp
from jax import lax
from jax.experimental import pallas as pl
from jax.experimental.pallas import tpu as pltpu
from jax.sharding import PartitionSpec as P

EPSILON = 1e-05
SUM_ROWS = 40


def stages_of(size):
    stages = []
    stride = 1
    while stride < size:
        radix = next(r for r in (4, 2, 3, 5, 7, size // stride) if (size // stride) % r == 0)
        stages.append((radix, stride))
        stride *= radix
    return stages


def sum_kernel(stages, own_ref, out_ref, *scratch):
    slots, (send_sem, recv_sem) = scratch[: len(stages)], scratch[len(stages) :]
    section = lax.axis_index("section")
    me = lax.axis_index("dp")
    barrier = pltpu.get_barrier_semaphore()
    peers = []
    for radix, stride in stages:
        digit = lax.rem(me // stride, radix)
        group = [
            me + (lax.rem(digit + step, radix) - digit) * stride for step in range(1, radix)
        ]
        peers.append((digit, group))
    total = sum(len(group) for _, group in peers)
    for _, group in peers:
        for peer in group:
            pl.semaphore_signal(
                barrier, inc=1, device_id=(section, peer), device_id_type=pl.DeviceIdType.MESH
            )
    pl.semaphore_wait(barrier, total)
    for index, (radix, stride) in enumerate(stages):
        digit, group = peers[index]
        held = slots[index]
        held[digit] = own_ref[...] if index == 0 else out_ref[...]
        copies = []
        for step, peer in enumerate(group):
            copy = pltpu.make_async_remote_copy(
                src_ref=held.at[digit],
                dst_ref=held.at[digit],
                send_sem=send_sem.at[index, step],
                recv_sem=recv_sem.at[index, step],
                device_id=(section, peer),
                device_id_type=pl.DeviceIdType.MESH,
            )
            copy.start()
            copies.append(copy)
        for copy in copies:
            copy.wait_recv()
        summed = held[0]
        for place in range(1, radix):
            summed = summed + held[place]
        out_ref[...] = summed
        for copy in copies:
            copy.wait_send()


def sum_over_groups(rows):
    stages = stages_of(lax.axis_size("dp"))
    widest = max(radix for radix, _ in stages)
    return pl.pallas_call(
        functools.partial(sum_kernel, stages),
        out_shape=jax.ShapeDtypeStruct(rows.shape, jnp.float32),
        in_specs=[pl.BlockSpec(memory_space=pltpu.VMEM)],
        out_specs=pl.BlockSpec(memory_space=pltpu.VMEM),
        scratch_shapes=[pltpu.VMEM((radix,) + rows.shape, jnp.float32) for radix, _ in stages]
        + [
            pltpu.SemaphoreType.DMA((len(stages), widest)),
            pltpu.SemaphoreType.DMA((len(stages), widest)),
        ],
        compiler_params=pltpu.CompilerParams(collective_id=0, has_side_effects=True),
        name="group_sum",
    )(rows)


def from_behind(shard, axis, by):
    size = lax.axis_size(axis)
    pairs = [(i, i + by) for i in range(size) if 0 <= i + by < size]
    return lax.ppermute(shard, axis, pairs)


def broadcast_rows(vector):
    return vector[..., None, None, None, :]


def affine_rows(normed, scale_by, offset_by):
    return normed * broadcast_rows(scale_by) + broadcast_rows(offset_by)


def silu_slope(active):
    sigmoid_of = jax.nn.sigmoid(active)
    return sigmoid_of * (1.0 + active * (1.0 - sigmoid_of))


def pixel_sums(values, pixel_weight):
    weighted = values * pixel_weight
    return jnp.stack(
        [jnp.sum(weighted, axis=(-4, -3, -2)), jnp.sum(weighted * values, axis=(-4, -3, -2))],
        axis=-2,
    )


def gradient_sums(upstream, normed, pixel_weight):
    weighted = upstream * pixel_weight
    return jnp.stack(
        [jnp.sum(weighted, axis=(-4, -3, -2)), jnp.sum(weighted * normed, axis=(-4, -3, -2))],
        axis=-2,
    )


def summed_members(members):
    rows = [member.reshape(-1, member.shape[-1]) for member in members]
    used = sum(row.shape[0] for row in rows)
    packed = jnp.concatenate(
        rows + [jnp.zeros((SUM_ROWS - used, rows[0].shape[-1]), jnp.float32)], axis=0
    )
    summed = sum_over_groups(packed)
    results = []
    offset = 0
    for member, row in zip(members, rows):
        results.append(summed[offset : offset + row.shape[0]].reshape(member.shape))
        offset += row.shape[0]
    return results


def normalize(values, moments, counted):
    average = moments[..., 0, :] / counted
    spread = moments[..., 1, :] / counted - average * average
    inverse = lax.rsqrt(spread + EPSILON)
    return ((values - broadcast_rows(average)) * broadcast_rows(inverse), inverse)


def norm_backward(upstream, normed, inverse, scale_by, sums, counted, pixel_weight):
    shift_part = broadcast_rows(sums[..., 0, :])
    scale_part = broadcast_rows(sums[..., 1, :])
    return (
        broadcast_rows(inverse * scale_by)
        * (upstream - (shift_part + normed * scale_part) / broadcast_rows(counted))
        * pixel_weight
    )


def window_blocks(values):
    leading = values.shape[:-3]
    height, breadth, channels = values.shape[-3:]
    return values.reshape(leading + (height // 2, 2, breadth // 2, 2, channels))


def soft_pool_blocks(blocks):
    summit = jnp.max(blocks, axis=(-4, -2), keepdims=True)
    return summit + jnp.log(jnp.mean(jnp.exp(blocks - summit), axis=(-4, -2), keepdims=True))


def soft_pool(values):
    pooled = soft_pool_blocks(window_blocks(values))
    return pooled.reshape(
        values.shape[:-3] + (values.shape[-3] // 2, values.shape[-2] // 2, values.shape[-1])
    )


def pool_back(upstream, values):
    blocks = window_blocks(values)
    pooled = soft_pool_blocks(blocks)
    weight_share = jnp.exp(blocks - pooled) * 0.25
    spread = upstream.reshape(pooled.shape) * weight_share
    return spread.reshape(values.shape)


def patch_columns(frames):
    height, breadth = (frames.shape[-3], frames.shape[-2])
    padding = [(0, 0)] * (frames.ndim - 3) + [(1, 1), (1, 1), (0, 0)]
    padded = jnp.pad(frames, padding)
    return jnp.concatenate(
        [
            padded[..., down_shift : down_shift + height, side_shift : side_shift + breadth, :]
            for down_shift in range(3)
            for side_shift in range(3)
        ],
        axis=-1,
    )


def columns_back(grad_columns, channels):
    height, breadth = (grad_columns.shape[-3], grad_columns.shape[-2])
    leading = [(0, 0)] * (grad_columns.ndim - 3)
    summed = None
    for tap_index in range(9):
        down_shift, side_shift = (tap_index // 3, tap_index % 3)
        piece_of = grad_columns[..., tap_index * channels : (tap_index + 1) * channels]
        placed = jnp.pad(
            piece_of, leading + [(down_shift, 2 - down_shift), (side_shift, 2 - side_shift), (0, 0)]
        )
        summed = placed if summed is None else summed + placed
    return summed[..., 1 : height + 1, 1 : breadth + 1, :]


def live_rows(pixel_weight, channels):
    live = jnp.sum(pixel_weight, axis=(-4, -3, -2, -1))
    return jnp.broadcast_to(live[:, None], (live.shape[0], channels))


def section_forward(frames, pixel_weight, weights):
    (
        first_conv,
        second_conv,
        squeeze,
        expand,
        task_conv,
        norm_gain,
        norm_shift,
        squeeze_gain,
        squeeze_shift,
    ) = weights
    channels = frames.shape[-1]
    tasks = squeeze.shape[0]
    input_columns = patch_columns(frames[0])
    first_pre = jnp.einsum(
        "mshwk,ok->mshwo", input_columns, first_conv, preferred_element_type=jnp.float32
    )
    first_moments = summed_members(
        [pixel_sums(first_pre, pixel_weight), live_rows(pixel_weight, channels)]
    )
    counted = first_moments[1] * (frames.shape[-3] * frames.shape[-2])
    first_normed, first_inverse = normalize(first_pre, first_moments[0], counted)
    first_output = jax.nn.silu(affine_rows(first_normed, norm_gain[0], norm_shift[0]))
    rounded_first = (first_output).astype(jnp.bfloat16)
    middle_columns = patch_columns(rounded_first)
    second_pre = jnp.einsum(
        "mshwk,ok->mshwo", middle_columns, second_conv, preferred_element_type=jnp.float32
    )
    earlier = frames[1:]
    narrow = jnp.einsum(
        "mshwc,trc->tmshwr",
        rounded_first,
        squeeze[:, :, :channels],
        preferred_element_type=jnp.float32,
    ) + jnp.einsum(
        "tmshwc,trc->tmshwr", earlier, squeeze[:, :, channels:], preferred_element_type=jnp.float32
    )
    middle_moments = summed_members([pixel_sums(second_pre, pixel_weight), pixel_sums(narrow, pixel_weight)])
    second_normed, second_inverse = normalize(second_pre, middle_moments[0], counted)
    narrow_normed, narrow_inverse = normalize(narrow, middle_moments[1], counted)
    shared_out = jax.nn.silu(affine_rows(second_normed, norm_gain[1], norm_shift[1]))
    rounded_hidden = jax.nn.silu(affine_rows(narrow_normed, squeeze_gain[:, None], squeeze_shift[:, None])).astype(
        jnp.bfloat16
    )
    widened = jnp.einsum(
        "tmshwr,tcr->tmshwc", rounded_hidden, expand, preferred_element_type=jnp.float32
    )
    mask_moments = summed_members([pixel_sums(widened, pixel_weight)])
    widened_normed, widened_inverse = normalize(widened, mask_moments[0], counted)
    task_mask = jax.nn.sigmoid(
        affine_rows(widened_normed, norm_gain[2 : 2 + tasks][:, None], norm_shift[2 : 2 + tasks][:, None])
    )
    rounded_attended = (task_mask * shared_out).astype(jnp.bfloat16)
    attended_columns = patch_columns(rounded_attended)
    task_pre = jnp.einsum(
        "tmshwk,tok->tmshwo", attended_columns, task_conv, preferred_element_type=jnp.float32
    )
    task_moments = summed_members([pixel_sums(task_pre, pixel_weight)])
    task_normed, task_inverse = normalize(task_pre, task_moments[0], counted)
    task_out = jax.nn.silu(
        affine_rows(task_normed, norm_gain[2 + tasks :][:, None], norm_shift[2 + tasks :][:, None])
    )
    pooled = jnp.concatenate([soft_pool(shared_out)[None], soft_pool(task_out)], axis=0)
    kept_state = (
        frames,
        counted,
        first_normed,
        first_inverse,
        rounded_first,
        second_normed,
        second_inverse,
        narrow_normed,
        narrow_inverse,
        rounded_hidden,
        widened_normed,
        widened_inverse,
        rounded_attended,
        task_normed,
        task_inverse,
    )
    return (pooled, kept_state)


def section_backward(upstream, kept_state, pixel_weight, squares, weights):
    (
        first_conv,
        second_conv,
        squeeze,
        expand,
        task_conv,
        norm_gain,
        norm_shift,
        squeeze_gain,
        squeeze_shift,
    ) = weights
    (
        frames,
        counted,
        first_normed,
        first_inverse,
        rounded_first,
        second_normed,
        second_inverse,
        narrow_normed,
        narrow_inverse,
        rounded_hidden,
        widened_normed,
        widened_inverse,
        rounded_attended,
        task_normed,
        task_inverse,
    ) = kept_state
    channels = frames.shape[-1]
    tasks = squeeze.shape[0]
    task_gain = norm_gain[2 + tasks :][:, None]
    mask_gain = norm_gain[2 : 2 + tasks][:, None]
    task_active = affine_rows(task_normed, task_gain, norm_shift[2 + tasks :][:, None])
    task_out = jax.nn.silu(task_active)
    grad_task_act = pool_back(upstream[1:], task_out) * silu_slope(task_active)
    task_sums, square_all = summed_members(
        [gradient_sums(grad_task_act, task_normed, pixel_weight), squares]
    )
    grad_task = norm_backward(
        grad_task_act, task_normed, task_inverse, task_gain, task_sums, counted, pixel_weight
    ).astype(jnp.bfloat16)
    attended_columns = patch_columns(rounded_attended)
    task_conv_grad = jnp.einsum(
        "tmshwo,tmshwk->tok", grad_task, attended_columns, preferred_element_type=jnp.float32
    )
    grad_attended = (
        columns_back(
            jnp.einsum(
                "tmshwo,tok->tmshwk", grad_task, task_conv, preferred_element_type=jnp.float32
            ),
            channels,
        )

    )
    second_active = affine_rows(second_normed, norm_gain[1], norm_shift[1])
    shared_out = jax.nn.silu(second_active)
    task_mask = jax.nn.sigmoid(affine_rows(widened_normed, mask_gain, norm_shift[2 : 2 + tasks][:, None]))
    grad_mask_act = grad_attended * shared_out * task_mask * (1.0 - task_mask)
    mask_sums = summed_members([gradient_sums(grad_mask_act, widened_normed, pixel_weight)])[0]
    grad_widened = norm_backward(
        grad_mask_act, widened_normed, widened_inverse, mask_gain, mask_sums, counted, pixel_weight
    ).astype(jnp.bfloat16)
    expand_grad = jnp.einsum(
        "tmshwc,tmshwr->tcr", grad_widened, rounded_hidden, preferred_element_type=jnp.float32
    )
    narrow_active = affine_rows(narrow_normed, squeeze_gain[:, None], squeeze_shift[:, None])
    grad_narrow_act = jnp.einsum(
        "tmshwc,tcr->tmshwr", grad_widened, expand, preferred_element_type=jnp.float32
    ) * silu_slope(narrow_active)
    grad_shared = pool_back(upstream[0], shared_out) + jnp.sum(grad_attended * task_mask, axis=0)
    grad_second_act = grad_shared * silu_slope(second_active)
    second_sums, narrow_sums = summed_members(
        [
            gradient_sums(grad_second_act, second_normed, pixel_weight),
            gradient_sums(grad_narrow_act, narrow_normed, pixel_weight),
        ]
    )
    grad_second = norm_backward(
        grad_second_act,
        second_normed,
        second_inverse,
        norm_gain[1],
        second_sums,
        counted,
        pixel_weight,
    ).astype(jnp.bfloat16)
    grad_narrow = norm_backward(
        grad_narrow_act,
        narrow_normed,
        narrow_inverse,
        squeeze_gain[:, None],
        narrow_sums,
        counted,
        pixel_weight,
    ).astype(jnp.bfloat16)
    middle_columns = patch_columns(rounded_first)
    second_conv_grad = jnp.einsum(
        "mshwo,mshwk->ok", grad_second, middle_columns, preferred_element_type=jnp.float32
    )
    earlier = frames[1:]
    squeeze_grad = jnp.concatenate(
        [
            jnp.einsum(
                "tmshwr,mshwc->trc", grad_narrow, rounded_first, preferred_element_type=jnp.float32
            ),
            jnp.einsum(
                "tmshwr,tmshwc->trc", grad_narrow, earlier, preferred_element_type=jnp.float32
            ),
        ],
        axis=-1,
    )
    grad_joined = jnp.einsum(
        "tmshwr,trc->tmshwc", grad_narrow, squeeze, preferred_element_type=jnp.float32
    )
    grad_first_out = (
        columns_back(
            jnp.einsum(
                "mshwo,ok->mshwk", grad_second, second_conv, preferred_element_type=jnp.float32
            ),
            channels,
        )
        + jnp.sum(grad_joined[..., :channels], axis=0)
    )
    grad_earlier = grad_joined[..., channels:]
    first_active = affine_rows(first_normed, norm_gain[0], norm_shift[0])
    grad_first_act = grad_first_out * silu_slope(first_active)
    first_sums = summed_members([gradient_sums(grad_first_act, first_normed, pixel_weight)])[0]
    grad_first = norm_backward(
        grad_first_act, first_normed, first_inverse, norm_gain[0], first_sums, counted, pixel_weight
    ).astype(jnp.bfloat16)
    input_columns = patch_columns(frames[0])
    first_conv_grad = jnp.einsum(
        "mshwo,mshwk->ok", grad_first, input_columns, preferred_element_type=jnp.float32
    )
    grad_shared_in = (
        columns_back(
            jnp.einsum("mshwo,ok->mshwk", grad_first, first_conv, preferred_element_type=jnp.float32),
            channels,
        )

    )
    grad_frames = jnp.concatenate([grad_shared_in[None], grad_earlier], axis=0)
    first_norm, second_norm, mask_norm, task_norm, narrow_norm = (
        jnp.sum(sums, axis=-3)
        for sums in (first_sums, second_sums, mask_sums, task_sums, narrow_sums)
    )
    norm_rows = jnp.concatenate(
        [first_norm[None], second_norm[None], mask_norm, task_norm], axis=0
    )
    weight_terms = (first_conv_grad, second_conv_grad, squeeze_grad, expand_grad, task_conv_grad)
    norm_terms = (norm_rows[:, 1], norm_rows[:, 0], narrow_norm[:, 1], narrow_norm[:, 0])
    return (grad_frames, weight_terms, norm_terms, square_all)


def shards(
    stream_in,
    image_count,
    out_grad,
    first_conv,
    second_conv,
    squeeze,
    expand,
    task_conv,
    norm_gain,
    norm_shift,
    squeeze_gain,
    squeeze_shift,
):
    weights = (
        first_conv[0],
        second_conv[0],
        squeeze[0],
        expand[0],
        task_conv[0],
        norm_gain[0],
        norm_shift[0],
        squeeze_gain[0],
        squeeze_shift[0],
    )
    maps_count, images, height, breadth, channels = stream_in.shape
    micro_count = image_count.shape[1]
    slot_count = images // micro_count
    leading_section = lax.axis_index("section") == 0
    live = jnp.arange(slot_count)[None, :] < image_count[0][:, None]
    pixel_weight = live.astype(jnp.float32)[:, :, None, None, None]

    def by_micro(maps):
        return maps.reshape((maps_count, micro_count, slot_count) + maps.shape[2:])

    def whole_pool(pooled):
        masked = pooled * pixel_weight
        squares = jnp.sum(masked * masked, axis=(1, 2, 3, 4, 5))
        return masked.astype(jnp.bfloat16), jnp.broadcast_to(squares[:, None], (maps_count, channels))

    one_pooled, one_state = section_forward(by_micro(stream_in), pixel_weight, weights)
    one_features, one_squares = whole_pool(one_pooled)
    arrived = from_behind(one_features, "section", 1)
    two_pooled, two_state = section_forward(arrived, pixel_weight, weights)
    two_features, two_squares = whole_pool(two_pooled)
    two_upstream = by_micro(out_grad).astype(jnp.float32) * pixel_weight
    two_back = section_backward(two_upstream, two_state, pixel_weight, two_squares, weights)
    sendback = two_back[0].astype(jnp.bfloat16)
    returned = from_behind(sendback, "section", -1)
    one_upstream = returned.astype(jnp.float32) * pixel_weight
    one_back = section_backward(one_upstream, one_state, pixel_weight, one_squares, weights)

    half = ((0, 0),) * 3 + ((0, height // 4), (0, breadth // 4), (0, 0))
    full = ((0, 0),) * 3 + ((0, height // 2), (0, breadth // 2), (0, 0))
    feature_out = jnp.where(leading_section, one_features, jnp.pad(two_features, half))
    feature_out = feature_out.reshape((maps_count, images) + feature_out.shape[3:])
    recorded = lax.optimization_barrier(sendback).astype(jnp.float32)
    input_grad_out = jnp.where(leading_section, one_back[0], jnp.pad(recorded, full))
    input_grad_out = input_grad_out.reshape((maps_count, images) + input_grad_out.shape[3:])
    reduced = tuple(
        lax.psum_scatter(
            jnp.where(leading_section, one, two).reshape(-1).astype(jnp.bfloat16),
            "dp",
            scatter_dimension=0,
            tiled=True,
        ).astype(jnp.float32)
        for one, two in zip(one_back[1], two_back[1])
    )
    norm_sums = tuple(
        jnp.where(leading_section, one, two) for one, two in zip(one_back[2], two_back[2])
    )
    live_images = jnp.sum(one_state[1][:, 0]) / (height * breadth)
    feature_pixels = jnp.where(leading_section, height * breadth // 4, height * breadth // 16)
    root_square = jnp.sqrt(
        jnp.where(leading_section, one_back[3], two_back[3])[:, 0]
        / (live_images * feature_pixels * channels)
    )
    return (
        feature_out[None],
        input_grad_out[None],
        reduced[0][None],
        reduced[1][None],
        reduced[2][None],
        reduced[3][None],
        reduced[4][None],
        norm_sums[0][None],
        norm_sums[1][None],
        norm_sums[2][None],
        norm_sums[3][None],
        root_square[None],
    )


TAPS = 9
MESH = pl.DeviceIdType.MESH
FIRST, SECOND, MASK, TASK, NARROW = 0, 1, 2, 5, 8
NORMS = 11
(F_FIRST, F_SECOND, B_FIRST, F_NARROW, F_MASK, F_TASK, B_NARROW, B_TASK, B_MASK) = range(9)
GROUPS_OF_SUMS = 9
(
    P_FIRST, P_FIRST_DONE, P_NARROW_DONE, P_MASK_DONE, P_ATTENDED, P_TASKED, P_SUMMED,
    P_TASK_DONE, P_BTASK_SUMS, P_BTASK_DONE, P_BMASK_START, P_BMASK_SUMS, P_BMASK_DONE,
    P_BNARROW_DONE, P_BFIRST_START, P_BFIRST_SUMS, P_BFIRST_DONE,
) = range(17)


def sigmoid(active):
    return 0.5 * jnp.tanh(0.5 * active) + 0.5


def silu_parts(active):
    sigmoid_of = sigmoid(active)
    return active * sigmoid_of, sigmoid_of * (1.0 + active * (1.0 - sigmoid_of))


def dot_nt(left, right):
    return lax.dot_general(
        left, right, (((1,), (1,)), ((), ())), preferred_element_type=jnp.float32
    )


def dot_nn(left, right):
    return lax.dot_general(
        left, right, (((1,), (0,)), ((), ())), preferred_element_type=jnp.float32
    )


def loop(count, body, start=0):
    lax.fori_loop(start, count, lambda i, _: (body(i), 0)[1], 0)


def main_kernel(plan, *refs):
    (
        count_ref, stream, cotangent, gain_in, shift_in, narrow_gain, narrow_shift,
        w1, w2, sq, ex, tc,
        o_ref, ig_ref, norm_ref, total_ref, a_one, a_two, d_one, d_two, pair_one, pair_two,
        q_one, q_two, dq_one, dq_two, beside, r_first, r_second, r_squeeze, r_expand, r_task,
        w1s, w2s, sqs, exs, tcs, gain, shift, x_one, x_two, og_ref, sg_in, sg_out,
        masks, pad, xh, aux, share, p_act, ub, ab, nb, dr, gp, rows, inv, tot, counts, osq,
        wide, tbuf, turned, joint, slots_one, slots_three, slots_four,
        held, dbuf, cols, out, stage_flat,
        w_load, sync_send, sync_recv, h_send, h_recv, a_send, a_recv, v_send, v_recv, q_recv, s_send, s_recv, u_send, u_recv,
        d_send, d_recv, dq_send, dq_recv, t_send, t_own, r_recv, load_sem,
    ) = refs
    lines, mates, tasks, c = plan["lines"], plan["mates"], plan["tasks"], plan["channels"]
    high, across, live = plan["high"], plan["across"], plan["live"]
    hc = c // 2
    active_of = dr.at[0]
    micro = masks.shape[0]
    section = lax.axis_index("section")
    other = 1 - section
    me = lax.axis_index("dp")
    z, j = me // mates, lax.rem(me, mates)
    unit = c // lines
    pieces = unit // mates
    task_rows = tasks * c // lines
    kinds = ((0, unit), (unit, unit), (0, task_rows), None, (2 * unit, task_rows))

    def plane_tasks(line):
        return (task_rows * line) // c, (task_rows * (line + 1) - 1) // c

    def plane_needs(line, task):
        first, last = plane_tasks(line)
        return (first <= task) & (task <= last)

    def device_needs(device, task):
        own = task_rows // mates
        return ((own * device) // c <= task) & (task <= (own * device + own - 1) // c)

    def mate(step):
        return z * mates + lax.rem(j + step, mates)

    def liner(step):
        return lax.rem(z + step, lines) * mates + j

    def remote(source, target, send, recv, to, device):
        return pltpu.make_async_remote_copy(
            src_ref=source, dst_ref=target, send_sem=send, recv_sem=recv,
            device_id=(to, device), device_id_type=MESH,
        )

    def got(some, recv):
        remote(some, some, sync_send.at[0, 0], recv, section, me).wait_recv()

    def sent(some, send):
        remote(some, some, send, sync_recv.at[0, 0], section, me).wait_send()

    def push(source, target, send, recv, to, device, own=None):
        same = (section == to) & (me == device)

        @pl.when(same)
        def _():
            pltpu.make_async_copy(source, target, recv if own is None else own).start()

        @pl.when(jnp.logical_not(same))
        def _():
            remote(source, target, send, recv, to, device).start()

    def pushed(some, send, to, device, own=None):
        same = (section == to) & (me == device)

        @pl.when(jnp.logical_not(same))
        def _():
            sent(some, send)

        if own is not None:

            @pl.when(same)
            def _():
                pltpu.make_async_copy(some, some, own).wait()

    def across_cores(source, target, send, recv):
        remote(source, target, send, recv, other, me).start()

    def sums_at(group):
        if group < 3:
            ref, at, count = slots_one, group, 2 if group == F_FIRST else 1
        elif group < 7:
            ref, at, count = slots_three, group - 3, 3
        else:
            ref, at, count = slots_four, group - 7, 4
        return ref.at[at], count, group

    def sums_place(group, stage, digits):
        ref, count, _ = sums_at(group)
        return ref.at[stage, digits, pl.ds(0, count)]

    def sums_send(group, stage, digit, devices):
        at = sums_at(group)[2]
        here = sums_place(group, stage, digit)
        for device in devices:
            remote(
                here, here, sync_send.at[at, stage], sync_recv.at[at, stage], section, device
            ).start()

    def sums_got(group, stage, digits):
        ref, count, at = sums_at(group)
        got(sums_place(group, stage, pl.ds(0, digits - 1)), sync_recv.at[at, stage])
        summed = ref[stage, 0, pl.ds(0, count)]
        for digit in range(1, digits):
            summed = summed + ref[stage, digit, pl.ds(0, count)]
        return summed

    def sums_start(group):
        sums_send(group, 0, j, [mate(step) for step in range(1, mates)])

    def sums_mid(group):
        ref, count, _ = sums_at(group)
        ref[1, z, pl.ds(0, count)] = sums_got(group, 0, mates)
        sums_send(group, 1, z, [liner(step) for step in range(1, lines)])

    def sums_end(group):
        count = sums_at(group)[1]
        tot[pl.ds(0, count)] = sums_got(group, 1, lines)

    def sums_sent(group):
        at = sums_at(group)[2]
        for stage, digits in enumerate((mates, lines)):
            sent(
                sums_place(group, stage, pl.ds(0, digits - 1)), sync_send.at[at, stage]
            )

    W_FIRST, W_SQUEEZE, W_SECOND, W_EXPAND, W_TASK = range(5)

    def weight_copy(index):
        if index >= W_TASK:
            source, target = tc.at[index - W_TASK], tcs.at[index - W_TASK]
        else:
            source, target = ((w1, w1s), (sq, sqs), (w2, w2s), (ex, exs))[index]
        return pltpu.make_async_copy(source, target, w_load.at[index])

    def make_block(b):
        leading = b == 0
        rows_high, rows_across, images = (
            (high, across, live) if leading else (high // 2, across // 2, 8)
        )
        per_row = images * rows_across
        n = rows_high * per_row
        wide_n = plan["wide"] if leading else 128
        pixels = float(rows_high * rows_across)
        half = per_row // 2
        source = x_one if leading else x_two
        a_ref, d_ref, pair_ref, q_ref, dq_ref = (
            (a_one, d_one, pair_one, q_one, dq_one) if leading
            else (a_two, d_two, pair_two, q_two, dq_two)
        )
        position = lax.rem(
            lax.broadcasted_iota(jnp.int32, (per_row, c), 0), jnp.int32(rows_across)
        )
        even = lax.rem(position, jnp.int32(2)) == 0
        span = pl.ds(0, n)
        used = pl.ds(0, per_row)

        def each(body):
            for h in range(rows_high):
                body(h)

        def part(h):
            return pl.ds(h * per_row, per_row)

        def shifted(values):
            left = jnp.where(position >= 1, pltpu.roll(values, 1, 0), 0.0)
            right = jnp.where(position <= rows_across - 2, pltpu.roll(values, per_row - 1, 0), 0.0)
            return [v.astype(jnp.bfloat16) for v in (left, values, right)]

        def put_pad(h, values, backward=False):
            sides = shifted(values)
            for side, v in enumerate(reversed(sides) if backward else sides):
                pad[pl.ds((h + 1) * per_row, per_row), pl.ds(side * c, c)] = v

        def conv_to(weight, store_at):
            for out in range(2):
                total_of = None
                for dy in range(3):
                    one = dot_nt(
                        pad[pl.ds(dy * per_row, n), :],
                        weight[pl.ds(out * hc, hc), pl.ds(dy * 3 * c, 3 * c)],
                    )
                    total_of = one if total_of is None else total_of + one
                store_at[:, pl.ds(out * hc, hc)] = total_of

        def conv_back_to(weight, store_at):
            for out in range(2):
                total_of = None
                for dy in range(3):
                    for side in range(3):
                        one = dot_nn(
                            pad[pl.ds((2 - dy) * per_row, n), pl.ds(side * c, c)],
                            weight[:, pl.ds((dy * 3 + side) * c + out * hc, hc)],
                        )
                        total_of = one if total_of is None else total_of + one
                store_at[:, pl.ds(out * hc, hc)] = total_of

        def write_stats(group, member, first, second):
            ref = sums_at(group)[0]
            for k in range(micro):
                weight = masks[k, used, :]
                ref[0, j, member, pl.ds(k, 1), :] = jnp.sum(first * weight, 0, keepdims=True)
                ref[0, j, member, pl.ds(micro + k, 1), :] = jnp.sum(
                    second * weight, 0, keepdims=True
                )

        def moments(group, member, values_ref):
            first = second = None
            for h in range(rows_high):
                v = values_ref[pl.ds(h * per_row, per_row), :]
                first = v if h == 0 else first + v
                second = v * v if h == 0 else second + v * v
            write_stats(group, member, first, second)

        def start(group):
            sums_start(group)

        def mid(group):
            sums_mid(group)

        def end(group):
            sums_end(group)

        def row(ref, k):
            return ref[pl.ds(k, 1), :]

        def total(member, k):
            return tot[member, pl.ds(k, 1), :]

        def norm_rows(index, member):
            mean_rows = inv_rows = None
            for k in range(micro):
                n_k = row(counts, k) * pixels
                mean = total(member, k) / n_k
                spread_of = total(member, micro + k) / n_k - mean * mean
                inverse = lax.rsqrt(spread_of + EPSILON)
                inv[index, pl.ds(k, 1), :] = inverse
                weight = masks[k, used, :]
                mean_rows = weight * mean if k == 0 else mean_rows + weight * mean
                inv_rows = weight * inverse if k == 0 else inv_rows + weight * inverse
            rows[0, used, :] = mean_rows
            rows[1, used, :] = inv_rows

        def normalized(index, h, raw):
            normed = (raw - rows[0, used, :]) * rows[1, used, :]
            xh[index, part(h), :] = normed
            return normed * gain[index] + shift[index]

        def back_rows(index, member):
            norm_ref[index] = tot[member]
            scale_rows = shift_rows = slope_rows = None
            for k in range(micro):
                n_k = row(counts, k) * pixels
                weight = masks[k, used, :]
                scale = inv[index, pl.ds(k, 1), :] * gain[index]
                by_shift = total(member, k) / n_k
                by_gain = total(member, micro + k) / n_k
                scale_rows = weight * scale if k == 0 else scale_rows + weight * scale
                shift_rows = weight * by_shift if k == 0 else shift_rows + weight * by_shift
                slope_rows = weight * by_gain if k == 0 else slope_rows + weight * by_gain
            rows[0, used, :] = scale_rows
            rows[1, used, :] = shift_rows
            rows[2, used, :] = slope_rows

        def partner(v):
            return jnp.where(even, pltpu.roll(v, per_row - 1, 0), pltpu.roll(v, 1, 0))

        def soft_pool(index, read):
            squares = None
            for pair in range(rows_high // 2):
                upper, lower = read(2 * pair), read(2 * pair + 1)
                top = jnp.maximum(upper, lower)
                top = jnp.maximum(top, partner(top))
                upper, lower = jnp.exp(upper - top), jnp.exp(lower - top)
                summed = upper + lower
                summed = summed + partner(summed)
                share[index, pl.ds(2 * pair * per_row, per_row), :] = upper / summed
                share[index, pl.ds((2 * pair + 1) * per_row, per_row), :] = lower / summed
                pooled = top + jnp.log(summed * 0.25)
                for lane in range(c // 128):
                    wide[lane, used, :] = pooled[:, lane * 128 : (lane + 1) * 128]
                pooled = jnp.concatenate(
                    [wide[lane, pl.ds(0, half, stride=2), :] for lane in range(c // 128)], axis=1
                )
                if leading:
                    kept = pooled
                    pooled = jnp.concatenate(
                        [pooled, jnp.zeros((32 - half, c), jnp.float32)], axis=0
                    )
                    o_ref[index, pl.ds(32 * pair, 32), :] = pooled.astype(jnp.bfloat16)
                else:
                    alive = lax.broadcasted_iota(jnp.int32, (half, c), 0) < live * (
                        rows_across // 2
                    )
                    kept = jnp.where(alive, pooled, 0.0)
                    o_ref[index, pl.ds(half * pair, half), :] = kept.astype(jnp.bfloat16)
                square = jnp.sum(kept * kept, 0, keepdims=True)
                squares = square if squares is None else squares + square
            osq[index] = squares
            if leading:
                across_cores(
                    o_ref.at[index], x_two.at[index], h_send.at[index], h_recv.at[index]
                )

        def widened(index, pair):
            if leading:
                upstream = sg_in[index, pl.ds(pl.multiple_of(32 * pair, 32), 32), :]
                upstream = upstream.astype(jnp.float32)[:half]
            else:
                upstream = og_ref[index]
            for lane in range(c // 128):
                piece = upstream[:, lane * 128 : (lane + 1) * 128]
                wide[lane, pl.ds(0, half, stride=2), :] = piece
                wide[lane, pl.ds(1, half, stride=2), :] = piece
            return jnp.concatenate(
                [wide[lane, used, :] for lane in range(c // 128)], axis=1
            )

        pair_at = 2 * (z // 2)
        far_at = lines - 2 - pair_at
        inner = (z == 1) | (z == 2)

        def send_shared(which):
            from_ref = shared_source(which)
            neighbour = 2 * pair_at + 1 - z
            for at, plane in enumerate((z, neighbour)):
                push(
                    from_ref, a_ref.at[which, z], a_send.at[b, which, at],
                    a_recv.at[b, which, 0], 0, plane * mates + j,
                )

        def shared_source(which):
            if leading:
                return source.at[0] if which == 0 else ub.at[span]
            return o_ref.at[0] if which == 0 else beside.at[0]

        def pair_lines(which, first):
            return a_ref.at[which, pl.ds(first, 2)]

        def relay_pair(which):
            got(pair_lines(which, 0), a_recv.at[b, which, 0])

            @pl.when(inner)
            def _():
                here = pair_lines(which, pair_at)
                remote(
                    here, here, a_send.at[b, which, 2], a_recv.at[b, which, 1], 0,
                    (lines - 1 - z) * mates + j,
                ).start()

        def relay_far(which):
            got(pair_lines(which, 0), a_recv.at[b, which, 1])

            @pl.when(inner)
            def _():
                here = pair_lines(which, far_at)
                remote(
                    here, here, a_send.at[b, which, 3], a_recv.at[b, which, 1], 0,
                    (2 * pair_at + 1 - z) * mates + j,
                ).start()

        def task_planes(task):
            first = (c * task) // task_rows
            return first, first + 1

        def task_slot(kind, task, plane):
            return 2 + 2 * kind + task - plane_tasks(plane)[0]

        def task_source(kind, task):
            if leading:
                return (
                    source.at[1 + task] if kind == 0
                    else ab.at[task, span] if kind == 1 else nb.at[task, span]
                )
            return o_ref.at[1 + task] if kind == 0 else beside.at[tasks * kind - 2 + task]

        def send_task(kind, task):
            first, last = task_planes(task)
            near = jnp.clip(z, first, last)
            passed_on = (z < first) | (z > last)
            tensor = 2 + tasks * kind + task
            push(
                task_source(kind, task), a_ref.at[task_slot(kind, task, near), z],
                a_send.at[b, tensor, 0],
                a_recv.at[b, tensor, jnp.where(passed_on, jnp.int32(0), jnp.int32(1))],
                0, near * mates + j,
            )

            @pl.when(jnp.logical_not(passed_on))
            def _():
                opposite = first + last - z
                push(
                    task_source(kind, task), a_ref.at[task_slot(kind, task, opposite), z],
                    a_send.at[b, tensor, 1], a_recv.at[b, tensor, 1], 0, opposite * mates + j,
                )

        def task_passes(task):
            first, last = task_planes(task)
            passes = []
            if first > 0:
                passes.append((first, 0, first, last))
            if last < lines - 1:
                passes.append((last, last + 1, lines - 1 - last, first))
            return passes

        def relay_task(kind, task):
            tensor = 2 + tasks * kind + task
            for plane, first, count, to_plane in task_passes(task):

                @pl.when(z == plane)
                def _():
                    some = pl.ds(first, count)
                    here = a_ref.at[task_slot(kind, task, plane), some]
                    got(here, a_recv.at[b, tensor, 0])
                    remote(
                        here, a_ref.at[task_slot(kind, task, to_plane), some],
                        a_send.at[b, tensor, 2], a_recv.at[b, tensor, 1], 0,
                        to_plane * mates + j,
                    ).start()

        def core_of(kind):
            return 0 if leading and kind < 2 else 1

        def deliver(at, slot, task=None):
            for step in range(mates):

                def send():
                    push(
                        a_ref.at[at], q_ref.at[slot, j], v_send.at[b, at, step],
                        q_recv.at[b, slot], core_of(at), mate(step),
                    )

                if task is None:
                    send()
                else:
                    pl.when(device_needs(mate(step), task))(send)

        def delivered(at, task=None):
            for step in range(mates):

                def wait():
                    pushed(a_ref.at[0], v_send.at[b, at, step], core_of(at), mate(step))

                if task is None:
                    wait()
                else:
                    pl.when(device_needs(mate(step), task))(wait)

        def task_done(kind, task):
            tensor = 2 + tasks * kind + task
            first, last = task_planes(task)
            for plane, count in ((first, lines - first), (last, last + 1)):

                @pl.when(z == plane)
                def _():
                    got(a_ref.at[0, pl.ds(0, count)], a_recv.at[b, tensor, 1])
                    at = task_slot(kind, task, plane)
                    if kind == 2:
                        deliver(at, at - 4, task)
                    else:
                        across_cores(
                            a_ref.at[at], a_ref.at[at], v_send.at[b, at, 0], v_recv.at[b, at]
                        )

        def task_got(kind, task):
            for plane in task_planes(task):
                at = task_slot(kind, task, plane)
                if kind == 2:

                    @pl.when((z == plane) & device_needs(me, task))
                    def _():
                        got(q_ref.at[0], q_recv.at[b, at - 4])

                else:

                    @pl.when(z == plane)
                    def _():
                        got(a_ref.at[0], v_recv.at[b, at])

        def shared_got(which):
            got(q_ref.at[0], q_recv.at[b, which])

        def relays(kind):
            for task in range(tasks):
                relay_task(kind, task)

        def done(kind):
            for task in range(tasks):
                task_done(kind, task)

        def exchange_activations():
            def here(index):
                if not leading:
                    got(beside.at[0], s_recv.at[index])

            def send_tasks(kind):
                for task in range(tasks):
                    if kind:
                        here(tasks * kind - 2 + task)
                    send_task(kind, task)

            send_shared(0)
            send_tasks(0)
            here(0)
            send_shared(1)
            relay_pair(0)
            relays(0)
            relay_pair(1)
            send_tasks(1)
            relay_far(0)
            deliver(0, 0)
            done(0)
            relays(1)
            relay_far(1)
            deliver(1, 1)
            if leading:
                across_cores(a_ref.at[1], q_ref.at[1, j], u_send.at[0], u_recv.at[0])
            send_tasks(2)
            done(1)
            relays(2)
            done(2)

        def exchange_sent():
            one_piece = a_ref.at[0, 0]
            for which in range(2):
                for at, plane in enumerate((z, 2 * pair_at + 1 - z)):
                    pushed(one_piece, a_send.at[b, which, at], 0, plane * mates + j)

                @pl.when(inner)
                def _():
                    for at in (2, 3):
                        sent(pair_lines(which, 0), a_send.at[b, which, at])

                delivered(which)
            if leading:
                sent(a_ref.at[0], u_send.at[0])
            for kind in range(3):
                for task in range(tasks):
                    first, last = task_planes(task)
                    tensor = 2 + tasks * kind + task
                    near = jnp.clip(z, first, last)
                    pushed(one_piece, a_send.at[b, tensor, 0], 0, near * mates + j)

                    @pl.when((z == first) | (z == last))
                    def _():
                        pushed(
                            one_piece, a_send.at[b, tensor, 1], 0, (first + last - z) * mates + j
                        )

                    for plane, _, count, _ in task_passes(task):

                        @pl.when(z == plane)
                        def _():
                            sent(a_ref.at[0, pl.ds(0, count)], a_send.at[b, tensor, 2])

                    for plane in (first, last):

                        @pl.when(z == plane)
                        def _():
                            at = task_slot(kind, task, plane)
                            if kind == 2:
                                delivered(at, task)
                            else:
                                sent(a_ref.at[0], v_send.at[b, at, 0])

        def spread_place(kind, task, k):
            offset, _ = kinds[kind]
            if kind < 2:
                return kind, k, offset
            number = lines * task + k
            at = pl.multiple_of(offset + lax.rem(number, tasks) * unit, unit)
            return (2 if kind == 4 else 0) + task, number // tasks, at

        def spread_refs(kind):
            return (joint, pair_ref) if kind == 2 else (turned, d_ref)

        def spread_lanes(kind):
            return pl.ds(0, 2 * n if kind == 2 else wide_n)

        def spread(kind, task=0):
            from_ref, target = spread_refs(kind)
            for k in range(lines):
                index, plane, offset = spread_place(kind, task, k)
                push(
                    from_ref.at[index, pl.ds(k * unit, unit), spread_lanes(kind)],
                    target.at[z, pl.ds(offset, unit)],
                    d_send.at[kind, task, k], d_recv.at[b, kind], core_of(kind), plane * mates + j,
                )

        def spread_sent(kind, task=0):
            from_ref, _ = spread_refs(kind)
            for k in range(lines):
                _, plane, _ = spread_place(kind, task, k)
                pushed(
                    from_ref.at[0, pl.ds(k * unit, unit), spread_lanes(kind)],
                    d_send.at[kind, task, k], core_of(kind), plane * mates + j,
                )

        def spread_got(kind):
            offset, count = kinds[kind]
            got(spread_refs(kind)[1].at[:, pl.ds(offset, count)], d_recv.at[b, kind])

        def rounded(index, member, slot, target, before=None):
            back_rows(index, member)
            first = 0 if before is None else n

            def body(h):
                value = rows[0, used, :] * (
                    dr[slot, part(h), :] - rows[1, used, :] - xh[index, part(h), :] * rows[2, used, :]
                )
                if target is None:
                    xh[index, part(h), :] = value
                else:
                    tbuf[pl.ds(first + h * per_row, per_row), :] = value
                put_pad(h, value, True)

            each(body)
            if target is None:
                return
            if before is None:
                tbuf[pl.ds(n, wide_n - n), :] = jnp.zeros((wide_n - n, c), jnp.float32)
                count = wide_n
            else:
                tbuf[span, :] = before[...]
                count = 2 * n
            target[:, pl.ds(0, count)] = jnp.transpose(tbuf[pl.ds(0, count), :]).astype(jnp.bfloat16)

        def middle():
            return pad[pl.ds(per_row, n), pl.ds(c, c)]

        def beside_core(from_ref, index):
            if not leading:
                across_cores(from_ref, beside.at[index], s_send.at[index], s_recv.at[index])

        def forward_start():
            if not leading:
                got(x_two.at[0], h_recv.at[0])
            each(lambda h: put_pad(h, source[0, part(h), :].astype(jnp.float32)))
            weight_copy(W_FIRST).wait()
            conv_to(w1s, xh.at[FIRST, span])
            moments(F_FIRST, 0, xh.at[FIRST])
            start(F_FIRST)

        def forward():
            for index in range(W_SECOND, W_TASK + tasks):
                weight_copy(index).start()
            if not leading:
                for index in range(1, 1 + tasks):
                    got(x_two.at[0], h_recv.at[index])
            weight_copy(W_SQUEEZE).wait()

            def outer_narrow(task):
                xh[NARROW + task, span] = dot_nt(source[1 + task], sqs[task, :, pl.ds(c, c)])

            outer_narrow(0)
            mid(F_FIRST)
            loop(tasks, outer_narrow, 1)
            end(F_FIRST)
            counts[...] = tot[1]
            total_ref[0] = tot[1]
            norm_rows(FIRST, 0)

            def first_act(h):
                active, slope = silu_parts(normalized(FIRST, h, xh[FIRST, part(h), :]))
                aux[FIRST, part(h), :] = slope
                ub[part(h), :] = active.astype(jnp.bfloat16)
                put_pad(h, active)

            each(first_act)
            beside_core(ub.at[span], 0)

            def narrow(task):
                xh[NARROW + task, span] += dot_nt(middle(), sqs[task, :, pl.ds(0, c)])
                moments(F_NARROW, task, xh.at[NARROW + task])

            loop(tasks, narrow)
            start(F_NARROW)
            weight_copy(W_SECOND).wait()
            conv_to(w2s, xh.at[SECOND, span])
            mid(F_NARROW)
            moments(F_SECOND, 0, xh.at[SECOND])
            start(F_SECOND)
            weight_copy(W_EXPAND).wait()
            end(F_NARROW)

            def mask_of(task):
                norm_rows(NARROW + task, task)

                def act(h):
                    active, slope = silu_parts(
                        normalized(NARROW + task, h, xh[NARROW + task, part(h), :])
                    )
                    aux[NARROW + task, part(h), :] = slope
                    ab[task, part(h), :] = active.astype(jnp.bfloat16)

                each(act)
                beside_core(ab.at[task, span], 1 + task)
                xh[MASK + task, span] = dot_nt(ab[task, span], exs[task])
                moments(F_MASK, task, xh.at[MASK + task])

            mask_of(0)
            mid(F_SECOND)
            loop(tasks, mask_of, 1)
            start(F_MASK)
            end(F_SECOND)
            norm_rows(SECOND, 0)

            def second_act(h):
                active, slope = silu_parts(normalized(SECOND, h, xh[SECOND, part(h), :]))
                aux[SECOND, part(h), :] = slope
                p_act[part(h), :] = active

            each(second_act)
            mid(F_MASK)
            soft_pool(0, lambda h: p_act[part(h), :])
            end(F_MASK)

            def task_conv(task):
                norm_rows(MASK + task, task)

                def act(h):
                    active = normalized(MASK + task, h, xh[MASK + task, part(h), :])
                    sigmoid_of = sigmoid(active)
                    aux[MASK + task, part(h), :] = sigmoid_of
                    attended = sigmoid_of * p_act[part(h), :]
                    nb[task, part(h), :] = attended.astype(jnp.bfloat16)
                    put_pad(h, attended)

                each(act)
                beside_core(nb.at[task, span], 1 + tasks + task)
                pltpu.make_async_copy(tc.at[task], tcs.at[task], w_load.at[W_TASK + task]).wait()
                conv_to(tcs.at[task], xh.at[TASK + task, span])
                moments(F_TASK, task, xh.at[TASK + task])

            loop(tasks, task_conv)
            start(F_TASK)
            mid(F_TASK)
            end(F_TASK)

            def task_pool(task):
                norm_rows(TASK + task, task)

                def act(h):
                    active, slope = silu_parts(
                        normalized(TASK + task, h, xh[TASK + task, part(h), :])
                    )
                    aux[TASK + task, part(h), :] = slope
                    active_of[part(h), :] = active

                each(act)
                soft_pool(1 + task, lambda h: active_of[part(h), :])

            loop(tasks, task_pool)
            squares = sums_at(B_TASK)[0]
            squares[0, j, tasks] = jnp.zeros((8, c), jnp.float32)
            for index in range(1 + tasks):
                squares[0, j, tasks, pl.ds(index, 1), :] = osq[index]

        def handed(index):
            if leading:
                got(sg_in.at[0], h_recv.at[1 + tasks + index])

        def backward():
            def task_start(task):
                handed(1 + task)
                first = second = None
                for pair in range(rows_high // 2):
                    upstream = widened(1 + task, pair)
                    for h in (2 * pair, 2 * pair + 1):
                        at = part(h)
                        up = upstream * share[1 + task, at, :] * aux[TASK + task, at, :]
                        dr[task, at, :] = up
                        by = up * xh[TASK + task, at, :]
                        first = up if first is None else first + up
                        second = by if second is None else second + by
                write_stats(B_TASK, task, first, second)

            loop(tasks, task_start)
            start(B_TASK)
            mid(B_TASK)
            end(B_TASK)
            total_ref[1] = tot[tasks]

            def task_back(task):
                rounded(TASK + task, task, task, None)
                conv_back_to(tcs.at[task], dr.at[task, span])
                first = second = None
                for h in range(rows_high):
                    at = part(h)
                    m, p = aux[MASK + task, at, :], p_act[at, :]
                    through = dr[task, at, :] * m

                    @pl.when(task == 0)
                    def _():
                        gp[at, :] = through

                    @pl.when(task > 0)
                    def _():
                        gp[at, :] += through

                    up = through * p * (1.0 - m)
                    dr[task, at, :] = up
                    by = up * xh[MASK + task, at, :]
                    first = up if first is None else first + up
                    second = by if second is None else second + by
                write_stats(B_MASK, task, first, second)

            loop(tasks, task_back)
            handed(0)
            first = second = None
            for pair in range(rows_high // 2):
                upstream = widened(0, pair)
                for h in (2 * pair, 2 * pair + 1):
                    at = part(h)
                    up = (gp[at, :] + upstream * share[0, at, :]) * aux[SECOND, at, :]
                    dr[3, at, :] = up
                    by = up * xh[SECOND, at, :]
                    first = up if first is None else first + up
                    second = by if second is None else second + by
            write_stats(B_MASK, tasks, first, second)
            start(B_MASK)
            mid(B_MASK)
            end(B_MASK)

            def mask_back(task):
                rounded(MASK + task, task, task, joint.at[task], xh.at[TASK + task, span])
                spread(2, task)
                dr[task, span] = dot_nn(middle(), exs[task])
                first = second = None
                for h in range(rows_high):
                    at = part(h)
                    up = dr[task, at, :] * aux[NARROW + task, at, :]
                    dr[task, at, :] = up
                    by = up * xh[NARROW + task, at, :]
                    first = up if first is None else first + up
                    second = by if second is None else second + by
                write_stats(B_NARROW, task, first, second)

            loop(tasks, mask_back)
            start(B_NARROW)
            rounded(SECOND, tasks, 3, turned.at[1])
            spread(1)
            mid(B_NARROW)
            conv_back_to(w2s, gp.at[span])
            end(B_NARROW)

            def narrow_back(task):
                rounded(NARROW + task, task, task, turned.at[2 + task])
                spread(4, task)
                gp[span, :] += dot_nn(middle(), sqs[task, :, pl.ds(0, c)])
                grad = dot_nn(middle(), sqs[task, :, pl.ds(c, c)])
                outer_grad(1 + task, grad)

            def outer_grad(index, grad):
                if leading:
                    ig_ref[index, span, :] = grad
                else:
                    low = grad.astype(jnp.bfloat16)
                    sg_out[index] = low
                    ig_ref[index, span, :] = low.astype(jnp.float32)
                    at = 1 + tasks + index
                    across_cores(
                        sg_out.at[index], sg_in.at[index], h_send.at[at], h_recv.at[at]
                    )

            loop(tasks, narrow_back)
            first = second = None
            for h in range(rows_high):
                at = part(h)
                up = gp[at, :] * aux[FIRST, at, :]
                dr[3, at, :] = up
                by = up * xh[FIRST, at, :]
                first = up if first is None else first + up
                second = by if second is None else second + by
            write_stats(B_FIRST, 0, first, second)
            start(B_FIRST)
            mid(B_FIRST)
            end(B_FIRST)
            rounded(FIRST, 0, 3, turned.at[0])
            if leading:
                spread(0)
            conv_back_to(w1s, dr.at[0, span])
            outer_grad(0, dr[0, span, :])
            if not leading:
                spread(0)

        def settle():
            if not leading:
                loop(1 + 2 * tasks, lambda i: sent(beside.at[0], s_send.at[i]))
            for kind in range(2):
                spread_sent(kind)
            for kind in (2, 4):
                for task in range(tasks):
                    spread_sent(kind, task)
            for group in range(GROUPS_OF_SUMS):
                sums_sent(group)
            for index in range(1 + tasks):
                if leading:
                    sent(o_ref.at[0], h_send.at[index])
                else:
                    sent(sg_out.at[0], h_send.at[1 + tasks + index])

        deep = lines * wide_n

        def fetch(from_ref, target, index):
            copy = pltpu.make_async_copy(from_ref, target, load_sem.at[index])
            copy.start()
            return copy

        def rows_held(buffer):
            return held[buffer, :, pl.ds(0, wide_n), :].reshape(deep, c)

        def slot_of(piece):
            return (task_rows * z + piece * unit) // c - plane_tasks(z)[0]

        def clear_tail():
            for buffer in range(2):
                held[buffer, :, pl.ds(n, wide_n - n), :] = jnp.zeros(
                    (lines, wide_n - n, c), jnp.bfloat16
                )

        second_at = n % 128
        own_rows = task_rows // mates

        def dealt(kind):
            return (pieces * kind, pieces) if kind < 2 else (2 * pieces, own_rows)

        def deal(kind):
            spread_got(kind)
            offset, _ = kinds[kind]
            at, count = dealt(kind)
            for step in range(mates):
                first = pl.multiple_of(offset + lax.rem(j + step, mates) * count, pieces)
                push(
                    spread_refs(kind)[1].at[:, pl.ds(first, count), pl.ds(0, wide_n)],
                    dq_ref.at[j, :, pl.ds(at, count)], dq_send.at[b, kind, step],
                    dq_recv.at[b, kind], core_of(kind), mate(step),
                )

        def deal_sent(kind):
            _, count = dealt(kind)
            for step in range(mates):
                pushed(
                    dq_ref.at[0, :, pl.ds(0, count)], dq_send.at[b, kind, step], core_of(kind),
                    mate(step),
                )

        def deal_got(kind):
            at, count = dealt(kind)
            got(dq_ref.at[:, :, pl.ds(at, count)], dq_recv.at[b, kind])

        def conv_unit(number, slot, buffer):
            def copies(column):
                which = lax.rem(column, 2)
                return (
                    pltpu.make_async_copy(
                        q_ref.at[slot, column], held.at[which, :, pl.ds(0, n)],
                        load_sem.at[which],
                    ),
                    pltpu.make_async_copy(
                        dq_ref.at[column, :, pl.ds(number * pieces, pieces)],
                        dbuf.at[which, :, :, pl.ds(0, wide_n)], load_sem.at[2 + which],
                    ),
                )

            for copy in copies(jnp.int32(0)):
                copy.start()
            lane = lax.broadcasted_iota(jnp.int32, (lines * pieces, wide_n), 1)
            here = lax.rem(lane, jnp.int32(rows_across))

            def column_terms(column):
                which = lax.rem(column, 2)

                @pl.when(column < mates - 1)
                def _():
                    for copy in copies(column + 1):
                        copy.start()

                for copy in copies(column):
                    copy.wait()
                values = dbuf[which, :, :, pl.ds(0, wide_n)].astype(jnp.float32)
                values = values.reshape(lines * pieces, wide_n)
                if number >= 2:
                    values = jnp.where(lane < n, values, 0.0)
                for side in range(3):
                    moved = values
                    if side == 0:
                        moved = jnp.where(
                            here <= rows_across - 2, pltpu.roll(values, wide_n - 1, 1), 0.0
                        )
                    elif side == 2:
                        moved = jnp.where(here >= 1, pltpu.roll(values, 1, 1), 0.0)
                    for down in range(3):
                        by = moved
                        if down == 0:
                            by = pltpu.roll(moved, wide_n - per_row, 1)
                        elif down == 2:
                            by = pltpu.roll(moved, per_row, 1)
                        by = by.astype(jnp.bfloat16)
                        at = pl.ds((3 * down + side) * pieces, pieces)
                        for line in range(lines):
                            cols[at, pl.ds(line * wide_n, wide_n)] = by[
                                line * pieces : (line + 1) * pieces
                            ]
                terms = dot_nn(cols[pl.ds(0, TAPS * pieces), pl.ds(0, deep)], rows_held(which))

                @pl.when(column == 0)
                def _():
                    for tap in range(TAPS):
                        out[buffer, :, pl.ds(tap * c, c)] = terms[
                            tap * pieces : (tap + 1) * pieces
                        ]

                @pl.when(column > 0)
                def _():
                    for tap in range(TAPS):
                        out[buffer, :, pl.ds(tap * c, c)] += terms[
                            tap * pieces : (tap + 1) * pieces
                        ]

            loop(mates, column_terms)

        def staged_conv(number, slot):
            buffer = turn[0] % 2
            turn[0] += 1
            target = (
                (r_first, r_second)[number] if number < 2
                else r_task.at[pl.ds((number - 2) * pieces, pieces)]
            )
            free(
                buffer,
                lambda: pushed(
                    out.at[buffer], t_send.at[b, number, 0], b, me, t_own.at[number, 0]
                ),
            )
            conv_unit(number, slot, buffer)
            push(
                out.at[buffer], target, t_send.at[b, number, 0], r_recv.at[number], b, me,
                t_own.at[number, 0],
            )

        def flat_terms(kind, staged, parts, lanes, first):
            offset, _ = kinds[kind]
            from_ref = spread_refs(kind)[1]
            copies = [
                fetch(
                    from_ref.at[line, pl.ds(offset + piece * unit, unit), lanes],
                    cols.at[pl.ds(piece * unit, unit), pl.ds(line * wide_n, wide_n)],
                    4 + piece * lines + line,
                )
                for piece in range(tasks)
                for line in range(lines)
            ]
            loads = []
            for at, a_kind in parts:
                for piece in range(tasks):
                    if a_kind is not None:
                        loads.append(a_ref.at[2 + 2 * a_kind + slot_of(piece)])
                    elif piece == 0:
                        loads.append(q_ref.at[1, j])

            def load(number):
                return pltpu.make_async_copy(
                    loads[number], held.at[number % 2, :, pl.ds(first, n)],
                    load_sem.at[number % 2],
                )

            load(0).start()
            for copy in copies:
                copy.wait()
            number = -1
            for at, a_kind in parts:
                for piece in range(tasks):
                    if a_kind is not None or piece == 0:
                        number += 1
                        load(number).wait()
                        if number + 1 < len(loads):
                            load(number + 1).start()
                    terms = dot_nn(
                        cols[pl.ds(piece * unit, unit), pl.ds(0, deep)], rows_held(number % 2)
                    )
                    staged[pl.ds(piece * unit, unit), pl.ds(at, c)] = terms.astype(jnp.bfloat16)

        def flat_push(target, staged, index):
            for mate_at in range(mates):
                push(
                    staged.at[pl.ds(mate_at * own_rows, own_rows)], target.at[j],
                    t_send.at[b, index, mate_at], r_recv.at[index], b, z * mates + mate_at,
                    t_own.at[index, mate_at],
                )

        def flat_sent(staged, index):
            for mate_at in range(mates):
                pushed(
                    staged.at[pl.ds(0, own_rows)], t_send.at[b, index, mate_at], b,
                    z * mates + mate_at, t_own.at[index, mate_at],
                )

        def free(name, waits):
            if name in in_use:
                in_use[name]()
            in_use[name] = waits

        def terms_second():
            deal_got(1)
            shared_got(1)
            staged_conv(1, 1)

        def terms_first():
            deal_got(0)
            shared_got(0)
            staged_conv(0, 0)

        def terms_squeeze():
            spread_got(4)
            if leading:
                got(a_ref.at[0], u_recv.at[0])
            for task in range(tasks):
                task_got(0, task)
            free(2, lambda: flat_sent(stage_flat, 5))
            flat_terms(4, stage_flat, [(0, None), (c, 0)], pl.ds(0, wide_n), 0)
            flat_push(r_squeeze, stage_flat, 5)

        def terms_expand():
            for task in range(tasks):
                task_got(1, task)
            staged = stage_flat.at[:, pl.ds(0, c)]
            free(2, lambda: flat_sent(staged, 6))
            for buffer in range(2):
                held[buffer, :, pl.ds(0, second_at), :] = jnp.zeros(
                    (lines, second_at, c), jnp.bfloat16
                )
            flat_terms(2, staged, [(0, 1)], pl.ds(n - second_at, wide_n), second_at)
            flat_push(r_expand, staged, 6)
            clear_tail()

        def terms_tasks():
            deal_got(2)
            for task in range(tasks):
                task_got(2, task)
            for number in range(own_rows // pieces):
                task = (own_rows * me + number * pieces) // c
                staged_conv(2 + number, 2 + task - plane_tasks(z)[0])

        def terms_got():
            if leading:
                for number in range(own_rows // pieces):
                    got(r_first, r_recv.at[2 + number])
            senders = pl.ds(0, mates if leading else mates - 1)
            for index, target in ((5, r_squeeze), (6, r_expand)):
                got(target.at[senders], r_recv.at[index])

        def set_up():
            image = lax.div(
                lax.broadcasted_iota(jnp.int32, (per_row, c), 0), jnp.int32(rows_across)
            )
            for k in range(micro):
                masks[k, used, :] = (
                    jnp.where(image == k, 1.0, 0.0)
                    + jnp.where(image == micro, fourth[k], 0.0)
                    + jnp.where(image == micro + 1, fifth[k], 0.0)
                )
            zero = jnp.zeros((per_row, 3 * c), jnp.bfloat16)
            pad[pl.ds(0, per_row), :] = zero
            pad[pl.ds(n + per_row, per_row), :] = zero

        return types.SimpleNamespace(
            forward_start=forward_start, forward=forward, backward=backward, settle=settle,
            set_up=set_up, clear_tail=clear_tail, exchange=exchange_activations,
            exchange_sent=exchange_sent,
            second=terms_second, first=terms_first, squeeze=terms_squeeze, expand=terms_expand,
            task_terms=terms_tasks, terms_got=terms_got, deal=deal, deal_sent=deal_sent,
        )

    weight_copy(W_FIRST).start()
    weight_copy(W_SQUEEZE).start()
    barrier = pltpu.get_barrier_semaphore()
    greeted = (
        [(section, mate(step)) for step in range(1, mates)]
        + [(section, liner(step)) for step in range(1, lines)]
        + [(other, mate(step)) for step in range(mates)]
        + [(other, liner(step)) for step in range(1, lines)]
    )
    for device in greeted:
        pl.semaphore_signal(barrier, inc=1, device_id=device, device_id_type=MESH)
    numbers = [count_ref[0, k] for k in range(micro)]
    double = [jnp.where(number >= 2, jnp.float32(1.0), jnp.float32(0.0)) for number in numbers]
    fourth, fifth = [], []
    before = jnp.float32(0.0)
    for k in range(micro):
        fourth.append(double[k] * (1.0 - before))
        fifth.append(double[k] * before)
        before = before + double[k]
    count_slot = sums_at(F_FIRST)[0]
    count_slot[0, j, 1] = jnp.zeros((8, c), jnp.float32)
    for k in range(micro):
        count_slot[0, j, 1, pl.ds(k, 1), :] = jnp.full((1, c), 1.0) * (1.0 + double[k])
    for index in range(NORMS):
        at = pl.ds(index if index < NARROW else index - NARROW, 1)
        gain[index] = (gain_in if index < NARROW else narrow_gain)[at, :]
        shift[index] = (shift_in if index < NARROW else narrow_shift)[at, :]
    in_use, turn = {}, [0]
    one, two = make_block(0), make_block(1)

    def picked_rows(values, index, h):
        doubles = [values[index, 2 * k + 1, h].astype(jnp.float32) for k in range(micro)]
        rows_of = [values[index, 2 * k, h].astype(jnp.float32) for k in range(micro)]
        for weight in (fourth, fifth):
            picked = doubles[0] * weight[0]
            for k in range(1, micro):
                picked = picked + doubles[k] * weight[k]
            rows_of.append(picked)
        return rows_of

    def compact(index):
        for h in range(high):
            x_one[index, pl.ds(h * live * across, live * across), :] = jnp.concatenate(
                picked_rows(stream, index, h), axis=0
            ).astype(jnp.bfloat16)

    def cotangents():
        for index in range(1 + tasks):
            og_ref[index] = jnp.zeros(og_ref.shape[1:], jnp.float32)
            for i, upstream in enumerate(picked_rows(cotangent, index, 0)):
                og_ref[index, pl.ds(i * (across // 4), across // 4), :] = upstream

    @pl.when(section == 0)
    def _():
        one.set_up()
        loop(1 + tasks, compact)
        pl.semaphore_wait(barrier, len(greeted))
        one.forward_start()
        one.forward()
        one.exchange()
        two.exchange()
        one.clear_tail()
        one.backward()
        one.deal(1)
        one.deal(0)
        one.second()
        one.first()
        for waits in in_use.values():
            waits()
        in_use.clear()
        for kind in range(2):
            one.deal_sent(kind)
        one.exchange_sent()
        two.exchange_sent()
        one.settle()
        one.terms_got()

    @pl.when(section == 1)
    def _():
        two.set_up()
        cotangents()
        pl.semaphore_wait(barrier, len(greeted))
        two.forward_start()
        two.forward()
        two.backward()
        for kind in range(3):
            two.deal(kind)
        two.clear_tail()
        two.expand()
        two.second()
        two.squeeze()
        two.task_terms()
        two.first()
        one.deal(2)
        one.clear_tail()
        one.expand()
        one.task_terms()
        one.squeeze()
        for waits in in_use.values():
            waits()
        one.deal_sent(2)
        for kind in range(3):
            two.deal_sent(kind)
        two.settle()
        two.terms_got()


def result_kernel(plan, *refs):
    (
        count_ref, first, second, squeeze, expand, task, pooled, grads, norms, totals,
        first_out, second_out, squeeze_out, expand_out, task_out, feature_out, input_out,
        gain_out, shift_out, narrow_gain_out, narrow_shift_out, rms_out,
    ) = refs
    mates, tasks, c = plan["mates"], plan["tasks"], plan["channels"]
    section = lax.axis_index("section")
    live, micro = plan["live"], plan["micro"]
    images_of = []
    before = jnp.int32(micro)
    for k in range(micro):
        double = count_ref[0, k] >= 2
        images_of.append(jnp.where(double, before, jnp.int32(-1)))
        before = before + jnp.where(double, jnp.int32(1), jnp.int32(0))

    def aligned(values, image, rows, used):
        start = image * rows
        values = pltpu.roll(values, values.shape[0] - start, 0) if start else values
        inside = lax.broadcasted_iota(jnp.int32, (8, c), 0) < used
        return jnp.where(inside, values[:8], 0.0)

    def by_slot(values, rows, used, store):
        two = [aligned(values, micro, rows, used), aligned(values, micro + 1, rows, used)]
        for k in range(micro):
            store(2 * k, aligned(values, k, rows, used))
            which = images_of[k]
            store(
                2 * k + 1,
                jnp.where(which == micro, two[0], jnp.where(which == micro + 1, two[1], 0.0)),
            )

    def place_out(high, across, images, leading):
        per_row = images * across
        for index in range(1 + tasks):
            for h in range(plan["high"]):

                def store(slot, values):
                    input_out[index, slot, h] = values

                if h < high:
                    by_slot(grads[index, pl.ds(h * per_row, per_row), :], across, across, store)
                else:
                    for slot in range(2 * micro):
                        store(slot, jnp.zeros((8, c), jnp.float32))
            for h in range(plan["high"] // 2):

                def store_feature(slot, values):
                    feature_out[index, slot, h] = values[: plan["across"] // 2].astype(
                        jnp.bfloat16
                    )

                if h < high // 2:
                    count = 8 * (across // 2)
                    by_slot(
                        pooled[index, pl.ds(h * count, count), :].astype(jnp.float32),
                        across // 2, across // 2, store_feature,
                    )
                else:
                    for slot in range(2 * micro):
                        store_feature(slot, jnp.zeros((8, c), jnp.float32))
        cells = float(high * across // 4 * c)
        live_total = jnp.sum(totals[0, pl.ds(0, micro), pl.ds(0, 1)], axis=0, keepdims=True)
        lane = lax.broadcasted_iota(jnp.int32, (1, 1 + tasks), 1)
        result = jnp.zeros((1, 1 + tasks), jnp.float32)
        for index in range(1 + tasks):
            square = jnp.sum(totals[1, pl.ds(index, 1), :], axis=1, keepdims=True)
            result = jnp.where(lane == index, jnp.sqrt(square / (live_total * cells)), result)
        rms_out[...] = result
        for index in range(NORMS):
            shift_sum = jnp.sum(norms[index, pl.ds(0, micro), :], axis=0, keepdims=True)
            gain_sum = jnp.sum(norms[index, pl.ds(micro, micro), :], axis=0, keepdims=True)
            if index < NARROW:
                gain_out[pl.ds(index, 1), :] = gain_sum
                shift_out[pl.ds(index, 1), :] = shift_sum
            else:
                narrow_gain_out[pl.ds(index - NARROW, 1), :] = gain_sum
                narrow_shift_out[pl.ds(index - NARROW, 1), :] = shift_sum

    @pl.when((pl.program_id(0) == 0) & (section == 0))
    def _():
        place_out(plan["high"], plan["across"], live, True)

    @pl.when((pl.program_id(0) == 0) & (section == 1))
    def _():
        place_out(plan["high"] // 2, plan["across"] // 2, 8, False)

    for terms, target in (
        (first, first_out), (second, second_out), (squeeze, squeeze_out),
        (expand, expand_out), (task, task_out),
    ):
        count, width = terms.shape[-2:]
        per_row = width // 128
        for lane in range(per_row):
            at = pl.ds(lane * 128, 128)
            if len(terms.shape) == 2:
                summed = terms[:, at]
            else:
                summed = terms[0, :, at].astype(jnp.float32)
                for place in range(1, mates):
                    summed = summed + terms[place, :, at].astype(jnp.float32)
            target[pl.ds(lane, count, stride=per_row), :] = summed


def gathered_shards(
    stream_in, image_count, out_grad, first_conv, second_conv, squeeze, expand, task_conv,
    norm_gain, norm_shift, squeeze_gain, squeeze_shift,
):
    maps, images, high, across, c = stream_in.shape
    micro = image_count.shape[1]
    tasks = maps - 1
    groups = lax.axis_size("dp")
    mates = 4
    lines = groups // mates
    live = images - 2
    n = high * live * across
    wide_n = 256
    plan = {
        "lines": lines, "mates": mates, "tasks": tasks, "channels": c,
        "high": high, "across": across, "live": live, "wide": wide_n, "micro": micro,
    }
    conv_rows = c // groups
    task_rows = tasks * c // groups
    bf16, f32 = jnp.bfloat16, jnp.float32
    vmem = pl.BlockSpec(memory_space=pltpu.VMEM)
    whole = pl.BlockSpec(memory_space=pl.ANY)
    shapes = (
        (conv_rows, TAPS * c), (conv_rows, TAPS * c), (task_rows, 2 * c), (task_rows, c),
        (task_rows, TAPS * c),
    )
    formed = (True, True, False, False, True)
    small = 64
    single_rows = (2 + tasks) * c // lines
    out_shape = (
        [
            jax.ShapeDtypeStruct((maps, small, c), bf16),
            jax.ShapeDtypeStruct((maps, n, c), f32),
            jax.ShapeDtypeStruct((NORMS, 8, c), f32),
            jax.ShapeDtypeStruct((2, 8, c), f32),
            jax.ShapeDtypeStruct((8, lines, n, c), bf16),
            jax.ShapeDtypeStruct((8, lines, small, c), bf16),
            jax.ShapeDtypeStruct((lines, single_rows, wide_n), bf16),
            jax.ShapeDtypeStruct((lines, single_rows, 128), bf16),
            jax.ShapeDtypeStruct((lines, mates * task_rows, 2 * n), bf16),
            jax.ShapeDtypeStruct((lines, mates * task_rows, 2 * small), bf16),
        ]
        + [
            jax.ShapeDtypeStruct((4, mates, lines, n, c), bf16),
            jax.ShapeDtypeStruct((4, mates, lines, small, c), bf16),
            jax.ShapeDtypeStruct((mates, lines, 2 * conv_rows + task_rows, wide_n), bf16),
            jax.ShapeDtypeStruct((mates, lines, 2 * conv_rows + task_rows, 128), bf16),
            jax.ShapeDtypeStruct((1 + 2 * tasks, small, c), bf16),
        ]
        + [
            jax.ShapeDtypeStruct(shape, f32) if whole_terms
            else jax.ShapeDtypeStruct((mates,) + shape, bf16)
            for shape, whole_terms in zip(shapes, formed)
        ]
    )
    row = live * across
    scratch = [
        pltpu.VMEM(shape, dtype)
        for shape, dtype in (
            ((c, TAPS * c), bf16),
            ((c, TAPS * c), bf16),
            ((tasks, c, 2 * c), bf16),
            ((tasks, c, c), bf16),
            ((tasks, c, TAPS * c), bf16),
            ((NORMS, 1, c), f32),
            ((NORMS, 1, c), f32),
            ((maps, n, c), bf16),
            ((maps, small, c), bf16),
            ((maps, 16, c), f32),
            ((maps, small, c), bf16),
            ((maps, small, c), bf16),
            ((micro, row, c), f32),
            (((high + 2) * row, 3 * c), bf16),
            ((NORMS, n, c), f32),
            ((NORMS, n, c), f32),
            ((maps, n, c), f32),
            ((n, c), f32),
            ((n, c), bf16),
            ((tasks, n, c), bf16),
            ((tasks, n, c), bf16),
            ((4, n, c), f32),
            ((n, c), f32),
            ((3, row, c), f32),
            ((NORMS, micro, c), f32),
            ((4, 8, c), f32),
            ((8, c), f32),
            ((maps, 1, c), f32),
            ((c // 128, row, 128), f32),
            ((2 * n, c), f32),
            ((2 + tasks, c, wide_n), bf16),
            ((tasks, c, 2 * n), bf16),
            ((3, 2, 4, 2, 8, c), f32),
            ((4, 2, 4, 3, 8, c), f32),
            ((2, 2, 4, 4, 8, c), f32),
            ((2, lines, wide_n, c), bf16),
            ((2, lines, conv_rows, wide_n), bf16),
            ((3 * c // lines, lines * wide_n), bf16),
            ((2, conv_rows, TAPS * c), f32),
            ((mates * task_rows, 2 * c), bf16),
        )
    ] + [
        pltpu.SemaphoreType.DMA(shape)
        for shape in (
            (4 + tasks,), (GROUPS_OF_SUMS, 2), (GROUPS_OF_SUMS, 2), (2 * maps,), (2 * maps,),
            (2, NORMS, 4), (2, NORMS, 2), (2, 8, mates), (2, 8), (2, 4), (1 + 2 * tasks,),
            (1 + 2 * tasks,), (1,), (1,), (5, tasks, lines), (2, 5),
            (2, 3, mates), (2, 3), (2, 7, mates),
            (7, mates), (7,), (4 + tasks * lines,),
        )
    ]
    results = pl.pallas_call(
        functools.partial(main_kernel, plan),
        out_shape=out_shape,
        in_specs=[pl.BlockSpec(memory_space=pltpu.SMEM)] + [vmem] * 6 + [whole] * 5,
        out_specs=[vmem] * 4 + [whole] * 16,
        scratch_shapes=scratch,
        compiler_params=pltpu.CompilerParams(
            collective_id=1, has_side_effects=True, vmem_limit_bytes=62 * 2**20
        ),
        name="blocks",
    )(
        image_count, stream_in, out_grad, norm_gain[0], norm_shift[0], squeeze_gain[0],
        squeeze_shift[0], first_conv[0], second_conv[0], squeeze[0], expand[0], task_conv[0],
    )
    pooled, grads, norms, totals = results[:4]
    terms = results[15:]
    steps = 2

    def flat(shape):
        return jax.ShapeDtypeStruct((shape[0] * shape[1] // 128, 128), f32)

    results = pl.pallas_call(
        functools.partial(result_kernel, plan),
        grid=(steps,),
        out_shape=[flat(shape) for shape in shapes]
        + [
            jax.ShapeDtypeStruct((maps, images, high // 2, across // 2, c), bf16),
            jax.ShapeDtypeStruct((maps, images, high, across, c), f32),
            jax.ShapeDtypeStruct((NARROW, c), f32),
            jax.ShapeDtypeStruct((NARROW, c), f32),
            jax.ShapeDtypeStruct((tasks, c), f32),
            jax.ShapeDtypeStruct((tasks, c), f32),
            jax.ShapeDtypeStruct((1, maps), f32),
        ],
        in_specs=[pl.BlockSpec(memory_space=pltpu.SMEM)]
        + [
            pl.BlockSpec((shape[0] // steps, shape[1]), lambda i: (i, 0)) if whole_terms
            else pl.BlockSpec((mates, shape[0] // steps, shape[1]), lambda i: (0, i, 0))
            for shape, whole_terms in zip(shapes, formed)
        ]
        + [vmem] * 4,
        out_specs=[
            pl.BlockSpec((shape[0] // steps * shape[1] // 128, 128), lambda i: (i, 0))
            for shape in shapes
        ]
        + [vmem] * 7,
        compiler_params=pltpu.CompilerParams(vmem_limit_bytes=62 * 2**20),
        name="results",
    )(image_count, *terms, pooled, grads, norms, totals)
    first_g, second_g, squeeze_g, expand_g, task_g = (
        grad.reshape(1, -1) for grad in results[:5]
    )
    feature_out, input_out, gain_g, shift_g, narrow_gain_g, narrow_shift_g, rms = results[5:]
    return (
        feature_out[None], input_out[None], first_g, second_g, squeeze_g, expand_g, task_g,
        gain_g[None], shift_g[None], narrow_gain_g[None], narrow_shift_g[None], rms,
    )


def solution(mesh):
    groups = mesh.shape["dp"]
    whole_tiles = groups == 4 * 4
    return jax.shard_map(
        gathered_shards if whole_tiles else shards,
        mesh=mesh,
        in_specs=(
            P(None, "dp", None, None, None),
            P("dp", None),
            P(None, "dp", None, None, None),
            P("section", None, None),
            P("section", None, None),
            P("section", None, None, None),
            P("section", None, None, None),
            P("section", None, None, None),
            P("section", None, None),
            P("section", None, None),
            P("section", None, None),
            P("section", None, None),
        ),
        out_specs=(
            P("section", None, "dp", None, None, None),
            P("section", None, "dp", None, None, None),
            P("section", "dp"),
            P("section", "dp"),
            P("section", "dp"),
            P("section", "dp"),
            P("section", "dp"),
            P("section", None, None),
            P("section", None, None),
            P("section", None, None),
            P("section", None, None),
            P("section", None),
        ),
        check_vma=False,
    )
```

time: 270 us -> 262 us (0.970); the launches traced: 269 us -> 258 us
  Pallas kernels: 265 us -> 254 us
    pallas_call x1, Pallas kernels: 259 us -> 248 us  [gathered_shards(): pl.pallas_call(functools.partial(main_kernel, plan), out_shape=out_shape,...]
where the time goes in v2:
time: 262 us; the launch traced here: 258 us
  Pallas kernels  254 us (97%)
  local copies, waits for them, and re-layouts  3.91 us (1%)
    pallas_call x1, Pallas kernels, gathered_shards(): pl.pallas_call(functools.partial(main_kernel, plan), out_shape=out_shape,...  248 us
    pallas_call x1, Pallas kernels, gathered_shards(): pl.pallas_call(functools.partial(result_kernel, plan), grid=(steps,), out...  5.45 us

profile of v2, /device:TPU:6, one launch (start us, length us, event | category | flops | bytes accessed | tf_op | source)
XLA Modules:
  0.0 258.1 jit_solution(13270661803265618256)
XLA Ops:
  0.6 1.3 copy_bitcast_fusion
  2.0 248.1 %blocks.1 = (bf16[4,64,512]{2,1,0:T(8,128)(2,1)}, f32[4,192,512]{2,1,0:T(8,128)}, f32[11,8,512]{2,1,0:T(8,128)}, f32[2,8,512]{2,1,0:T(8,128)}, bf16[8,4,192,512]...) custom-call(s32[1,4]{1,0:T(1,128)} %refs_0_.3, ...), custom_call_target="tpu_custom_call" | custom-call | tf_op jit(solution)/shard_map/blocks/pallas_call | solution.py:2084
  250.0 5.5 %results.1 = (f32[1152,128]{1,0:T(8,128)}, f32[1152,128]{1,0:T(8,128)}, f32[768,128]{1,0:T(8,128)}, f32[384,128]{1,0:T(8,128)}, f32[3456,128]{1,0:T(8,128)}, /*i...) custom-call(s32[1,4]{1,0:T(1,128)} %refs_0_.3, ...), custom_call_target="tpu_custom_call" | custom-call | tf_op jit(solution)/shard_map/results/pallas_call | solution.py:2105
  255.5 1.3 copy.24
  256.8 1.3 copy.25

commit v3 on v2

--- a/solution.py
+++ b/solution.py
@@ -1007,7 +1007,7 @@
                     ).start()
 
         def core_of(kind):
-            return 0 if leading and kind < 2 else 1
+            return 0 if kind < 2 else 1
 
         def deliver(at, slot, task=None):
             for step in range(mates):
@@ -1101,8 +1101,7 @@
             relays(1)
             relay_far(1)
             deliver(1, 1)
-            if leading:
-                across_cores(a_ref.at[1], q_ref.at[1, j], u_send.at[0], u_recv.at[0])
+            across_cores(a_ref.at[1], q_ref.at[1, j], u_send.at[b], u_recv.at[b])
             send_tasks(2)
             done(1)
             relays(2)
@@ -1120,8 +1119,7 @@
                         sent(pair_lines(which, 0), a_send.at[b, which, at])
 
                 delivered(which)
-            if leading:
-                sent(a_ref.at[0], u_send.at[0])
+            sent(a_ref.at[0], u_send.at[b])
             for kind in range(3):
                 for task in range(tasks):
                     first, last = task_planes(task)
@@ -1348,7 +1346,7 @@
             if leading:
                 got(sg_in.at[0], h_recv.at[1 + tasks + index])
 
-        def backward():
+        def backward(work):
             def task_start(task):
                 handed(1 + task)
                 first = second = None
@@ -1365,7 +1363,9 @@
 
             loop(tasks, task_start)
             start(B_TASK)
+            work(0)
             mid(B_TASK)
+            work(1)
             end(B_TASK)
             total_ref[1] = tot[tasks]
 
@@ -1407,7 +1407,9 @@
                     second = by if second is None else second + by
             write_stats(B_MASK, tasks, first, second)
             start(B_MASK)
+            work(2)
             mid(B_MASK)
+            work(3)
             end(B_MASK)
 
             def mask_back(task):
@@ -1462,7 +1464,9 @@
                 second = by if second is None else second + by
             write_stats(B_FIRST, 0, first, second)
             start(B_FIRST)
+            work(4)
             mid(B_FIRST)
+            work(5)
             end(B_FIRST)
             rounded(FIRST, 0, 3, turned.at[0])
             if leading:
@@ -1701,8 +1705,7 @@
 
         def terms_squeeze():
             spread_got(4)
-            if leading:
-                got(a_ref.at[0], u_recv.at[0])
+            got(a_ref.at[0], u_recv.at[b])
             for task in range(tasks):
                 task_got(0, task)
             free(2, lambda: flat_sent(stage_flat, 5))
@@ -1731,9 +1734,9 @@
                 staged_conv(2 + number, 2 + task - plane_tasks(z)[0])
 
         def terms_got():
-            if leading:
-                for number in range(own_rows // pieces):
-                    got(r_first, r_recv.at[2 + number])
+            away = range(2, 2 + own_rows // pieces) if leading else range(2)
+            for number in away:
+                got(r_first, r_recv.at[number])
             senders = pl.ds(0, mates if leading else mates - 1)
             for index, target in ((5, r_squeeze), (6, r_expand)):
                 got(target.at[senders], r_recv.at[index])
@@ -1785,8 +1788,8 @@
         count_slot[0, j, 1, pl.ds(k, 1), :] = jnp.full((1, c), 1.0) * (1.0 + double[k])
     for index in range(NORMS):
         at = pl.ds(index if index < NARROW else index - NARROW, 1)
-        gain[index] = (gain_in if index < NARROW else narrow_gain)[at, :]
-        shift[index] = (shift_in if index < NARROW else narrow_shift)[at, :]
+        gain[index] = gain_in[at, :] if index < NARROW else narrow_gain[index - NARROW]
+        shift[index] = shift_in[at, :] if index < NARROW else narrow_shift[index - NARROW]
     in_use, turn = {}, [0]
     one, two = make_block(0), make_block(1)
 
@@ -1821,17 +1824,32 @@
         one.forward()
         one.exchange()
         two.exchange()
-        one.clear_tail()
-        one.backward()
-        one.deal(1)
+
+        def work(place):
+            if place == 0:
+                two.clear_tail()
+                two.deal(1)
+            elif place == 1:
+                two.second()
+            elif place == 2:
+                two.deal(0)
+            elif place == 3:
+                two.first()
+                one.clear_tail()
+            elif place == 4:
+                one.deal(1)
+            else:
+                one.second()
+
+        one.backward(work)
         one.deal(0)
-        one.second()
         one.first()
         for waits in in_use.values():
             waits()
         in_use.clear()
         for kind in range(2):
             one.deal_sent(kind)
+            two.deal_sent(kind)
         one.exchange_sent()
         two.exchange_sent()
         one.settle()
@@ -1844,15 +1862,12 @@
         pl.semaphore_wait(barrier, len(greeted))
         two.forward_start()
         two.forward()
-        two.backward()
-        for kind in range(3):
-            two.deal(kind)
+        two.backward(lambda place: None)
+        two.deal(2)
         two.clear_tail()
         two.expand()
-        two.second()
         two.squeeze()
         two.task_terms()
-        two.first()
         one.deal(2)
         one.clear_tail()
         one.expand()
@@ -1861,8 +1876,7 @@
         for waits in in_use.values():
             waits()
         one.deal_sent(2)
-        for kind in range(3):
-            two.deal_sent(kind)
+        two.deal_sent(2)
         two.settle()
         two.terms_got()
 
@@ -1943,8 +1957,8 @@
                 gain_out[pl.ds(index, 1), :] = gain_sum
                 shift_out[pl.ds(index, 1), :] = shift_sum
             else:
-                narrow_gain_out[pl.ds(index - NARROW, 1), :] = gain_sum
-                narrow_shift_out[pl.ds(index - NARROW, 1), :] = shift_sum
+                narrow_gain_out[index - NARROW] = gain_sum
+                narrow_shift_out[index - NARROW] = shift_sum
 
     @pl.when((pl.program_id(0) == 0) & (section == 0))
     def _():
@@ -2076,7 +2090,7 @@
         for shape in (
             (4 + tasks,), (GROUPS_OF_SUMS, 2), (GROUPS_OF_SUMS, 2), (2 * maps,), (2 * maps,),
             (2, NORMS, 4), (2, NORMS, 2), (2, 8, mates), (2, 8), (2, 4), (1 + 2 * tasks,),
-            (1 + 2 * tasks,), (1,), (1,), (5, tasks, lines), (2, 5),
+            (1 + 2 * tasks,), (2,), (2,), (5, tasks, lines), (2, 5),
             (2, 3, mates), (2, 3), (2, 7, mates),
             (7, mates), (7,), (4 + tasks * lines,),
         )
@@ -2092,8 +2106,8 @@
         ),
         name="blocks",
     )(
-        image_count, stream_in, out_grad, norm_gain[0], norm_shift[0], squeeze_gain[0],
-        squeeze_shift[0], first_conv[0], second_conv[0], squeeze[0], expand[0], task_conv[0],
+        image_count, stream_in, out_grad, norm_gain[0], norm_shift[0],
+        jnp.swapaxes(squeeze_gain, 0, 1), jnp.swapaxes(squeeze_shift, 0, 1), first_conv[0], second_conv[0], squeeze[0], expand[0], task_conv[0],
     )
     pooled, grads, norms, totals = results[:4]
     terms = results[15:]
@@ -2111,8 +2125,8 @@
             jax.ShapeDtypeStruct((maps, images, high, across, c), f32),
             jax.ShapeDtypeStruct((NARROW, c), f32),
             jax.ShapeDtypeStruct((NARROW, c), f32),
-            jax.ShapeDtypeStruct((tasks, c), f32),
-            jax.ShapeDtypeStruct((tasks, c), f32),
+            jax.ShapeDtypeStruct((tasks, 1, c), f32),
+            jax.ShapeDtypeStruct((tasks, 1, c), f32),
             jax.ShapeDtypeStruct((1, maps), f32),
         ],
         in_specs=[pl.BlockSpec(memory_space=pltpu.SMEM)]
@@ -2136,7 +2150,8 @@
     feature_out, input_out, gain_g, shift_g, narrow_gain_g, narrow_shift_g, rms = results[5:]
     return (
         feature_out[None], input_out[None], first_g, second_g, squeeze_g, expand_g, task_g,
-        gain_g[None], shift_g[None], narrow_gain_g[None], narrow_shift_g[None], rms,
+        gain_g[None], shift_g[None], jnp.swapaxes(narrow_gain_g, 0, 1),
+        jnp.swapaxes(narrow_shift_g, 0, 1), rms,
     )
 
 

time: 262 us -> 261 us (level)
  local copies, waits for them, and re-layouts: 3.91 us -> 0 us
  Pallas kernels: 254 us -> 257 us
    unnamed x3 -> x0, local copies, waits for them, and re-layouts: 3.91 us -> none
    pallas_call x1, Pallas kernels: 248 us -> 251 us  [gathered_shards(): pl.pallas_call(functools.partial(main_kernel, plan), out_shape=out_shape,...]
where the time goes in v3:
time: 261 us; the launch traced here: 258 us
  Pallas kernels  257 us (98%)
    pallas_call x1, Pallas kernels, gathered_shards(): pl.pallas_call(functools.partial(main_kernel, plan), out_shape=out_shape,...  251 us
    pallas_call x1, Pallas kernels, gathered_shards(): pl.pallas_call(functools.partial(result_kernel, plan), grid=(steps,), out...  5.37 us

profile of v3, /device:TPU:6, one launch (start us, length us, event | category | flops | bytes accessed | tf_op | source)
XLA Modules:
  0.0 257.5 jit_solution(14449390435580666745)
XLA Ops:
  0.6 251.3 %blocks.1 = (bf16[4,64,512]{2,1,0:T(8,128)(2,1)}, f32[4,192,512]{2,1,0:T(8,128)}, f32[11,8,512]{2,1,0:T(8,128)}, f32[2,8,512]{2,1,0:T(8,128)}, bf16[8,4,192,512]...) custom-call(s32[1,4]{1,0:T(1,128)} %refs_0_.3, ...), custom_call_target="tpu_custom_call" | custom-call | tf_op jit(solution)/shard_map/blocks/pallas_call | solution.py:2098
  252.0 5.4 %results.1 = (f32[1152,128]{1,0:T(8,128)}, f32[1152,128]{1,0:T(8,128)}, f32[768,128]{1,0:T(8,128)}, f32[384,128]{1,0:T(8,128)}, f32[3456,128]{1,0:T(8,128)}, /*i...) custom-call(s32[1,4]{1,0:T(1,128)} %refs_0_.3, ...), custom_call_target="tpu_custom_call" | custom-call | tf_op jit(solution)/shard_map/results/pallas_call | solution.py:2119

commit v4 on v2

--- a/solution.py
+++ b/solution.py
@@ -1348,7 +1348,7 @@
             if leading:
                 got(sg_in.at[0], h_recv.at[1 + tasks + index])
 
-        def backward():
+        def backward(work):
             def task_start(task):
                 handed(1 + task)
                 first = second = None
@@ -1462,7 +1462,9 @@
                 second = by if second is None else second + by
             write_stats(B_FIRST, 0, first, second)
             start(B_FIRST)
+            work(0)
             mid(B_FIRST)
+            work(1)
             end(B_FIRST)
             rounded(FIRST, 0, 3, turned.at[0])
             if leading:
@@ -1785,8 +1787,8 @@
         count_slot[0, j, 1, pl.ds(k, 1), :] = jnp.full((1, c), 1.0) * (1.0 + double[k])
     for index in range(NORMS):
         at = pl.ds(index if index < NARROW else index - NARROW, 1)
-        gain[index] = (gain_in if index < NARROW else narrow_gain)[at, :]
-        shift[index] = (shift_in if index < NARROW else narrow_shift)[at, :]
+        gain[index] = gain_in[at, :] if index < NARROW else narrow_gain[index - NARROW]
+        shift[index] = shift_in[at, :] if index < NARROW else narrow_shift[index - NARROW]
     in_use, turn = {}, [0]
     one, two = make_block(0), make_block(1)
 
@@ -1822,10 +1824,8 @@
         one.exchange()
         two.exchange()
         one.clear_tail()
-        one.backward()
-        one.deal(1)
+        one.backward(lambda place: one.second() if place else one.deal(1))
         one.deal(0)
-        one.second()
         one.first()
         for waits in in_use.values():
             waits()
@@ -1844,7 +1844,7 @@
         pl.semaphore_wait(barrier, len(greeted))
         two.forward_start()
         two.forward()
-        two.backward()
+        two.backward(lambda place: None)
         for kind in range(3):
             two.deal(kind)
         two.clear_tail()
@@ -1943,8 +1943,8 @@
                 gain_out[pl.ds(index, 1), :] = gain_sum
                 shift_out[pl.ds(index, 1), :] = shift_sum
             else:
-                narrow_gain_out[pl.ds(index - NARROW, 1), :] = gain_sum
-                narrow_shift_out[pl.ds(index - NARROW, 1), :] = shift_sum
+                narrow_gain_out[index - NARROW] = gain_sum
+                narrow_shift_out[index - NARROW] = shift_sum
 
     @pl.when((pl.program_id(0) == 0) & (section == 0))
     def _():
@@ -2076,7 +2076,7 @@
         for shape in (
             (4 + tasks,), (GROUPS_OF_SUMS, 2), (GROUPS_OF_SUMS, 2), (2 * maps,), (2 * maps,),
             (2, NORMS, 4), (2, NORMS, 2), (2, 8, mates), (2, 8), (2, 4), (1 + 2 * tasks,),
-            (1 + 2 * tasks,), (1,), (1,), (5, tasks, lines), (2, 5),
+            (1 + 2 * tasks,), (2,), (2,), (5, tasks, lines), (2, 5),
             (2, 3, mates), (2, 3), (2, 7, mates),
             (7, mates), (7,), (4 + tasks * lines,),
         )
@@ -2092,8 +2092,8 @@
         ),
         name="blocks",
     )(
-        image_count, stream_in, out_grad, norm_gain[0], norm_shift[0], squeeze_gain[0],
-        squeeze_shift[0], first_conv[0], second_conv[0], squeeze[0], expand[0], task_conv[0],
+        image_count, stream_in, out_grad, norm_gain[0], norm_shift[0],
+        jnp.swapaxes(squeeze_gain, 0, 1), jnp.swapaxes(squeeze_shift, 0, 1), first_conv[0], second_conv[0], squeeze[0], expand[0], task_conv[0],
     )
     pooled, grads, norms, totals = results[:4]
     terms = results[15:]
@@ -2111,8 +2111,8 @@
             jax.ShapeDtypeStruct((maps, images, high, across, c), f32),
             jax.ShapeDtypeStruct((NARROW, c), f32),
             jax.ShapeDtypeStruct((NARROW, c), f32),
-            jax.ShapeDtypeStruct((tasks, c), f32),
-            jax.ShapeDtypeStruct((tasks, c), f32),
+            jax.ShapeDtypeStruct((tasks, 1, c), f32),
+            jax.ShapeDtypeStruct((tasks, 1, c), f32),
             jax.ShapeDtypeStruct((1, maps), f32),
         ],
         in_specs=[pl.BlockSpec(memory_space=pltpu.SMEM)]
@@ -2136,15 +2136,16 @@
     feature_out, input_out, gain_g, shift_g, narrow_gain_g, narrow_shift_g, rms = results[5:]
     return (
         feature_out[None], input_out[None], first_g, second_g, squeeze_g, expand_g, task_g,
-        gain_g[None], shift_g[None], narrow_gain_g[None], narrow_shift_g[None], rms,
+        gain_g[None], shift_g[None], jnp.swapaxes(narrow_gain_g, 0, 1),
+        jnp.swapaxes(narrow_shift_g, 0, 1), rms,
     )
 
 
 def solution(mesh):
     groups = mesh.shape["dp"]
-    whole_tiles = groups == 4 * 4
+    four_by_four = groups == 4 * 4
     return jax.shard_map(
-        gathered_shards if whole_tiles else shards,
+        gathered_shards if four_by_four else shards,
         mesh=mesh,
         in_specs=(
             P(None, "dp", None, None, None),

time: 262 us -> 258 us (0.985)
  local copies, waits for them, and re-layouts: 3.91 us -> 0 us
    unnamed x3 -> x0, local copies, waits for them, and re-layouts: 3.91 us -> none
where the time goes in v4:
time: 258 us; the launch traced here: 254 us
  Pallas kernels  254 us (98%)
    pallas_call x1, Pallas kernels, gathered_shards(): pl.pallas_call(functools.partial(main_kernel, plan), out_shape=out_shape,...  248 us
    pallas_call x1, Pallas kernels, gathered_shards(): pl.pallas_call(functools.partial(result_kernel, plan), grid=(steps,), out...  5.37 us

profile of v4, /device:TPU:6, one launch (start us, length us, event | category | flops | bytes accessed | tf_op | source)
XLA Modules:
  0.0 254.4 jit_solution(14972708502937386855)
XLA Ops:
  0.6 248.2 %blocks.1 = (bf16[4,64,512]{2,1,0:T(8,128)(2,1)}, f32[4,192,512]{2,1,0:T(8,128)}, f32[11,8,512]{2,1,0:T(8,128)}, f32[2,8,512]{2,1,0:T(8,128)}, bf16[8,4,192,512]...) custom-call(s32[1,4]{1,0:T(1,128)} %refs_0_.3, ...), custom_call_target="tpu_custom_call" | custom-call | tf_op jit(solution)/shard_map/blocks/pallas_call | solution.py:2084
  248.9 5.4 %results.1 = (f32[1152,128]{1,0:T(8,128)}, f32[1152,128]{1,0:T(8,128)}, f32[768,128]{1,0:T(8,128)}, f32[384,128]{1,0:T(8,128)}, f32[3456,128]{1,0:T(8,128)}, /*i...) custom-call(s32[1,4]{1,0:T(1,128)} %refs_0_.3, ...), custom_call_target="tpu_custom_call" | custom-call | tf_op jit(solution)/shard_map/results/pallas_call | solution.py:2105
